TPU v7x, 32 devices: a whole 2x2x4 slice. The times are simulated.
32 devices in a mesh: tm: 2 (over x), space: 16 (over z, y, core).
Axes of the slice: x: 2, y: 2, z: 4, core: 2. Of those that a mesh axis runs over, the one named last changes fastest.
Arguments:
- panels_in: float32 [32, 8192], P(None, 'space'), may hold values from -120 to 120
- blocks: float32 [4, 128, 3, 4096], P('tm', 'space'), may hold values from -0.4375 to 0.4375
- block_mask: int32 [4, 128, 3], P('tm', 'space'), may hold values 0 or 1
- mixing: float32 [4, 4, 8, 8], P('tm'), may hold values from -0.6 to 0.6
Outputs:
- forward_states: float32 [2, 32, 8192], P('tm', None, 'space')
- adjoint_states: float32 [2, 32, 8192], P('tm', None, 'space')
All inputs are finite; a program needn't handle non-finite values. No bound on the sum of `block_mask` on one device may be relied on, other than what follows from the above.
Results may differ from a plain program's by a relative error of at most 0.0003.
Values sent between devices are 32-bit elements; how exact they have to be, the bound alone decides.
No kernel may reach another device: no remote copies, remote signals or barrier semaphores. Data moves between devices by JAX's collectives and lax.ppermute only.
A program may use at most 64 MiB of HBM per device.

v0:
```python
import jax
import jax.numpy as jnp
from jax import lax
from jax.sharding import PartitionSpec as P

BLOCK = 64
COLS = 8
PANELS = 4
TRANSFER_RUN = 2


def extended_2(block, sides, width):
    for axis, dim in sides:
        count = lax.axis_size(axis)
        forward = [(i, i + 1) for i in range(count - 1)]
        backward = [(target, source) for source, target in forward]
        low = lax.ppermute(
            lax.slice_in_dim(block, block.shape[dim] - width, None, axis=dim), axis, forward
        )
        high = lax.ppermute(lax.slice_in_dim(block, 0, width, axis=dim), axis, backward)
        block = jnp.concatenate([low, block, high], axis=dim)
    return block


def shifted(block, axis, distance):
    devices = range(lax.axis_size(axis))
    route = [(i - distance, i) for i in devices if i - distance in devices]
    return lax.ppermute(block, axis, route)


def push_step(blocks_here, working):
    count_cols = working.shape[0]
    count_blocks = blocks_here.shape[0]
    reshaped_block = working.reshape(count_cols, count_blocks, BLOCK)
    padded = jnp.pad(reshaped_block, ((0, 0), (1, 1), (0, 0)))
    pieces = jnp.stack(
        [
            padded[:, 0:count_blocks],
            padded[:, 1 : count_blocks + 1],
            padded[:, 2 : count_blocks + 2],
        ],
        axis=2,
    )
    matrices = blocks_here.reshape(count_blocks, 3, BLOCK, BLOCK)
    result = jnp.einsum("bjik,cbjk->cbi", matrices, pieces, precision=lax.Precision.HIGHEST)
    return result.reshape(count_cols, count_blocks * BLOCK)


def pull_step(blocks_here, working):
    count_cols = working.shape[0]
    count_blocks = blocks_here.shape[0]
    reshaped_block = working.reshape(count_cols, count_blocks, BLOCK)
    matrices = blocks_here.reshape(count_blocks, 3, BLOCK, BLOCK)
    products = jnp.einsum(
        "bjik,cbi->cbjk", matrices, reshaped_block, precision=lax.Precision.HIGHEST
    )
    first_part = products[:, :, 0]
    middle_part = products[:, :, 1]
    last_part = products[:, :, 2]
    result = (
        middle_part
        + jnp.pad(first_part[:, 1:], ((0, 0), (0, 1), (0, 0)))
        + jnp.pad(last_part[:, :-1], ((0, 0), (1, 0), (0, 0)))
    )
    return result.reshape(count_cols, count_blocks * BLOCK)


def mix_columns(working, expansion_weights):
    panel_count = expansion_weights.shape[0]
    reshaped_block = working.reshape(panel_count, COLS, working.shape[1])
    blended_panel = jnp.einsum(
        "yit,yif->ytf", expansion_weights, reshaped_block, precision=lax.Precision.HIGHEST
    )
    return working - blended_panel.reshape(working.shape)


def rescale(current):
    own_sums = jnp.sum(current * current, axis=1)
    all_sums = lax.psum(own_sums, "space")
    box_total = current.shape[1] * lax.axis_size("space")
    return current / jnp.sqrt(all_sums / box_total + 1e-06)[:, None]


def owner_pair(current, expansion_weights, extended, forward):
    box_count = current.shape[1]
    margin = TRANSFER_RUN * BLOCK
    if forward:
        step_order = list(range(TRANSFER_RUN))
        apply_step = push_step
    else:
        step_order = list(range(TRANSFER_RUN - 1, -1, -1))
        apply_step = pull_step
    working = extended_2(current, (("space", 1),), margin)
    for step_index in step_order:
        working = mix_columns(
            apply_step(extended[step_index], working), expansion_weights[step_index]
        )
    current = working[:, margin : margin + box_count]
    return rescale(current)


def sweep(source, mixing, extended, forward, columns_pass):
    owning_devices = lax.axis_size("tm")
    own_index = lax.axis_index("tm")
    if forward:
        position = own_index
    else:
        position = owning_devices - 1 - own_index
    passes = source.shape[0] // columns_pass

    def one_section(section_index, carry):
        incoming, stored = carry
        panel_index = section_index - position
        current = jnp.where(position == 0, source, incoming)
        result = owner_pair(current, mixing, extended, forward)
        in_range = (panel_index >= 0) & (panel_index < passes)
        stored = jnp.where(in_range, result, stored)
        if forward:
            incoming = shifted(result, "tm", 1)
        else:
            incoming = shifted(result, "tm", -1)
        return (incoming, stored)

    start_carry = (jnp.zeros((columns_pass, source.shape[1]), jnp.float32), jnp.zeros_like(source))
    return lax.fori_loop(0, passes + owning_devices - 1, one_section, start_carry)[1]


def shards(panels_in, blocks, block_mask, mixing):
    masked = blocks * block_mask.astype(jnp.float32)[:, :, :, None]
    rim_blocks = jnp.concatenate([masked[:, :TRANSFER_RUN], masked[:, -TRANSFER_RUN:]], axis=1)
    received = extended_2(rim_blocks, (("space", 1),), TRANSFER_RUN)
    extended = jnp.concatenate(
        [received[:, :TRANSFER_RUN], masked, received[:, 3 * TRANSFER_RUN :]], axis=1
    )
    columns_pass = PANELS * COLS
    forward_store = sweep(panels_in, mixing, extended, True, columns_pass)
    adjoint_store = sweep(forward_store, mixing, extended, False, columns_pass)
    return (forward_store[None], adjoint_store[None])


def solution(mesh):
    return jax.shard_map(
        shards,
        mesh=mesh,
        in_specs=(
            P(None, "space"),
            P("tm", "space", None, None),
            P("tm", "space", None),
            P("tm", None, None, None),
        ),
        out_specs=(P("tm", None, "space"), P("tm", None, "space")),
        check_vma=False,
    )
```

profile of v0, /device:TPU:0, one launch (start us, length us, event | category | flops | bytes accessed | tf_op | source)
XLA Modules:
  0.0 222.8 jit_solution(1405172959727927514)
XLA Ops:
  0.6 0.7 convert_element_type.24
  1.3 1.3 broadcast_multiply_fusion
  2.7 1.3 collective-permute-start.7
  4.0 3.0 %collective-permute-start.6 = (f32[2,2,3,4096]{3,1,2,0:T(2,128)S(1)}, f32[2,2,3,4096]{3,1,2,0:T(2,128)S(1)}, u32[]{:S(2)}, u32[]{:S(2)}) collective-permute-start(f32[2,2,3,4096]{3,1,2,0:T(2,128)S(1)} %get-tuple-element.506), channel_id=1, source_target_pairs={{0,1},{1,2},{2,3},{3,4},{4,5},{5,6},{6,7},{7,8},{8,9},{9,10},{10,1... | collective-permute-start | bytes 589832 | tf_op jit(solution)/shard_map/ppermute | solution.py:17
  7.1 0.7 copy.38
  7.8 0.3 collective-permute-done.6
  8.1 0.3 pad_maximum_fusion.2
  8.4 0.2 copy-done.7
  8.6 110.8 %while.36 = (s32[]{:T(128)}, f32[32,512]{1,0:T(8,128)S(1)}, f32[32,512]{1,0:T(8,128)}, pred[]{:T(512)}, f32[32,512]{1,0:T(8,128)S(1)}, /*index=5*/f32[2,12,3,409...) while((s32[]{:T(128)}, f32[32,512]{1,0:T(8,128)S(1)}, ...), condition=%wide.region_3.4_spmd.clone, body=%wide.region_0.3_spmd.clone.sunk | while | flops 118464584 | bytes 14689466 | solution.py:125
  8.6 0.6 fusion.81
  9.3 1.3 collective-permute-start
  10.6 8.2 %collective-permute-start.1 = (f32[32,128]{1,0:T(8,128)}, f32[32,128]{1,0:T(8,128)}, u32[]{:S(2)}, u32[]{:S(2)}) collective-permute-start(f32[32,128]{1,0:T(8,128)} %get-tuple-element.621), channel_id=1, source_target_pairs={{0,1},{1,2},{2,3},{3,4},{4,5},{5,6},{6,7},{7,8},{8,9},{9,10},{10,1... | collective-permute-start | bytes 49160 | tf_op jit(solution)/shard_map/while/body/eval_jaxpr/ppermute | solution.py:17
  18.7 1.0 fusion.80
  19.7 1.6 squeeze.158
  21.3 1.5 squeeze.159
  22.8 0.9 pad_maximum_fusion.5
  24.1 1.1 copy-done
  25.1 1.4 fusion.83
  26.8 0.2 convolution_bitcast_fusion.14
  27.2 1.4 convolution_bitcast_fusion.15
  29.4 32.7 %psum.32 = f32[32]{0:T(128)S(1)} all-reduce(f32[32]{0:T(128)S(1)} %multiply_reduce_fusion.4), channel_id=1, replica_groups=mesh['tm'=2,'space'=16] {'space'}, use_global_device_ids=true, to_apply=%region_2.2 | all-reduce | flops 32 | bytes 256 | tf_op jit(solution)/shard_map/while/body/eval_jaxpr/psum | solution.py:79
  62.2 3.4 %collective-permute-start.2 = (f32[32,512]{1,0:T(8,128)S(1)}, f32[32,512]{1,0:T(8,128)S(1)}, u32[]{:S(2)}, u32[]{:S(2)}) collective-permute-start(f32[32,512]{1,0:T(8,128)S(1)} %get-tuple-element.626), channel_id=1, source_target_pairs={{0,16},{1,17},{2,18},{3,19},{4,20},{5,21},{6,22},{7,23},{8,24},{9,... | collective-permute-start | bytes 196616 | tf_op jit(solution)/shard_map/while/body/eval_jaxpr/ppermute | solution.py:28
  65.6 1.9 collective-permute-done.2
  67.5 0.6 fusion.81
  68.1 1.3 collective-permute-start
  69.4 3.6 %collective-permute-start.1 = (f32[32,128]{1,0:T(8,128)}, f32[32,128]{1,0:T(8,128)}, u32[]{:S(2)}, u32[]{:S(2)}) collective-permute-start(f32[32,128]{1,0:T(8,128)} %get-tuple-element.621), channel_id=1, source_target_pairs={{0,1},{1,2},{2,3},{3,4},{4,5},{5,6},{6,7},{7,8},{8,9},{9,10},{10,1... | collective-permute-start | bytes 49160 | tf_op jit(solution)/shard_map/while/body/eval_jaxpr/ppermute | solution.py:17
  73.0 1.0 fusion.80
  74.0 1.6 squeeze.158
  75.6 1.5 squeeze.159
  77.1 0.9 pad_maximum_fusion.5
  78.4 1.1 copy-done
  79.5 1.4 fusion.83
  81.1 0.2 convolution_bitcast_fusion.14
  81.6 1.4 convolution_bitcast_fusion.15
  83.7 29.5 %psum.32 = f32[32]{0:T(128)S(1)} all-reduce(f32[32]{0:T(128)S(1)} %multiply_reduce_fusion.4), channel_id=1, replica_groups=mesh['tm'=2,'space'=16] {'space'}, use_global_device_ids=true, to_apply=%region_2.2 | all-reduce | flops 32 | bytes 256 | tf_op jit(solution)/shard_map/while/body/eval_jaxpr/psum | solution.py:79
  113.3 4.3 %collective-permute-start.2 = (f32[32,512]{1,0:T(8,128)S(1)}, f32[32,512]{1,0:T(8,128)S(1)}, u32[]{:S(2)}, u32[]{:S(2)}) collective-permute-start(f32[32,512]{1,0:T(8,128)S(1)} %get-tuple-element.626), channel_id=1, source_target_pairs={{0,16},{1,17},{2,18},{3,19},{4,20},{5,21},{6,22},{7,23},{8,24},{9,... | collective-permute-start | bytes 196616 | tf_op jit(solution)/shard_map/while/body/eval_jaxpr/ppermute | solution.py:28
  117.5 1.9 collective-permute-done.2
  119.4 103.4 %while.37 = (s32[]{:T(128)}, f32[32,512]{1,0:T(8,128)S(1)}, f32[32,512]{1,0:T(8,128)}, pred[]{:T(512)}, f32[32,512]{1,0:T(8,128)}, /*index=5*/f32[2,12,3,4096]{3...) while((s32[]{:T(128)}, f32[32,512]{1,0:T(8,128)S(1)}, ...), condition=%wide.region_7.8_spmd.clone, body=%wide.region_4.7_spmd.clone.sunk | while | flops 118267976 | bytes 12952698 | solution.py:125
  119.5 0.6 fusion.94
  120.1 1.3 collective-permute-start.3
  121.4 3.6 %collective-permute-start.4 = (f32[32,128]{1,0:T(8,128)}, f32[32,128]{1,0:T(8,128)}, u32[]{:S(2)}, u32[]{:S(2)}) collective-permute-start(f32[32,128]{1,0:T(8,128)} %get-tuple-element.639), channel_id=1, source_target_pairs={{0,1},{1,2},{2,3},{3,4},{4,5},{5,6},{6,7},{7,8},{8,9},{9,10},{10,1... | collective-permute-start | bytes 49160 | tf_op jit(solution)/shard_map/while/body/eval_jaxpr/ppermute | solution.py:17
  125.0 1.0 fusion.93
  126.0 1.6 squeeze.160
  127.6 1.5 squeeze.161
  129.1 0.9 pad_maximum_fusion.6
  130.1 2.1 convolution_bitcast_fusion.17
  132.6 0.4 copy-done.6
  133.4 0.9 convolution_bitcast_fusion.19
  135.1 29.5 %psum.33 = f32[32]{0:T(128)S(1)} all-reduce(f32[32]{0:T(128)S(1)} %multiply_reduce_fusion.5), channel_id=1, replica_groups=mesh['tm'=2,'space'=16] {'space'}, use_global_device_ids=true, to_apply=%region_6.6 | all-reduce | flops 32 | bytes 256 | tf_op jit(solution)/shard_map/while/body/eval_jaxpr/psum | solution.py:79
  164.7 1.3 collective-permute-start.5
  166.0 5.4 %collective-permute-done.5 = f32[32,512]{1,0:T(8,128)S(1)} collective-permute-done((f32[32,512]{1,0:T(8,128)S(1)}, f32[32,512]{1,0:T(8,128)S(1)}, u32[]{:S(2)}, u32[]{:S(2)}) %collective-permute-start.5) | collective-permute-done | bytes 65568 | tf_op jit(solution)/shard_map/while/body/eval_jaxpr/ppermute | solution.py:28
  171.4 0.6 fusion.94
  172.1 1.3 collective-permute-start.3
  173.3 3.6 %collective-permute-start.4 = (f32[32,128]{1,0:T(8,128)}, f32[32,128]{1,0:T(8,128)}, u32[]{:S(2)}, u32[]{:S(2)}) collective-permute-start(f32[32,128]{1,0:T(8,128)} %get-tuple-element.639), channel_id=1, source_target_pairs={{0,1},{1,2},{2,3},{3,4},{4,5},{5,6},{6,7},{7,8},{8,9},{9,10},{10,1... | collective-permute-start | bytes 49160 | tf_op jit(solution)/shard_map/while/body/eval_jaxpr/ppermute | solution.py:17
  177.0 1.0 fusion.93
  178.0 1.6 squeeze.160
  179.6 1.5 squeeze.161
  181.1 0.9 pad_maximum_fusion.6
  182.0 2.1 convolution_bitcast_fusion.17
  184.6 0.4 copy-done.6
  185.3 0.9 convolution_bitcast_fusion.19
  187.0 29.5 %psum.33 = f32[32]{0:T(128)S(1)} all-reduce(f32[32]{0:T(128)S(1)} %multiply_reduce_fusion.5), channel_id=1, replica_groups=mesh['tm'=2,'space'=16] {'space'}, use_global_device_ids=true, to_apply=%region_6.6 | all-reduce | flops 32 | bytes 256 | tf_op jit(solution)/shard_map/while/body/eval_jaxpr/psum | solution.py:79
  216.6 1.3 collective-permute-start.5
  217.9 4.9 %collective-permute-done.5 = f32[32,512]{1,0:T(8,128)S(1)} collective-permute-done((f32[32,512]{1,0:T(8,128)S(1)}, f32[32,512]{1,0:T(8,128)S(1)}, u32[]{:S(2)}, u32[]{:S(2)}) %collective-permute-start.5) | collective-permute-done | bytes 65568 | tf_op jit(solution)/shard_map/while/body/eval_jaxpr/ppermute | solution.py:28
  (132 shorter events, 6.6 us)
Async XLA Ops:
  1.3 5.8 %copy-start.11 = (f32[2,4,8,8]{3,2,1,0:T(8,128)S(1)}, f32[2,4,8,8]{3,2,1,0:T(8,128)}, u32[]{:S(2)}) copy-start(f32[2,4,8,8]{3,2,1,0:T(8,128)} %param.11) | copy-start | bytes 6148
  2.7 5.1 %collective-permute-start.7 = (f32[2,2,3,4096]{3,1,2,0:T(2,128)S(1)}, f32[2,2,3,4096]{3,1,2,0:T(2,128)S(1)}, u32[]{:S(2)}, u32[]{:S(2)}) collective-permute-start(f32[2,2,3,4096]{3,1,2,0:T(2,128)S(1)} %get-tuple-element.507), channel_id=1, source_target_pairs={{1,0},{2,1},{3,2},{4,3},{5,4},{6,5},{7,6},{8,7},{9,8},{10,9},{11,1... | collective-permute-start | bytes 589832 | tf_op jit(solution)/shard_map/ppermute | solution.py:20
  4.0 4.1 %collective-permute-start.6 = (f32[2,2,3,4096]{3,1,2,0:T(2,128)S(1)}, f32[2,2,3,4096]{3,1,2,0:T(2,128)S(1)}, u32[]{:S(2)}, u32[]{:S(2)}) collective-permute-start(f32[2,2,3,4096]{3,1,2,0:T(2,128)S(1)} %get-tuple-element.506), channel_id=1, source_target_pairs={{0,1},{1,2},{2,3},{3,4},{4,5},{5,6},{6,7},{7,8},{8,9},{9,10},{10,1... | collective-permute-start | bytes 589832 | tf_op jit(solution)/shard_map/ppermute | solution.py:17
  7.8 0.8 copy-start.7
  8.6 10.1 %copy-start.1 = (f32[32,512]{1,0:T(8,128)}, f32[32,512]{1,0:T(8,128)S(1)}, u32[]{:S(2)}) copy-start(f32[32,512]{1,0:T(8,128)S(1)} %broadcast_select_fusion.4) | copy-start | bytes 196612 | tf_op jit(solution)/shard_map/while
  9.3 13.5 %collective-permute-start = (f32[32,128]{1,0:T(8,128)}, f32[32,128]{1,0:T(8,128)S(1)}, u32[]{:S(2)}, u32[]{:S(2)}) collective-permute-start(f32[32,128]{1,0:T(8,128)} %get-tuple-element.620), channel_id=1, source_target_pairs={{1,0},{2,1},{3,2},{4,3},{5,4},{6,5},{7,6},{8,7},{9,8},{10,9},{11,1... | collective-permute-start | bytes 49160 | tf_op jit(solution)/shard_map/while/body/eval_jaxpr/ppermute | solution.py:20
  10.6 12.3 %collective-permute-start.1 = (f32[32,128]{1,0:T(8,128)}, f32[32,128]{1,0:T(8,128)}, u32[]{:S(2)}, u32[]{:S(2)}) collective-permute-start(f32[32,128]{1,0:T(8,128)} %get-tuple-element.621), channel_id=1, source_target_pairs={{0,1},{1,2},{2,3},{3,4},{4,5},{5,6},{6,7},{7,8},{8,9},{9,10},{10,1... | collective-permute-start | bytes 49160 | tf_op jit(solution)/shard_map/while/body/eval_jaxpr/ppermute | solution.py:17
  23.9 1.3 copy-start
  25.1 1.6 copy-start.5
  28.6 33.4 %copy-start.3 = (f32[32,512]{1,0:T(8,128)S(1)}, f32[32,512]{1,0:T(8,128)}, u32[]{:S(2)}) copy-start(f32[32,512]{1,0:T(8,128)} %get-tuple-element.658) | copy-start | bytes 196612 | tf_op jit(solution)/shard_map/while
  28.7 38.8 %copy-start.8 = (f32[32,512]{1,0:T(8,128)S(1)}, f32[32,512]{1,0:T(8,128)}, u32[]{:S(2)}) copy-start(f32[32,512]{1,0:T(8,128)} %get-tuple-element.721) | copy-start | bytes 196612 | tf_op jit(solution)/shard_map/while
  62.1 5.3 %copy-start.4 = (f32[32,512]{1,0:T(8,128)}, f32[32,512]{1,0:T(8,128)S(1)}, u32[]{:S(2)}) copy-start(f32[32,512]{1,0:T(8,128)S(1)} %get-tuple-element.668) | copy-start | bytes 196612 | tf_op jit(solution)/shard_map/while
  62.2 5.3 %collective-permute-start.2 = (f32[32,512]{1,0:T(8,128)S(1)}, f32[32,512]{1,0:T(8,128)S(1)}, u32[]{:S(2)}, u32[]{:S(2)}) collective-permute-start(f32[32,512]{1,0:T(8,128)S(1)} %get-tuple-element.626), channel_id=1, source_target_pairs={{0,16},{1,17},{2,18},{3,19},{4,20},{5,21},{6,22},{7,23},{8,24},{9,... | collective-permute-start | bytes 196616 | tf_op jit(solution)/shard_map/while/body/eval_jaxpr/ppermute | solution.py:28
  67.5 5.6 %copy-start.1 = (f32[32,512]{1,0:T(8,128)}, f32[32,512]{1,0:T(8,128)S(1)}, u32[]{:S(2)}) copy-start(f32[32,512]{1,0:T(8,128)S(1)} %broadcast_select_fusion.4) | copy-start | bytes 196612 | tf_op jit(solution)/shard_map/while
  68.1 9.0 %collective-permute-start = (f32[32,128]{1,0:T(8,128)}, f32[32,128]{1,0:T(8,128)S(1)}, u32[]{:S(2)}, u32[]{:S(2)}) collective-permute-start(f32[32,128]{1,0:T(8,128)} %get-tuple-element.620), channel_id=1, source_target_pairs={{1,0},{2,1},{3,2},{4,3},{5,4},{6,5},{7,6},{8,7},{9,8},{10,9},{11,1... | collective-permute-start | bytes 49160 | tf_op jit(solution)/shard_map/while/body/eval_jaxpr/ppermute | solution.py:20
  69.4 7.7 %collective-permute-start.1 = (f32[32,128]{1,0:T(8,128)}, f32[32,128]{1,0:T(8,128)}, u32[]{:S(2)}, u32[]{:S(2)}) collective-permute-start(f32[32,128]{1,0:T(8,128)} %get-tuple-element.621), channel_id=1, source_target_pairs={{0,1},{1,2},{2,3},{3,4},{4,5},{5,6},{6,7},{7,8},{8,9},{9,10},{10,1... | collective-permute-start | bytes 49160 | tf_op jit(solution)/shard_map/while/body/eval_jaxpr/ppermute | solution.py:17
  78.2 1.3 copy-start
  79.5 1.6 copy-start.5
  83.0 30.2 %copy-start.3 = (f32[32,512]{1,0:T(8,128)S(1)}, f32[32,512]{1,0:T(8,128)}, u32[]{:S(2)}) copy-start(f32[32,512]{1,0:T(8,128)} %get-tuple-element.658) | copy-start | bytes 196612 | tf_op jit(solution)/shard_map/while
  83.0 36.5 %copy-start.8 = (f32[32,512]{1,0:T(8,128)S(1)}, f32[32,512]{1,0:T(8,128)}, u32[]{:S(2)}) copy-start(f32[32,512]{1,0:T(8,128)} %get-tuple-element.721) | copy-start | bytes 196612 | tf_op jit(solution)/shard_map/while
  113.3 6.2 %copy-start.4 = (f32[32,512]{1,0:T(8,128)}, f32[32,512]{1,0:T(8,128)S(1)}, u32[]{:S(2)}) copy-start(f32[32,512]{1,0:T(8,128)S(1)} %get-tuple-element.668) | copy-start | bytes 196612 | tf_op jit(solution)/shard_map/while
  113.3 6.2 %collective-permute-start.2 = (f32[32,512]{1,0:T(8,128)S(1)}, f32[32,512]{1,0:T(8,128)S(1)}, u32[]{:S(2)}, u32[]{:S(2)}) collective-permute-start(f32[32,512]{1,0:T(8,128)S(1)} %get-tuple-element.626), channel_id=1, source_target_pairs={{0,16},{1,17},{2,18},{3,19},{4,20},{5,21},{6,22},{7,23},{8,24},{9,... | collective-permute-start | bytes 196616 | tf_op jit(solution)/shard_map/while/body/eval_jaxpr/ppermute | solution.py:28
  119.5 5.6 %copy-start.2 = (f32[32,512]{1,0:T(8,128)}, f32[32,512]{1,0:T(8,128)S(1)}, u32[]{:S(2)}) copy-start(f32[32,512]{1,0:T(8,128)S(1)} %broadcast_select_fusion.5) | copy-start | bytes 196612 | tf_op jit(solution)/shard_map/while
  120.1 9.0 %collective-permute-start.3 = (f32[32,128]{1,0:T(8,128)}, f32[32,128]{1,0:T(8,128)S(1)}, u32[]{:S(2)}, u32[]{:S(2)}) collective-permute-start(f32[32,128]{1,0:T(8,128)} %get-tuple-element.638), channel_id=1, source_target_pairs={{1,0},{2,1},{3,2},{4,3},{5,4},{6,5},{7,6},{8,7},{9,8},{10,9},{11,1... | collective-permute-start | bytes 49160 | tf_op jit(solution)/shard_map/while/body/eval_jaxpr/ppermute | solution.py:20
  121.4 7.7 %collective-permute-start.4 = (f32[32,128]{1,0:T(8,128)}, f32[32,128]{1,0:T(8,128)}, u32[]{:S(2)}, u32[]{:S(2)}) collective-permute-start(f32[32,128]{1,0:T(8,128)} %get-tuple-element.639), channel_id=1, source_target_pairs={{0,1},{1,2},{2,3},{3,4},{4,5},{5,6},{6,7},{7,8},{8,9},{9,10},{10,1... | collective-permute-start | bytes 49160 | tf_op jit(solution)/shard_map/while/body/eval_jaxpr/ppermute | solution.py:17
  132.3 0.8 copy-start.6
  134.3 30.2 %copy-start.9 = (f32[32,512]{1,0:T(8,128)S(1)}, f32[32,512]{1,0:T(8,128)}, u32[]{:S(2)}) copy-start(f32[32,512]{1,0:T(8,128)} %get-tuple-element.688) | copy-start | bytes 196612 | tf_op jit(solution)/shard_map/while
  164.7 6.7 %copy-start.10 = (f32[32,512]{1,0:T(8,128)}, f32[32,512]{1,0:T(8,128)S(1)}, u32[]{:S(2)}) copy-start(f32[32,512]{1,0:T(8,128)S(1)} %get-tuple-element.698) | copy-start | bytes 196612 | tf_op jit(solution)/shard_map/while
  164.7 6.7 %collective-permute-start.5 = (f32[32,512]{1,0:T(8,128)S(1)}, f32[32,512]{1,0:T(8,128)S(1)}, u32[]{:S(2)}, u32[]{:S(2)}) collective-permute-start(f32[32,512]{1,0:T(8,128)S(1)} %get-tuple-element.644), channel_id=1, source_target_pairs={{16,0},{17,1},{18,2},{19,3},{20,4},{21,5},{22,6},{23,7},{24,8},{25... | collective-permute-start | bytes 196616 | tf_op jit(solution)/shard_map/while/body/eval_jaxpr/ppermute | solution.py:28
  171.4 5.6 %copy-start.2 = (f32[32,512]{1,0:T(8,128)}, f32[32,512]{1,0:T(8,128)S(1)}, u32[]{:S(2)}) copy-start(f32[32,512]{1,0:T(8,128)S(1)} %broadcast_select_fusion.5) | copy-start | bytes 196612 | tf_op jit(solution)/shard_map/while
  172.1 9.0 %collective-permute-start.3 = (f32[32,128]{1,0:T(8,128)}, f32[32,128]{1,0:T(8,128)S(1)}, u32[]{:S(2)}, u32[]{:S(2)}) collective-permute-start(f32[32,128]{1,0:T(8,128)} %get-tuple-element.638), channel_id=1, source_target_pairs={{1,0},{2,1},{3,2},{4,3},{5,4},{6,5},{7,6},{8,7},{9,8},{10,9},{11,1... | collective-permute-start | bytes 49160 | tf_op jit(solution)/shard_map/while/body/eval_jaxpr/ppermute | solution.py:20
  173.3 7.7 %collective-permute-start.4 = (f32[32,128]{1,0:T(8,128)}, f32[32,128]{1,0:T(8,128)}, u32[]{:S(2)}, u32[]{:S(2)}) collective-permute-start(f32[32,128]{1,0:T(8,128)} %get-tuple-element.639), channel_id=1, source_target_pairs={{0,1},{1,2},{2,3},{3,4},{4,5},{5,6},{6,7},{7,8},{8,9},{9,10},{10,1... | collective-permute-start | bytes 49160 | tf_op jit(solution)/shard_map/while/body/eval_jaxpr/ppermute | solution.py:17
  184.2 0.8 copy-start.6
  186.3 30.2 %copy-start.9 = (f32[32,512]{1,0:T(8,128)S(1)}, f32[32,512]{1,0:T(8,128)}, u32[]{:S(2)}) copy-start(f32[32,512]{1,0:T(8,128)} %get-tuple-element.688) | copy-start | bytes 196612 | tf_op jit(solution)/shard_map/while
  216.6 6.2 %copy-start.10 = (f32[32,512]{1,0:T(8,128)}, f32[32,512]{1,0:T(8,128)S(1)}, u32[]{:S(2)}) copy-start(f32[32,512]{1,0:T(8,128)S(1)} %get-tuple-element.698) | copy-start | bytes 196612 | tf_op jit(solution)/shard_map/while
  216.6 6.2 %collective-permute-start.5 = (f32[32,512]{1,0:T(8,128)S(1)}, f32[32,512]{1,0:T(8,128)S(1)}, u32[]{:S(2)}, u32[]{:S(2)}) collective-permute-start(f32[32,512]{1,0:T(8,128)S(1)} %get-tuple-element.644), channel_id=1, source_target_pairs={{16,0},{17,1},{18,2},{19,3},{20,4},{21,5},{22,6},{23,7},{24,8},{25... | collective-permute-start | bytes 196616 | tf_op jit(solution)/shard_map/while/body/eval_jaxpr/ppermute | solution.py:28
where the time goes:
time: 224 us; the launch traced here: 223 us
  blocking collectives  121 us (54%)
  starting transfers between devices  38.8 us (17%)
  local copies, waits for them, and re-layouts  26.8 us (12%)
  waiting for transfers between devices  14.4 us (6%)
  matrix products  13.4 us (6%)
  other arithmetic  6.87 us (3%)
    psum x4, blocking collectives, rescale(): all_sums = lax.psum(own_sums, 'space')  121 us
    ppermute x5, starting transfers between devices, extended_2(): lax.ppermute(lax.slice_in_dim(block, block.shape[dim] - width, None, axis...  22.1 us
    ppermute x4, waiting for transfers between devices, shifted(): return lax.ppermute(block, axis, route)  14 us
    ppermute x4, starting transfers between devices, shifted(): return lax.ppermute(block, axis, route)  10.2 us
    ppermute x5, starting transfers between devices, extended_2(): lax.ppermute(lax.slice_in_dim(block, 0, width, axis=dim), axis, backward)  6.41 us
    squeeze x4, local copies, waits for them, and re-layouts, push_step(): matrices = blocks_here.reshape(count_blocks, 3, BLOCK, BLOCK)  6.2 us
    squeeze x4, local copies, waits for them, and re-layouts, pull_step(): matrices = blocks_here.reshape(count_blocks, 3, BLOCK, BLOCK)  6.2 us
    dot_general x4, matrix products, pull_step(): jnp.einsum('bjik,cbi->cbjk', matrices, reshaped_block, precision=lax.Prec...  6.05 us
  transfers between devices with their start and end apart: 14, of which 5 were waited for; matrix products, arithmetic and copies ran while one was open for 8% of the time, Pallas kernels for 0%

commit v1 on v0

v1 whole, which is shorter than its diff:
```python
import functools

import jax
import jax.numpy as jnp
from jax import lax
from jax.experimental import pallas as pl
from jax.experimental.pallas import tpu as pltpu
from jax.sharding import PartitionSpec as P

BLOCK = 64
COLS = 8
PANELS = 4
ROWS = COLS * PANELS
RUN = 2
GROUP = 4
RIM_A = 5
RIM_B = 4
DOWN = 2.0**-16
BF = jnp.bfloat16
F32 = jnp.float32
HIGH = lax.Precision.HIGHEST
NT = (((1,), (1,)), ((), ()))
NN = (((1,), (0,)), ((), ()))
TN = (((0,), (0,)), ((), ()))
VM = pl.BlockSpec(memory_space=pltpu.VMEM)


def call(kernel, outs, args, scratch=(), flops=10**6):
    shapes = [jax.ShapeDtypeStruct(shape, dtype) for shape, dtype in outs]
    return pl.pallas_call(
        kernel,
        out_shape=shapes,
        in_specs=[VM] * len(args),
        out_specs=[VM] * len(outs),
        scratch_shapes=list(scratch),
        compiler_params=pltpu.CompilerParams(vmem_limit_bytes=12 << 20),
        cost_estimate=pl.CostEstimate(flops=flops, bytes_accessed=10**6, transcendentals=0),
    )(*args)


def inside():
    place, last = lax.axis_index("space"), lax.axis_size("space") - 1
    return jnp.where((place == 0) | (place == last), 0.0, 1.0).astype(F32)


def parity():
    return lax.rem(lax.axis_index("space"), 2)


def iota(shape, dim):
    return lax.broadcasted_iota(jnp.int32, shape, dim)


def edge_kernel(nb, blocks, mask, panels, to_a, to_b):
    width = panels.shape[1]

    def emit(dst, row, start, keep=1.0):
        for j in range(3):
            line = blocks[0, j, row : row + 1, :] * (mask[0, j, row : row + 1, 0:1] * keep)
            for r in range(32):
                dst[j * 32 + r : j * 32 + r + 1, :] = line[:, r * 128 : (r + 1) * 128]
        dst[96:128, :] = panels[:, start : start + 128]

    @pl.when(parity() == 0)
    def _():
        emit(to_a, nb - 1, width - 128)
        emit(to_b, 0, 0, inside())

    @pl.when(parity() == 1)
    def _():
        emit(to_a, 0, 0)
        emit(to_b, nb - 1, width - 128, inside())


def far_kernel(nb, blocks, mask, to_a, to_b):
    def emit(dst, row_a, row_b, keep=1.0):
        for j in range(3):
            for r in range(32):
                lanes = slice(r * 128, (r + 1) * 128)
                va = blocks[0, j, :, lanes] * (mask[0, j] * keep)
                vb = blocks[1, j, :, lanes] * (mask[1, j] * keep)
                dst[pl.ds(j * 32 + r, RIM_A - 1, stride=96), :] = va[row_a : row_a + RIM_A - 1]
                dst[pl.ds(96 * (RIM_A - 1) + j * 32 + r, RIM_B, stride=96), :] = vb[row_b : row_b + RIM_B]

    @pl.when(parity() == 0)
    def _():
        emit(to_a, nb - RIM_A, nb - RIM_B)
        emit(to_b, 1, 0, inside())

    @pl.when(parity() == 1)
    def _():
        emit(to_a, 1, 0)
        emit(to_b, nb - RIM_A, nb - RIM_B, inside())


def banded(y, p):
    low = iota(y[0].shape, 1) < BLOCK
    zero = jnp.zeros_like(y[0])
    turned = [pltpu.roll(v, BLOCK, 1) for v in y]
    at_low, at_high = (y, turned) if p == 0 else (turned, y)
    first = (jnp.where(low, at_low[0], at_high[1]), jnp.where(low, at_low[2], zero))
    second = (jnp.where(low, zero, at_high[0]), jnp.where(low, at_low[1], at_high[2]))
    return first, second


def split2(x):
    high = x.astype(BF)
    return high, (x - high.astype(F32)).astype(BF)


def split_halves(wide, at, hi, lo):
    for half in range(2):
        lanes = slice(half * 128, half * 128 + 128)
        hi[:, lanes], lo[:, lanes] = split2(wide[at + half])


def own_kernel(nb, blocks, mask, mixing, a_hi, a_lo, b_hi, b_lo, expand, wide):
    for t, hi, lo in ((0, a_hi, a_lo), (1, b_hi, b_lo)):
        is_first = lax.rem(iota((nb, 128), 0), 2) == (1 - t)
        for r in range(32):
            lanes = slice(r * 128, (r + 1) * 128)
            y = [blocks[t, j, :, lanes] * mask[t, j] for j in range(3)]
            for p in range(2):
                first, second = banded(y, p)
                for half in range(2):
                    wide[2 * t + half, pl.ds(2 * r + p, nb, stride=BLOCK), :] = jnp.where(
                        is_first, first[half], second[half]
                    )
        split_halves(wide, 2 * t, hi, lo)
    pick = (lax.rem(iota((COLS, 128), 1), COLS) == iota((COLS, 128), 0)).astype(F32)
    row, lane = iota((ROWS, 128), 0), lax.rem(iota((ROWS, 128), 1), ROWS)
    same = (row // COLS) == (lane // COLS)
    step = []
    for t in range(RUN):
        m = mixing[t].reshape(ROWS, COLS)
        spread = lax.dot_general(m, pick, NN, precision=HIGH, preferred_element_type=F32)
        step.append((row == lane).astype(F32) - jnp.where(same, spread, 0.0))
    for i, (x, y) in enumerate(((step[0], step[1]), (step[1], step[0]))):
        e = lax.dot_general(x[:, :ROWS], y, NN, precision=HIGH, preferred_element_type=F32)
        expand[i * COLS : (i + 1) * COLS, :] = (
            e[0:COLS] + e[COLS : 2 * COLS] + e[2 * COLS : 3 * COLS] + e[3 * COLS :]
        )


def rim_row(dst, index, first, from_a, from_b, base, left):
    use_b = (parity() == 0) == left
    y = []
    for j in range(3):
        rows = slice(base + j * 32, base + j * 32 + 32)
        y.append(jnp.where(use_b, from_b[rows, :], from_a[rows, :]))
    for p in range(2):
        tiles = banded(y, p)[0 if first else 1]
        for half in range(2):
            dst[half, pl.ds(index * BLOCK + p, 32, stride=2), :] = tiles[half]


def rim_kernel(near_a, near_b, far_a, far_b, a_hi, a_lo, b_hi, b_lo, wide_a, wide_b):
    for i in range(RIM_A - 1):
        rim_row(wide_a, i, (RIM_A - i) % 2 == 1, far_a, far_b, i * 96, True)
        rim_row(wide_a, RIM_A + 1 + i, i % 2 == 0, far_a, far_b, i * 96, False)
    rim_row(wide_a, RIM_A - 1, True, near_a, near_b, 0, True)
    rim_row(wide_a, RIM_A, False, near_a, near_b, 0, False)
    for i in range(RIM_B):
        base = (RIM_A - 1 + i) * 96
        rim_row(wide_b, i, (RIM_B - i) % 2 == 0, far_a, far_b, base, True)
        rim_row(wide_b, RIM_B + i, i % 2 == 0, far_a, far_b, base, False)
    split_halves(wide_a, 0, a_hi, a_lo)
    split_halves(wide_b, 0, b_hi, b_lo)


def pair_tile(own, rim, depth, nb, b):
    def row(k):
        if 0 <= k < nb:
            return own[k * BLOCK : (k + 1) * BLOCK, :]
        k = k + depth if k < 0 else depth + k - nb
        return rim[k * BLOCK : (k + 1) * BLOCK, :]

    return jnp.concatenate([row(b), row(b + 1)], axis=0)


def product(x, w, dims):
    o = lax.dot_general(x, w, dims, preferred_element_type=F32)
    return (o[ROWS:, 128:] + o[ROWS:, :128] + o[:ROWS, 128:]) + o[:ROWS, :128]


def push(v, tiles):
    x = jnp.concatenate(split2(v), axis=0)
    outs = []
    for i, (hi, lo) in enumerate(tiles):
        outs.append(product(x[:, i * 128 : i * 128 + 256], jnp.concatenate([hi, lo], axis=0), NT))
    return jnp.concatenate(outs, axis=1)


def pull(v, tiles):
    x = jnp.concatenate(split2(v), axis=0)
    outs = []
    for i in range(len(tiles) - 1):
        parts = [
            jnp.concatenate([tiles[i][s][:, 128:], tiles[i + 1][s][:, :128]], axis=0) for s in range(2)
        ]
        outs.append(product(x[:, i * 128 : i * 128 + 256], jnp.concatenate(parts, axis=1), NN))
    return jnp.concatenate(outs, axis=1)


def tiles_of(refs, depth, nb, first, last):
    own_hi, own_lo, rim_hi, rim_lo = refs
    return [
        (pair_tile(own_hi, rim_hi, depth, nb, b), pair_tile(own_lo, rim_lo, depth, nb, b))
        for b in range(first, last, 2)
    ]


def gram(u):
    u1, rest = u.astype(BF), u
    rest = rest - u1.astype(F32)
    u2 = rest.astype(BF)
    u3 = (rest - u2.astype(F32)).astype(BF)
    stack = jnp.concatenate([u3, u2, u1], axis=0)
    total = None
    for part in (u3, u2, u1):
        g = lax.dot_general(stack, jnp.concatenate([part] * 4, axis=0), NT, preferred_element_type=F32)
        g = (g[:ROWS] + g[ROWS : 2 * ROWS]) + g[2 * ROWS :]
        total = g if total is None else total + g
    panel = lax.rem(iota((COLS, 128), 1), ROWS) // COLS
    out = jnp.zeros((COLS, 128), F32)
    for p in range(PANELS):
        out = out + jnp.where(panel == p, total[p * COLS : (p + 1) * COLS], 0.0)
    return out


def noted(meta, slot, g, e):
    mine = (iota((COLS, 128), 1) // ROWS) == slot
    return jnp.concatenate(
        [jnp.where(mine, g, meta[:COLS]), jnp.where(mine, e, meta[COLS : 2 * COLS]), meta[2 * COLS :]], axis=0
    )


def by_side(e_a, e_b):
    even = parity() == 0
    return jnp.where(even, e_b, e_a), jnp.where(even, e_a, e_b)


def push_kernel(nb, owner, slot, reach, old, main, edge_a, edge_b, near_a, near_b, a_hi, a_lo, b_hi, b_lo, expand,
                out, out_a, out_b, meta, wide):
    own = nb * BLOCK

    @pl.when(lax.axis_index("tm") != owner)
    def _():
        meta[...] = old[...]

    @pl.when(lax.axis_index("tm") == owner)
    def _():
        rim_row(wide, 0, True, near_a, near_b, 0, True)
        rim_row(wide, 1, False, near_a, near_b, 0, False)
        rim_hi, rim_lo = split2(jnp.concatenate([wide[0], wide[1]], axis=1))
        w_edge = edge_a.shape[1]
        left, right = by_side(edge_a[...], edge_b[...])
        v = jnp.concatenate([left[:, w_edge - 128 :], main[:, :own], right[:, :128]], axis=1)
        w = push(v, tiles_of((a_hi, a_lo, rim_hi, rim_lo), 1, nb, -1, nb))
        u = push(w, tiles_of((b_hi, b_lo, None, None), 0, nb, 0, nb))
        known = old[...] if main.shape[1] == own else main[:, own:]
        now = noted(known, slot, gram(u), expand[:COLS])
        out[:, :own] = u
        out[:, own:] = now
        meta[...] = now
        low, high = u[:, :reach], u[:, own - reach :]
        out_b[...], out_a[...] = by_side(high, low)


def turn_kernel(nb, owner, slot, old, main, edge_a, edge_b, a_hi, a_lo, b_hi, b_lo, ra_hi, ra_lo, rb_hi, rb_lo,
                expand, first_out, out, meta):
    own = nb * BLOCK

    @pl.when(lax.axis_index("tm") != owner)
    def _():
        meta[...] = old[...]

    @pl.when(lax.axis_index("tm") == owner)
    def _():
        left, right = by_side(edge_a[...], edge_b[...])
        v = jnp.concatenate([left, main[:, :own], right], axis=1)
        tiles_a = tiles_of((a_hi, a_lo, ra_hi, ra_lo), RIM_A, nb, -RIM_A, nb + RIM_A)
        tiles_b = tiles_of((b_hi, b_lo, rb_hi, rb_lo), RIM_B, nb, -RIM_B, nb + RIM_B)
        u = push(push(v, tiles_a), tiles_b)
        u_own = u[:, 256 : 256 + own]
        first_out[...] = u_own
        back = pull(pull(u * DOWN, tiles_b), tiles_a[1:-1])
        now = noted(main[:, own:], slot, gram(u_own), expand[:COLS])
        now = noted(now, slot + 1, gram(back[:, 128 : 128 + own]), expand[COLS:] * (1.0 / DOWN))
        out[:, : own + 256] = back
        out[:, own + 256 :] = now
        meta[...] = now


def pull_kernel(nb, owner, slot, old, ext, a_hi, a_lo, b_hi, b_lo, ra_hi, ra_lo, rb_hi, rb_lo, expand, out, meta):
    own = nb * BLOCK

    @pl.when(lax.axis_index("tm") != owner)
    def _():
        meta[...] = old[...]

    @pl.when(lax.axis_index("tm") == owner)
    def _():
        y = pull(ext[:, : own + 256], tiles_of((b_hi, b_lo, rb_hi, rb_lo), RIM_B, nb, -2, nb + 2))
        u = pull(y, tiles_of((a_hi, a_lo, ra_hi, ra_lo), RIM_A, nb, -1, nb + 1))
        out[...] = u
        meta[...] = noted(ext[:, own + 256 :], slot, gram(u), expand[COLS:])


def scale_kernel(stages, boxes, offsets, grams, meta, *refs):
    panels, (out_f, out_a) = refs[: len(stages)], refs[len(stages) :]
    own = out_f.shape[1]
    total = grams[0]
    for i in range(1, grams.shape[0]):
        total = total + grams[i]
    total = total * (1.0 / boxes)
    growth = meta[COLS : 2 * COLS, :]
    row, lane = iota((ROWS, ROWS), 0), iota((ROWS, ROWS), 1)
    same = (row // COLS) == (lane // COLS)
    me = lax.axis_index("tm")

    def full(x, n):
        return jnp.where(same, jnp.concatenate([x[:, n * ROWS : (n + 1) * ROWS]] * PANELS, axis=0), 0.0)

    dot = functools.partial(lax.dot_general, precision=HIGH, preferred_element_type=F32)
    back = None
    for n, (owner, forward) in enumerate(stages):
        e = full(growth, n)
        h = e if back is None else dot(back, e, NN)
        square = jnp.sum(h * dot(full(total, n), h, NN), axis=0, keepdims=True)
        back = h / jnp.sqrt(jnp.maximum(square, 0.0) + 1e-06)

        @pl.when(me == owner)
        def _(n=n, back=back, out=out_f if forward else out_a):
            u = panels[n][:, offsets[n] : offsets[n] + own]
            out[...] = dot(back, u, TN)


def shards(panels_in, blocks, block_mask, mixing):
    owners, count = lax.axis_size("tm"), lax.axis_size("space")
    me, place = lax.axis_index("tm"), lax.axis_index("space")
    nb, own = blocks.shape[1], panels_in.shape[1]
    even = lax.rem(place, 2) == 0
    bf, f32 = (lambda *s: (s, BF)), (lambda *s: (s, F32))

    def partner_a(s):
        return s ^ 1

    def partner_b(s):
        t = s + 1 if s % 2 else s - 1
        return t if 0 <= t < count else s

    def beside(x, to):
        return lax.ppermute(x, "space", [(s, to(s)) for s in range(count)])

    def hop(x, shift, to):
        route = [
            (t * count + s, (t + shift) % owners * count + to(s)) for t in range(owners) for s in range(count)
        ]
        return lax.ppermute(x, ("tm", "space"), route)

    b, j = iota((RUN, nb, 3), 1), iota((RUN, nb, 3), 2)
    outside = ((place == 0) & (b == 0) & (j == 0)) | ((place == count - 1) & (b == nb - 1) & (j == 2))
    present = jnp.where(outside, 0, block_mask).astype(F32).transpose(0, 2, 1)
    mask = jnp.broadcast_to(present[..., None], (RUN, 3, nb, 128))
    rows = blocks.transpose(0, 2, 1, 3)

    near = call(functools.partial(edge_kernel, nb), [f32(128, 128)] * 2, (rows, mask, panels_in))
    near_a, near_b = beside(near[0], partner_a), beside(near[1], partner_b)
    far_rows = 96 * (RIM_A - 1 + RIM_B)
    far = call(functools.partial(far_kernel, nb), [f32(far_rows, 128)] * 2, (rows, mask))
    far_a, far_b = beside(far[0], partner_a), beside(far[1], partner_b)
    *own_tiles, expand = call(
        functools.partial(own_kernel, nb),
        [bf(own, 256)] * 4 + [f32(2 * COLS, 128)],
        (rows, mask, mixing),
        [pltpu.VMEM((2 * RUN, own, 128), F32)],
    )
    depth_a, depth_b = 2 * RIM_A * BLOCK, 2 * RIM_B * BLOCK
    rim_tiles = call(
        rim_kernel,
        [bf(depth_a, 256)] * 2 + [bf(depth_b, 256)] * 2,
        (near_a, near_b, far_a, far_b),
        [pltpu.VMEM((2, depth_a, 128), F32), pltpu.VMEM((2, depth_b, 128), F32)],
    )

    meta = jnp.zeros((ROWS, 128), F32)
    main, edge_a, edge_b = panels_in, near_a[96:], near_b[96:]
    ext = None
    stages = 2 * owners
    owner_of = [k if k < owners else stages - 1 - k for k in range(stages)]
    result = None
    kept, offsets = [], []
    k = 0
    while k < stages:
        turning = k == owners - 1 and (k + 1) % GROUP != 0
        owner, slot = owner_of[k], k % GROUP
        if turning:
            first, ext, meta = call(
                functools.partial(turn_kernel, nb, owner, slot),
                [f32(ROWS, own), f32(ROWS, own + 384), f32(ROWS, 128)],
                (meta, main, edge_a, edge_b, *own_tiles, *rim_tiles, expand),
            )
            kept += [first, ext]
            offsets += [0, 128]
            current = ext[:, 128 : 128 + own]
            k += 2
        elif k < owners:
            reach = 384 if k + 1 == owners - 1 and (k + 2) % GROUP != 0 else 128
            main, edge_a, edge_b, meta = call(
                functools.partial(push_kernel, nb, owner, slot, reach),
                [f32(ROWS, own + 128), f32(ROWS, reach), f32(ROWS, reach), f32(ROWS, 128)],
                (meta, main, edge_a, edge_b, near_a, near_b, *own_tiles, expand),
                [pltpu.VMEM((2, 2 * BLOCK, 128), F32)],
            )
            kept.append(main)
            offsets.append(0)
            current = main[:, :own]
            k += 1
        else:
            current, meta = call(
                functools.partial(pull_kernel, nb, owner, slot),
                [f32(ROWS, own), f32(ROWS, 128)],
                (meta, ext, *own_tiles, *rim_tiles, expand),
            )
            ext = None
            kept.append(current)
            offsets.append(0)
            k += 1

        fresh = False
        if k % GROUP == 0 or k == stages:
            start = k - len(kept)
            todo = [(owner_of[i], i < owners) for i in range(start, k)]
            every = jnp.broadcast_to(meta[None, :COLS], (count, COLS, 128))
            grams = lax.all_to_all(every, "space", 0, 0)
            pair = call(
                functools.partial(scale_kernel, todo, count * own, offsets),
                [f32(ROWS, own)] * 2,
                (grams, meta, *kept),
            )
            if result is None:
                result = pair
            else:
                live = [
                    functools.reduce(jnp.logical_or, [me == o for o, f in todo if f == way], jnp.bool_(False))
                    for way in (True, False)
                ]
                result = [jnp.where(c, new, old) for c, new, old in zip(live, pair, result)]
            current = pair[0 if k - 1 < owners else 1]
            meta, ext, fresh = jnp.zeros((ROWS, 128), F32), None, True
            kept, offsets = [], []
        if k == stages:
            break

        shift = owner_of[k] - owner_of[k - 1]
        if ext is not None:
            ext = hop(ext, shift, lambda s: s)
            continue
        turns_next = k == owners - 1 and (k + 1) % GROUP != 0
        reach = 384 if turns_next else 128
        if fresh or k > owners or main.shape[1] == own:
            main = jnp.concatenate([current, meta], axis=1)
            low, high = current[:, :reach], current[:, own - reach :]
            edge_a, edge_b = jnp.where(even, high, low), jnp.where(even, low, high)
        main = hop(main, shift, lambda s: s)
        edge_a, edge_b = hop(edge_a, shift, partner_a), hop(edge_b, shift, partner_b)
        if k >= owners:
            left, right = jnp.where(even, edge_b, edge_a), jnp.where(even, edge_a, edge_b)
            ext = jnp.concatenate([left, main[:, :own], right, main[:, own:]], axis=1)
    return result[0][None], result[1][None]


def solution(mesh):
    return jax.shard_map(
        shards,
        mesh=mesh,
        in_specs=(
            P(None, "space"),
            P("tm", "space", None, None),
            P("tm", "space", None),
            P("tm", None, None, None),
        ),
        out_specs=(P("tm", None, "space"), P("tm", None, "space")),
        check_vma=False,
    )
```

time: 224 us -> 48.1 us (0.21)
  blocking collectives: 121 us -> 14.5 us
  local copies, waits for them, and re-layouts: 26.8 us -> 1.93 us
  starting transfers between devices: 38.8 us -> 17.7 us
  matrix products: 13.4 us -> 0 us
  waiting for transfers between devices: 14.4 us -> 6.32 us
  other arithmetic: 6.87 us -> 0.09 us
  Pallas kernels: 0 us -> 6.46 us
    psum x4 -> x0, blocking collectives: 121 us -> none  [rescale(): all_sums = lax.psum(own_sums, 'space')]
    ppermute x14 -> x8, starting transfers between devices: 38.8 us -> 17.7 us  [the longest x4 11.9 us: hop(): return lax.ppermute(x, ('tm', 'space'), route)]
    all_to_all x0 -> x1, blocking collectives: none -> 14.5 us  [shards(): grams = lax.all_to_all(every, 'space', 0, 0)]
    dot_general x16 -> x0, matrix products: 13.4 us -> none  [the longest x4 6.05 us: pull_step(): jnp.einsum('bjik,cbi->cbjk', matrices, reshaped_block, precision=lax.Prec...]
    squeeze x12 -> x0, local copies, waits for them, and re-layouts: 12.5 us -> none  [the longest x4 6.2 us: push_step(): matrices = blocks_here.reshape(count_blocks, 3, BLOCK, BLOCK)]
    ppermute x14 -> x8, waiting for transfers between devices: 14.4 us -> 6.32 us  [the longest x4 6.31 us: hop(): return lax.ppermute(x, ('tm', 'space'), route)]
    slice x17 -> x3, local copies, waits for them, and re-layouts: 6.67 us -> 0.01 us  [the longest x1 0.01 us: shards(): every = jnp.broadcast_to(meta[None, :COLS], (count, COLS, 128))]
    pallas_call x0 -> x8, Pallas kernels: none -> 6.46 us  [call(): pl.pallas_call(kernel, out_shape=shapes, in_specs=[VM] * len(args), out_s...]
  transfers between devices with their start and end apart: 14 -> 8, of which waited for: 5 -> 3; matrix products, arithmetic and copies ran while one was open for 8% -> 0% of each run, Pallas kernels for 0% -> 5%
where the time goes in v1:
time: 48.1 us; the launch traced here: 47.8 us
  starting transfers between devices  17.7 us (37%)
  blocking collectives  14.5 us (30%)
  Pallas kernels  6.46 us (13%)
  waiting for transfers between devices  6.32 us (13%)
  local copies, waits for them, and re-layouts  1.93 us (4%)
  between operations  0.79 us (2%)
    all_to_all x1, blocking collectives, shards(): grams = lax.all_to_all(every, 'space', 0, 0)  14.5 us
    ppermute x4, starting transfers between devices, hop(): return lax.ppermute(x, ('tm', 'space'), route)  11.9 us
    pallas_call x8, Pallas kernels, call(): pl.pallas_call(kernel, out_shape=shapes, in_specs=[VM] * len(args), out_s...  6.46 us
    ppermute x4, waiting for transfers between devices, hop(): return lax.ppermute(x, ('tm', 'space'), route)  6.31 us
    ppermute x4, starting transfers between devices, beside(): return lax.ppermute(x, 'space', [(s, to(s)) for s in range(count)])  5.8 us
    unnamed x8, local copies, waits for them, and re-layouts  1.82 us
  transfers between devices with their start and end apart: 8, of which 3 were waited for; matrix products, arithmetic and copies ran while one was open for 0% of the time, Pallas kernels for 5%

profile of v1, /device:TPU:0, one launch (start us, length us, event | category | flops | bytes accessed | tf_op | source)
XLA Modules:
  0.0 47.8 jit_solution(3365249886818397981)
XLA Ops:
  0.7 0.0 copy-start.3
  0.7 0.7 %copy-done.3 = s32[2,8,3]{1,0,2:T(2,128)S(1)} copy-done((s32[2,8,3]{1,0,2:T(2,128)S(1)}, s32[2,8,3]{1,0,2:T(2,128)}, u32[]{:S(2)}) %copy-start.3) | copy-done | bytes 216
  1.4 0.1 fusion.1
  1.4 0.1 broadcast_in_dim.24.mask
  1.5 0.0 copy-start
  1.5 1.1 %copy-done = f32[2,8,3,4096]{3,1,2,0:T(8,128)S(1)} copy-done((f32[2,8,3,4096]{3,1,2,0:T(8,128)S(1)}, f32[2,8,3,4096]{3,1,2,0:T(8,128)}, u32[]{:S(2)}) %copy-start) | copy-done | bytes 786456
  2.6 0.0 copy-start.1
  2.6 0.5 %shard_map.62 = (f32[768,128]{1,0:T(8,128)S(1)}, f32[768,128]{1,0:T(8,128)S(1)}) custom-call(f32[2,3,8,4096]{3,2,1,0:T(8,128)S(1)} %bitcast.5, f32[2,3,8,128]{3,2,1,0:T(8,128)S(1)} %broadcast_in_dim.24.mask), custom_call_target="tpu_custom_call" | custom-call | flops 1000000 | bytes 1000000 | tf_op jit(solution)/shard_map/pallas_call | solution.py:30
  3.2 0.5 %collective-permute-start.5 = (f32[768,128]{1,0:T(8,128)S(1)}, f32[768,128]{1,0:T(8,128)S(1)}, u32[]{:S(2)}, u32[]{:S(2)}) collective-permute-start(f32[768,128]{1,0:T(8,128)S(1)} %get-tuple-element.37), channel_id=1, source_target_pairs={{0,1},{1,0},{2,3},{3,2},{4,5},{5,4},{6,7},{7,6},{8,9},{9,8},{10,11... | collective-permute-start | bytes 1179656 | tf_op jit(solution)/shard_map/ppermute | solution.py:354
  3.7 0.0 copy-start.2
  3.7 0.8 %collective-permute-start.6 = (f32[768,128]{1,0:T(8,128)S(1)}, f32[768,128]{1,0:T(8,128)S(1)}, u32[]{:S(2)}, u32[]{:S(2)}) collective-permute-start(f32[768,128]{1,0:T(8,128)S(1)} %get-tuple-element.38), channel_id=1, source_target_pairs={{0,0},{1,2},{2,1},{3,4},{4,3},{5,6},{6,5},{7,8},{8,7},{9,10},{10,9... | collective-permute-start | bytes 1179656 | tf_op jit(solution)/shard_map/ppermute | solution.py:354
  4.5 0.0 copy-done.1
  4.5 0.2 shard_map.59
  4.7 3.8 %collective-permute-start = (f32[128,128]{1,0:T(8,128)S(1)}, f32[128,128]{1,0:T(8,128)S(1)}, u32[]{:S(2)}, u32[]{:S(2)}) collective-permute-start(f32[128,128]{1,0:T(8,128)S(1)} %get-tuple-element.26), channel_id=1, source_target_pairs={{0,1},{1,0},{2,3},{3,2},{4,5},{5,4},{6,7},{7,6},{8,9},{9,8},{10,11... | collective-permute-start | bytes 196616 | tf_op jit(solution)/shard_map/ppermute | solution.py:354
  8.5 0.7 %collective-permute-start.1 = (f32[128,128]{1,0:T(8,128)S(1)}, f32[128,128]{1,0:T(8,128)S(1)}, u32[]{:S(2)}, u32[]{:S(2)}) collective-permute-start(f32[128,128]{1,0:T(8,128)S(1)} %get-tuple-element.27), channel_id=1, source_target_pairs={{0,0},{1,2},{2,1},{3,4},{4,3},{5,6},{6,5},{7,8},{8,7},{9,10},{10,9... | collective-permute-start | bytes 196616 | tf_op jit(solution)/shard_map/ppermute | solution.py:354
  9.1 0.0 copy-done.2
  9.2 1.1 %shard_map.60 = (bf16[512,256]{1,0:T(8,128)(2,1)S(1)}, bf16[512,256]{1,0:T(8,128)(2,1)S(1)}, bf16[512,256]{1,0:T(8,128)(2,1)S(1)}, bf16[512,256]{1,0:T(8,128)(2,1)S(1)}, f32[16,128]{1,0:T(8,128)S(1)}) custom-call(f32[2,3,8,4096]{3,2,1,0:T(8,128)S(1)} %bitcast.7, f32[2,3,8,128]{3,2,1,0:T(8,128)S(1)} %broadcast_in_dim.24.mask, f32[2,4,8,8]{3,2,1,0:T(8,128)S(1)} %copy-done.2), custom_call_target="tpu_custom_call" | custom-call | flops 1000000 | bytes 1000000 | tf_op jit(solution)/shard_map/pallas_call | solution.py:30
  10.2 0.0 collective-permute-done.near_a
  10.3 0.0 collective-permute-done.1.near_b
  10.3 1.0 %shard_map.61 = (f32[32,640]{1,0:T(8,128)S(1)}, f32[32,384]{1,0:T(8,128)S(1)}, f32[32,384]{1,0:T(8,128)S(1)}, f32[32,128]{1,0:T(8,128)S(1)}) custom-call(f32[32,128]{1,0:T(8,128)S(1)} %broadcast_in_dim.12.old, f32[32,512]{1,0:T(8,128)S(1)} %copy-done.1, f32[32,128]{1,0:T(8,128)S(1)} %slice.12.edge_a, f32[32,128]{1,0:T(8,128)S(1)} %slice.13.edge_b, ...), custom_call_target="tpu_custom_call" | custom-call | flops 1000000 | bytes 1000000 | tf_op jit(solution)/shard_map/pallas_call | solution.py:30
  11.3 0.6 %collective-permute-start.2 = (f32[32,640]{1,0:T(8,128)S(1)}, f32[32,640]{1,0:T(8,128)S(1)}, u32[]{:S(2)}, u32[]{:S(2)}) collective-permute-start(f32[32,640]{1,0:T(8,128)S(1)} %get-tuple-element.34.refs_0_), channel_id=1, source_target_pairs={{0,16},{1,17},{2,18},{3,19},{4,20},{5,21},{6,22},{7,23},{8,24},{9,... | collective-permute-start | bytes 245768 | tf_op jit(solution)/shard_map/ppermute | solution.py:360
  11.9 9.0 %collective-permute-start.3 = (f32[32,384]{1,0:T(8,128)S(1)}, f32[32,384]{1,0:T(8,128)S(1)}, u32[]{:S(2)}, u32[]{:S(2)}) collective-permute-start(f32[32,384]{1,0:T(8,128)S(1)} %get-tuple-element.35), channel_id=1, source_target_pairs={{0,17},{1,16},{2,19},{3,18},{4,21},{5,20},{6,23},{7,22},{8,25},{9,... | collective-permute-start | bytes 147464 | tf_op jit(solution)/shard_map/ppermute | solution.py:360
  20.9 0.5 %collective-permute-start.4 = (f32[32,384]{1,0:T(8,128)S(1)}, f32[32,384]{1,0:T(8,128)S(1)}, u32[]{:S(2)}, u32[]{:S(2)}) collective-permute-start(f32[32,384]{1,0:T(8,128)S(1)} %get-tuple-element.36), channel_id=1, source_target_pairs={{0,16},{1,18},{2,17},{3,20},{4,19},{5,22},{6,21},{7,24},{8,23},{9,... | collective-permute-start | bytes 147464 | tf_op jit(solution)/shard_map/ppermute | solution.py:360
  21.4 0.0 collective-permute-done.5.far_a
  21.4 0.0 collective-permute-done.6.far_b
  21.4 0.4 shard_map.63
  21.8 2.3 %collective-permute-done.3.edge_a = f32[32,384]{1,0:T(8,128)S(1)} collective-permute-done((f32[32,384]{1,0:T(8,128)S(1)}, f32[32,384]{1,0:T(8,128)S(1)}, u32[]{:S(2)}, u32[]{:S(2)}) %collective-permute-start.3) | collective-permute-done | bytes 49184 | tf_op jit(solution)/shard_map/ppermute | solution.py:360
  24.1 1.1 %collective-permute-done.4.edge_b = f32[32,384]{1,0:T(8,128)S(1)} collective-permute-done((f32[32,384]{1,0:T(8,128)S(1)}, f32[32,384]{1,0:T(8,128)S(1)}, u32[]{:S(2)}, u32[]{:S(2)}) %collective-permute-start.4) | collective-permute-done | bytes 49184 | tf_op jit(solution)/shard_map/ppermute | solution.py:360
  25.2 0.0 collective-permute-done.2.main
  25.2 1.8 %collective-permute-start.7 = (f32[32,896]{1,0:T(8,128)S(1)}, f32[32,896]{1,0:T(8,128)S(1)}, u32[]{:S(2)}, u32[]{:S(2)}) collective-permute-start(f32[32,896]{1,0:T(8,128)S(1)} %get-tuple-element.44.refs_2_), channel_id=1, source_target_pairs={{0,16},{1,17},{2,18},{3,19},{4,20},{5,21},{6,22},{7,23},{8,24},{9,... | collective-permute-start | bytes 344072 | tf_op jit(solution)/shard_map/ppermute | solution.py:360
  27.0 3.0 %collective-permute-done.7.ext = f32[32,896]{1,0:T(8,128)S(1)} collective-permute-done((f32[32,896]{1,0:T(8,128)S(1)}, f32[32,896]{1,0:T(8,128)S(1)}, u32[]{:S(2)}, u32[]{:S(2)}) %collective-permute-start.7) | collective-permute-done | bytes 114720 | tf_op jit(solution)/shard_map/ppermute | solution.py:360
  30.0 0.8 %shard_map.65 = (f32[32,512]{1,0:T(8,128)S(1)}, f32[32,128]{1,0:T(8,128)S(1)}) custom-call(f32[32,128]{1,0:T(8,128)S(1)} %get-tuple-element.43.old, f32[32,896]{1,0:T(8,128)S(1)} %collective-permute-done.7.ext, bf16[512,256]{1,0:T(8,128)(2,1)S(1)} %get-tuple-element.28.a_hi, bf16[512,256]{1,0:T(8,128)(2,1)S(1)} %get-tuple-element.29.a_lo, ...), custom_call_target="tpu_custom_call" | custom-call | flops 1000000 | bytes 1000000 | tf_op jit(solution)/shard_map/pallas_call | solution.py:30
  30.7 14.5 %all_to_all.5.grams = f32[16,8,128]{2,1,0:T(8,128)S(1)} all-to-all(f32[16,8,128]{2,1,0:T(8,128)S(1)} %broadcast_in_dim.25), channel_id=1, replica_groups=mesh['tm'=2,'space'=16] {'space'}, dimensions={0} | all-to-all | bytes 131072 | tf_op jit(solution)/shard_map/all_to_all | solution.py:436
  45.2 2.6 %shard_map.66 = (f32[32,512]{1,0:T(8,128)}, f32[32,512]{1,0:T(8,128)}) custom-call(f32[16,8,128]{2,1,0:T(8,128)S(1)} %all_to_all.5.grams, f32[32,128]{1,0:T(8,128)S(1)} %get-tuple-element.45.meta, f32[32,640]{1,0:T(8,128)S(1)} %get-tuple-element.34.refs_0_, f32[32,512]{1,0:T(8,128)S(1)} %get-tuple-element.46.refs_1_, ...), custom_call_target="tpu_custom_call" | custom-call | flops 1000000 | bytes 1000000 | tf_op jit(solution)/shard_map/pallas_call | solution.py:30
  (9 shorter events, 0.0 us)
Async XLA Ops:
  0.7 0.7 %copy-start.3 = (s32[2,8,3]{1,0,2:T(2,128)S(1)}, s32[2,8,3]{1,0,2:T(2,128)}, u32[]{:S(2)}) copy-start(s32[2,8,3]{1,0,2:T(2,128)} %param.6) | copy-start | bytes 580
  1.5 1.1 %copy-start = (f32[2,8,3,4096]{3,1,2,0:T(8,128)S(1)}, f32[2,8,3,4096]{3,1,2,0:T(8,128)}, u32[]{:S(2)}) copy-start(f32[2,8,3,4096]{3,1,2,0:T(8,128)} %param.5) | copy-start | bytes 2359300
  2.6 1.8 %copy-start.1 = (f32[32,512]{1,0:T(8,128)S(1)}, f32[32,512]{1,0:T(8,128)}, u32[]{:S(2)}) copy-start(f32[32,512]{1,0:T(8,128)} %main.1) | copy-start | bytes 196612
  3.2 18.3 %collective-permute-start.5 = (f32[768,128]{1,0:T(8,128)S(1)}, f32[768,128]{1,0:T(8,128)S(1)}, u32[]{:S(2)}, u32[]{:S(2)}) collective-permute-start(f32[768,128]{1,0:T(8,128)S(1)} %get-tuple-element.37), channel_id=1, source_target_pairs={{0,1},{1,0},{2,3},{3,2},{4,5},{5,4},{6,7},{7,6},{8,9},{9,8},{10,11... | collective-permute-start | bytes 1179656 | tf_op jit(solution)/shard_map/ppermute | solution.py:354
  3.7 5.5 %copy-start.2 = (f32[2,4,8,8]{3,2,1,0:T(8,128)S(1)}, f32[2,4,8,8]{3,2,1,0:T(8,128)}, u32[]{:S(2)}) copy-start(f32[2,4,8,8]{3,2,1,0:T(8,128)} %mixing.1) | copy-start | bytes 6148
  3.7 17.8 %collective-permute-start.6 = (f32[768,128]{1,0:T(8,128)S(1)}, f32[768,128]{1,0:T(8,128)S(1)}, u32[]{:S(2)}, u32[]{:S(2)}) collective-permute-start(f32[768,128]{1,0:T(8,128)S(1)} %get-tuple-element.38), channel_id=1, source_target_pairs={{0,0},{1,2},{2,1},{3,4},{4,3},{5,6},{6,5},{7,8},{8,7},{9,10},{10,9... | collective-permute-start | bytes 1179656 | tf_op jit(solution)/shard_map/ppermute | solution.py:354
  4.7 5.6 %collective-permute-start = (f32[128,128]{1,0:T(8,128)S(1)}, f32[128,128]{1,0:T(8,128)S(1)}, u32[]{:S(2)}, u32[]{:S(2)}) collective-permute-start(f32[128,128]{1,0:T(8,128)S(1)} %get-tuple-element.26), channel_id=1, source_target_pairs={{0,1},{1,0},{2,3},{3,2},{4,5},{5,4},{6,7},{7,6},{8,9},{9,8},{10,11... | collective-permute-start | bytes 196616 | tf_op jit(solution)/shard_map/ppermute | solution.py:354
  8.5 1.8 %collective-permute-start.1 = (f32[128,128]{1,0:T(8,128)S(1)}, f32[128,128]{1,0:T(8,128)S(1)}, u32[]{:S(2)}, u32[]{:S(2)}) collective-permute-start(f32[128,128]{1,0:T(8,128)S(1)} %get-tuple-element.27), channel_id=1, source_target_pairs={{0,0},{1,2},{2,1},{3,4},{4,3},{5,6},{6,5},{7,8},{8,7},{9,10},{10,9... | collective-permute-start | bytes 196616 | tf_op jit(solution)/shard_map/ppermute | solution.py:354
  11.3 13.9 %collective-permute-start.2 = (f32[32,640]{1,0:T(8,128)S(1)}, f32[32,640]{1,0:T(8,128)S(1)}, u32[]{:S(2)}, u32[]{:S(2)}) collective-permute-start(f32[32,640]{1,0:T(8,128)S(1)} %get-tuple-element.34.refs_0_), channel_id=1, source_target_pairs={{0,16},{1,17},{2,18},{3,19},{4,20},{5,21},{6,22},{7,23},{8,24},{9,... | collective-permute-start | bytes 245768 | tf_op jit(solution)/shard_map/ppermute | solution.py:360
  11.9 12.2 %collective-permute-start.3 = (f32[32,384]{1,0:T(8,128)S(1)}, f32[32,384]{1,0:T(8,128)S(1)}, u32[]{:S(2)}, u32[]{:S(2)}) collective-permute-start(f32[32,384]{1,0:T(8,128)S(1)} %get-tuple-element.35), channel_id=1, source_target_pairs={{0,17},{1,16},{2,19},{3,18},{4,21},{5,20},{6,23},{7,22},{8,25},{9,... | collective-permute-start | bytes 147464 | tf_op jit(solution)/shard_map/ppermute | solution.py:360
  20.9 4.2 %collective-permute-start.4 = (f32[32,384]{1,0:T(8,128)S(1)}, f32[32,384]{1,0:T(8,128)S(1)}, u32[]{:S(2)}, u32[]{:S(2)}) collective-permute-start(f32[32,384]{1,0:T(8,128)S(1)} %get-tuple-element.36), channel_id=1, source_target_pairs={{0,16},{1,18},{2,17},{3,20},{4,19},{5,22},{6,21},{7,24},{8,23},{9,... | collective-permute-start | bytes 147464 | tf_op jit(solution)/shard_map/ppermute | solution.py:360
  25.2 4.8 %collective-permute-start.7 = (f32[32,896]{1,0:T(8,128)S(1)}, f32[32,896]{1,0:T(8,128)S(1)}, u32[]{:S(2)}, u32[]{:S(2)}) collective-permute-start(f32[32,896]{1,0:T(8,128)S(1)} %get-tuple-element.44.refs_2_), channel_id=1, source_target_pairs={{0,16},{1,17},{2,18},{3,19},{4,20},{5,21},{6,22},{7,23},{8,24},{9,... | collective-permute-start | bytes 344072 | tf_op jit(solution)/shard_map/ppermute | solution.py:360

commit v2 on v1

--- a/solution.py
+++ b/solution.py
@@ -25,16 +25,16 @@
 VM = pl.BlockSpec(memory_space=pltpu.VMEM)
 
 
-def call(kernel, outs, args, scratch=(), flops=10**6):
+def call(kernel, outs, args, scratch=(), flops=10**6, far=0, limit=12):
     shapes = [jax.ShapeDtypeStruct(shape, dtype) for shape, dtype in outs]
     return pl.pallas_call(
         kernel,
         out_shape=shapes,
-        in_specs=[VM] * len(args),
+        in_specs=[pl.BlockSpec(memory_space=pltpu.HBM)] * far + [VM] * (len(args) - far),
         out_specs=[VM] * len(outs),
         scratch_shapes=list(scratch),
-        compiler_params=pltpu.CompilerParams(vmem_limit_bytes=12 << 20),
-        cost_estimate=pl.CostEstimate(flops=flops, bytes_accessed=10**6, transcendentals=0),
+        compiler_params=pltpu.CompilerParams(vmem_limit_bytes=limit << 20),
+        cost_estimate=pl.CostEstimate(flops=flops, bytes_accessed=10**5, transcendentals=0),
     )(*args)
 
 
@@ -51,46 +51,61 @@
     return lax.broadcasted_iota(jnp.int32, shape, dim)
 
 
-def edge_kernel(nb, blocks, mask, panels, to_a, to_b):
+def presence(mask, t, j, nb):
+    place, last = lax.axis_index("space"), lax.axis_size("space") - 1
+    here = jnp.broadcast_to(mask[j, t : t + 1, :], (nb, nb))
+    diagonal = iota((nb, nb), 0) == iota((nb, nb), 1)
+    column = jnp.sum(jnp.where(diagonal, here, 0), axis=1, keepdims=True).astype(F32)
+    if j == 0:
+        column = jnp.where((iota((nb, 1), 0) == 0) & (place == 0), 0.0, column)
+    if j == 2:
+        column = jnp.where((iota((nb, 1), 0) == nb - 1) & (place == last), 0.0, column)
+    return column
+
+
+def first_kernel(out):
+    out[...] = jnp.zeros_like(out)
+
+
+def edge_kernel(nb, turning, _, blocks, mask, panels, near_b, to_a, *far_b):
     width = panels.shape[1]
-
-    def emit(dst, row, start, keep=1.0):
-        for j in range(3):
-            line = blocks[0, j, row : row + 1, :] * (mask[0, j, row : row + 1, 0:1] * keep)
+    turns = lax.axis_index("tm") == turning
+
+    def near(dst, low_side, column, keep=1.0):
+        edge = 0 if low_side else nb - 1
+        inner = 1 if low_side else nb - 2
+        rest = [(edge, 0), (edge, 1), (inner, 0)] if low_side else [(inner, 2), (edge, 1), (edge, 2)]
+        slots = [(0, edge, j, j) for j in range(3)] + [(1, b, j, 4 + i) for i, (b, j) in enumerate(rest)]
+        for t, b, j, slot in slots:
+            line = blocks[t, j, b : b + 1, :] * (column[t][j][b : b + 1, :] * keep)
             for r in range(32):
-                dst[j * 32 + r : j * 32 + r + 1, :] = line[:, r * 128 : (r + 1) * 128]
-        dst[96:128, :] = panels[:, start : start + 128]
-
-    @pl.when(parity() == 0)
-    def _():
-        emit(to_a, nb - 1, width - 128)
-        emit(to_b, 0, 0, inside())
-
-    @pl.when(parity() == 1)
-    def _():
-        emit(to_a, 0, 0)
-        emit(to_b, nb - 1, width - 128, inside())
-
-
-def far_kernel(nb, blocks, mask, to_a, to_b):
-    def emit(dst, row_a, row_b, keep=1.0):
-        for j in range(3):
+                dst[slot * 32 + r : slot * 32 + r + 1, :] = line[:, r * 128 : (r + 1) * 128]
+        dst[96:128, :] = panels[:, :128] if low_side else panels[:, width - 128 :]
+
+    for side in range(2):
+
+        @pl.when((parity() == side) & jnp.logical_not(turns))
+        def _():
+            column = [[presence(mask, t, j, nb) for j in range(3)] for t in range(RUN)]
+            near(near_b, side == 0, column, inside())
+            near(to_a, side == 1, column)
+
+    if not far_b:
+        return
+
+    @pl.when(turns)
+    def _():
+        even = parity() == 0
+        keep = inside()
+        for t, rows, start in ((0, RIM_A, 0), (1, RIM_B, 96 * RIM_A)):
+            column = [jnp.broadcast_to(presence(mask, t, j, nb), (nb, 128)) for j in range(3)]
             for r in range(32):
-                lanes = slice(r * 128, (r + 1) * 128)
-                va = blocks[0, j, :, lanes] * (mask[0, j] * keep)
-                vb = blocks[1, j, :, lanes] * (mask[1, j] * keep)
-                dst[pl.ds(j * 32 + r, RIM_A - 1, stride=96), :] = va[row_a : row_a + RIM_A - 1]
-                dst[pl.ds(96 * (RIM_A - 1) + j * 32 + r, RIM_B, stride=96), :] = vb[row_b : row_b + RIM_B]
-
-    @pl.when(parity() == 0)
-    def _():
-        emit(to_a, nb - RIM_A, nb - RIM_B)
-        emit(to_b, 1, 0, inside())
-
-    @pl.when(parity() == 1)
-    def _():
-        emit(to_a, 1, 0)
-        emit(to_b, nb - RIM_A, nb - RIM_B, inside())
+                for j in range(3):
+                    y = blocks[t, j, :, r * 128 : (r + 1) * 128] * column[j]
+                    to = pl.ds(start + j * 32 + r, rows, stride=96)
+                    head, tail = y[:rows], y[nb - rows :]
+                    to_a[to, :] = jnp.where(even, tail, head)
+                    far_b[0][to, :] = jnp.where(even, head, tail) * keep
 
 
 def banded(y, p):
@@ -108,6 +123,13 @@
     return high, (x - high.astype(F32)).astype(BF)
 
 
+def split3(x):
+    first = x.astype(BF)
+    x = x - first.astype(F32)
+    second = x.astype(BF)
+    return first, second, (x - second.astype(F32)).astype(BF)
+
+
 def split_halves(wide, at, hi, lo):
     for half in range(2):
         lanes = slice(half * 128, half * 128 + 128)
@@ -117,9 +139,10 @@
 def own_kernel(nb, blocks, mask, mixing, a_hi, a_lo, b_hi, b_lo, expand, wide):
     for t, hi, lo in ((0, a_hi, a_lo), (1, b_hi, b_lo)):
         is_first = lax.rem(iota((nb, 128), 0), 2) == (1 - t)
+        column = [jnp.broadcast_to(presence(mask, t, j, nb), (nb, 128)) for j in range(3)]
         for r in range(32):
             lanes = slice(r * 128, (r + 1) * 128)
-            y = [blocks[t, j, :, lanes] * mask[t, j] for j in range(3)]
+            y = [blocks[t, j, :, lanes] * column[j] for j in range(3)]
             for p in range(2):
                 first, second = banded(y, p)
                 for half in range(2):
@@ -142,28 +165,45 @@
         )
 
 
-def rim_row(dst, index, first, from_a, from_b, base, left):
+def taken(from_a, from_b, left, start):
     use_b = (parity() == 0) == left
-    y = []
-    for j in range(3):
-        rows = slice(base + j * 32, base + j * 32 + 32)
-        y.append(jnp.where(use_b, from_b[rows, :], from_a[rows, :]))
+    return jnp.where(use_b, from_b[start : start + 32, :], from_a[start : start + 32, :])
+
+
+def rim_row(dst, index, first, y):
     for p in range(2):
         tiles = banded(y, p)[0 if first else 1]
         for half in range(2):
             dst[half, pl.ds(index * BLOCK + p, 32, stride=2), :] = tiles[half]
 
 
-def rim_kernel(near_a, near_b, far_a, far_b, a_hi, a_lo, b_hi, b_lo, wide_a, wide_b):
-    for i in range(RIM_A - 1):
-        rim_row(wide_a, i, (RIM_A - i) % 2 == 1, far_a, far_b, i * 96, True)
-        rim_row(wide_a, RIM_A + 1 + i, i % 2 == 0, far_a, far_b, i * 96, False)
-    rim_row(wide_a, RIM_A - 1, True, near_a, near_b, 0, True)
-    rim_row(wide_a, RIM_A, False, near_a, near_b, 0, False)
-    for i in range(RIM_B):
-        base = (RIM_A - 1 + i) * 96
-        rim_row(wide_b, i, (RIM_B - i) % 2 == 0, far_a, far_b, base, True)
-        rim_row(wide_b, RIM_B + i, i % 2 == 0, far_a, far_b, base, False)
+def edge_rows(near_a, near_b, dst):
+    for left in (True, False):
+        rim_row(dst, 1 - left, left, [taken(near_a, near_b, left, j * 32) for j in range(3)])
+
+
+def rim_kernel(turning, far_b, far_a, a_hi, a_lo, b_hi, b_lo, wide_a, wide_b):
+    @pl.when(lax.axis_index("tm") == turning)
+    def _():
+        for dst, depth, start, odd in ((wide_a, RIM_A, 0, 1), (wide_b, RIM_B, 96 * RIM_A, 0)):
+            for i in range(depth):
+                for left in (True, False):
+                    y = [taken(far_a, far_b, left, start + i * 96 + j * 32) for j in range(3)]
+                    place = i - depth if left else i
+                    rim_row(dst, i if left else depth + i, place % 2 == odd, y)
+        split_halves(wide_a, 0, a_hi, a_lo)
+        split_halves(wide_b, 0, b_hi, b_lo)
+
+
+def pull_rim_kernel(near_a, near_b, a_hi, a_lo, b_hi, b_lo, wide_a, wide_b):
+    edge_rows(near_a, near_b, wide_a)
+    none = jnp.zeros((32, 128), F32)
+    left = [taken(near_a, near_b, True, (4 + i) * 32) for i in range(3)]
+    right = [taken(near_a, near_b, False, (4 + i) * 32) for i in range(3)]
+    rim_row(wide_b, 0, True, [none, none, left[0]])
+    rim_row(wide_b, 1, False, [none, left[1], left[2]])
+    rim_row(wide_b, 2, True, [right[0], right[1], none])
+    rim_row(wide_b, 3, False, [right[2], none, none])
     split_halves(wide_a, 0, a_hi, a_lo)
     split_halves(wide_b, 0, b_hi, b_lo)
 
@@ -211,10 +251,7 @@
 
 
 def gram(u):
-    u1, rest = u.astype(BF), u
-    rest = rest - u1.astype(F32)
-    u2 = rest.astype(BF)
-    u3 = (rest - u2.astype(F32)).astype(BF)
+    u1, u2, u3 = split3(u)
     stack = jnp.concatenate([u3, u2, u1], axis=0)
     total = None
     for part in (u3, u2, u1):
@@ -240,7 +277,7 @@
     return jnp.where(even, e_b, e_a), jnp.where(even, e_a, e_b)
 
 
-def push_kernel(nb, owner, slot, reach, old, main, edge_a, edge_b, near_a, near_b, a_hi, a_lo, b_hi, b_lo, expand,
+def push_kernel(nb, owner, slot, reach, old, edge_b, main, edge_a, near_b, near_a, a_hi, a_lo, b_hi, b_lo, expand,
                 out, out_a, out_b, meta, wide):
     own = nb * BLOCK
 
@@ -250,8 +287,7 @@
 
     @pl.when(lax.axis_index("tm") == owner)
     def _():
-        rim_row(wide, 0, True, near_a, near_b, 0, True)
-        rim_row(wide, 1, False, near_a, near_b, 0, False)
+        edge_rows(near_a, near_b, wide)
         rim_hi, rim_lo = split2(jnp.concatenate([wide[0], wide[1]], axis=1))
         w_edge = edge_a.shape[1]
         left, right = by_side(edge_a[...], edge_b[...])
@@ -267,7 +303,7 @@
         out_b[...], out_a[...] = by_side(high, low)
 
 
-def turn_kernel(nb, owner, slot, old, main, edge_a, edge_b, a_hi, a_lo, b_hi, b_lo, ra_hi, ra_lo, rb_hi, rb_lo,
+def turn_kernel(nb, owner, slot, old, edge_b, main, edge_a, a_hi, a_lo, b_hi, b_lo, ra_hi, ra_lo, rb_hi, rb_lo,
                 expand, first_out, out, meta):
     own = nb * BLOCK
 
@@ -301,39 +337,60 @@
 
     @pl.when(lax.axis_index("tm") == owner)
     def _():
-        y = pull(ext[:, : own + 256], tiles_of((b_hi, b_lo, rb_hi, rb_lo), RIM_B, nb, -2, nb + 2))
-        u = pull(y, tiles_of((a_hi, a_lo, ra_hi, ra_lo), RIM_A, nb, -1, nb + 1))
+        y = pull(ext[:, : own + 256], tiles_of((b_hi, b_lo, rb_hi, rb_lo), 2, nb, -2, nb + 2))
+        u = pull(y, tiles_of((a_hi, a_lo, ra_hi, ra_lo), 1, nb, -1, nb + 1))
         out[...] = u
         meta[...] = noted(ext[:, own + 256 :], slot, gram(u), expand[COLS:])
+
+
+def exact(x, y):
+    width = y.shape[1]
+    xs, ys = split3(x), split3(y)
+    o = lax.dot_general(
+        jnp.concatenate(xs, axis=0), jnp.concatenate(ys, axis=1), NN, preferred_element_type=F32
+    )
+    piece = [[o[i * ROWS : (i + 1) * ROWS, j * width : (j + 1) * width] for j in range(3)] for i in range(3)]
+    small = (piece[0][2] + piece[2][0]) + piece[1][1]
+    return (small + (piece[0][1] + piece[1][0])) + piece[0][0]
 
 
 def scale_kernel(stages, boxes, offsets, grams, meta, *refs):
     panels, (out_f, out_a) = refs[: len(stages)], refs[len(stages) :]
     own = out_f.shape[1]
-    total = grams[0]
-    for i in range(1, grams.shape[0]):
-        total = total + grams[i]
-    total = total * (1.0 / boxes)
+    parts = [grams[i] for i in range(grams.shape[0])]
+    while len(parts) > 1:
+        parts = [a + b for a, b in zip(parts[::2], parts[1::2])] + parts[len(parts) // 2 * 2 :]
+    total = parts[0] * (1.0 / boxes)
     growth = meta[COLS : 2 * COLS, :]
-    row, lane = iota((ROWS, ROWS), 0), iota((ROWS, ROWS), 1)
-    same = (row // COLS) == (lane // COLS)
+    row, lane = iota((ROWS, 128), 0), iota((ROWS, 128), 1)
+    same = (row // COLS) == (lax.rem(lane, ROWS) // COLS)
     me = lax.axis_index("tm")
 
     def full(x, n):
-        return jnp.where(same, jnp.concatenate([x[:, n * ROWS : (n + 1) * ROWS]] * PANELS, axis=0), 0.0)
-
-    dot = functools.partial(lax.dot_general, precision=HIGH, preferred_element_type=F32)
-    back = None
+        turns = [x if k == n else pltpu.roll(x, ((k - n) % 4) * ROWS, 1) for k in range(4)]
+        group = lane[:COLS] // ROWS
+        spread = turns[0]
+        for k in range(1, 4):
+            spread = jnp.where(group == k, turns[k], spread)
+        return jnp.where(same, jnp.concatenate([spread] * PANELS, axis=0), 0.0)
+
+    back, select = None, {True: None, False: None}
     for n, (owner, forward) in enumerate(stages):
         e = full(growth, n)
-        h = e if back is None else dot(back, e, NN)
-        square = jnp.sum(h * dot(full(total, n), h, NN), axis=0, keepdims=True)
-        back = h / jnp.sqrt(jnp.maximum(square, 0.0) + 1e-06)
-
-        @pl.when(me == owner)
-        def _(n=n, back=back, out=out_f if forward else out_a):
-            u = panels[n][:, offsets[n] : offsets[n] + own]
-            out[...] = dot(back, u, TN)
+        h = e if back is None else exact(back[:, :ROWS], e)
+        square = jnp.sum(h * exact(full(total, n)[:, :ROWS], h), axis=0, keepdims=True)
+        back = h * lax.rsqrt(jnp.maximum(square, 0.0) + 1e-06)
+        u = panels[n][:, offsets[n] : offsets[n] + own]
+        old = select[forward]
+        select[forward] = (back, u) if old is None else (
+            jnp.where(me == owner, back, old[0]), jnp.where(me == owner, u, old[1])
+        )
+    for forward, out in ((True, out_f), (False, out_a)):
+        if select[forward] is None:
+            out[...] = jnp.zeros_like(out)
+        else:
+            b, u = select[forward]
+            out[...] = exact(b[:, :ROWS].T, u)
 
 
 def shards(panels_in, blocks, block_mask, mixing):
@@ -350,8 +407,9 @@
         t = s + 1 if s % 2 else s - 1
         return t if 0 <= t < count else s
 
-    def beside(x, to):
-        return lax.ppermute(x, "space", [(s, to(s)) for s in range(count)])
+    def beside(x, to, only=None):
+        route = [(t * count + s, t * count + to(s)) for t in (only or range(owners)) for s in range(count)]
+        return lax.ppermute(x, ("tm", "space"), route)
 
     def hop(x, shift, to):
         route = [
@@ -359,33 +417,40 @@
         ]
         return lax.ppermute(x, ("tm", "space"), route)
 
-    b, j = iota((RUN, nb, 3), 1), iota((RUN, nb, 3), 2)
-    outside = ((place == 0) & (b == 0) & (j == 0)) | ((place == count - 1) & (b == nb - 1) & (j == 2))
-    present = jnp.where(outside, 0, block_mask).astype(F32).transpose(0, 2, 1)
-    mask = jnp.broadcast_to(present[..., None], (RUN, 3, nb, 128))
-    rows = blocks.transpose(0, 2, 1, 3)
-
-    near = call(functools.partial(edge_kernel, nb), [f32(128, 128)] * 2, (rows, mask, panels_in))
-    near_a, near_b = beside(near[0], partner_a), beside(near[1], partner_b)
-    far_rows = 96 * (RIM_A - 1 + RIM_B)
-    far = call(functools.partial(far_kernel, nb), [f32(far_rows, 128)] * 2, (rows, mask))
-    far_a, far_b = beside(far[0], partner_a), beside(far[1], partner_b)
+    rows, mask = blocks.transpose(0, 2, 1, 3), block_mask.transpose(2, 0, 1)
+    vm = lambda *s: pltpu.VMEM(s, F32)
+    turn = owners % GROUP != 0
+    turning = owners - 1 if turn else owners
+    begin = call(first_kernel, [f32(8, 128)], (), flops=10**9)
+    far_rows = 96 * (RIM_A + RIM_B)
+    sizes = [224, far_rows, far_rows] if turn else [224, 224]
+    edges = call(
+        functools.partial(edge_kernel, nb, turning),
+        [f32(n, 128) for n in sizes],
+        (*begin, rows, mask, panels_in),
+    )
+    near_b, near_a = beside(edges[0], partner_b, range(turning)), beside(edges[1], partner_a)
+    if turn:
+        far_b = beside(edges[2], partner_b, [turning])
+    rows, mask, mixing, _ = lax.optimization_barrier((rows, mask, mixing, edges))
     *own_tiles, expand = call(
         functools.partial(own_kernel, nb),
         [bf(own, 256)] * 4 + [f32(2 * COLS, 128)],
         (rows, mask, mixing),
-        [pltpu.VMEM((2 * RUN, own, 128), F32)],
+        [vm(2 * RUN, own, 128)],
     )
-    depth_a, depth_b = 2 * RIM_A * BLOCK, 2 * RIM_B * BLOCK
-    rim_tiles = call(
-        rim_kernel,
-        [bf(depth_a, 256)] * 2 + [bf(depth_b, 256)] * 2,
-        (near_a, near_b, far_a, far_b),
-        [pltpu.VMEM((2, depth_a, 128), F32), pltpu.VMEM((2, depth_b, 128), F32)],
-    )
+
+    def rim_call(kernel, deep_a, deep_b, args):
+        deep_a, deep_b = 2 * deep_a * BLOCK, 2 * deep_b * BLOCK
+        outs, scratch = [bf(deep_a, 256)] * 2 + [bf(deep_b, 256)] * 2, [vm(2, deep_a, 128), vm(2, deep_b, 128)]
+        return call(kernel, outs, args, scratch)
+
+    pull_rims = rim_call(pull_rim_kernel, 1, 2, (near_a, near_b))
+    if turn:
+        turn_rims = rim_call(functools.partial(rim_kernel, turning), RIM_A, RIM_B, (far_b, near_a))
 
     meta = jnp.zeros((ROWS, 128), F32)
-    main, edge_a, edge_b = panels_in, near_a[96:], near_b[96:]
+    main, edge_a, edge_b = panels_in, near_a[96:128], near_b[96:128]
     ext = None
     stages = 2 * owners
     owner_of = [k if k < owners else stages - 1 - k for k in range(stages)]
@@ -399,7 +464,7 @@
             first, ext, meta = call(
                 functools.partial(turn_kernel, nb, owner, slot),
                 [f32(ROWS, own), f32(ROWS, own + 384), f32(ROWS, 128)],
-                (meta, main, edge_a, edge_b, *own_tiles, *rim_tiles, expand),
+                (meta, edge_b, main, edge_a, *own_tiles, *turn_rims, expand),
             )
             kept += [first, ext]
             offsets += [0, 128]
@@ -410,7 +475,7 @@
             main, edge_a, edge_b, meta = call(
                 functools.partial(push_kernel, nb, owner, slot, reach),
                 [f32(ROWS, own + 128), f32(ROWS, reach), f32(ROWS, reach), f32(ROWS, 128)],
-                (meta, main, edge_a, edge_b, near_a, near_b, *own_tiles, expand),
+                (meta, edge_b, main, edge_a, near_b, near_a, *own_tiles, expand),
                 [pltpu.VMEM((2, 2 * BLOCK, 128), F32)],
             )
             kept.append(main)
@@ -421,7 +486,7 @@
             current, meta = call(
                 functools.partial(pull_kernel, nb, owner, slot),
                 [f32(ROWS, own), f32(ROWS, 128)],
-                (meta, ext, *own_tiles, *rim_tiles, expand),
+                (meta, ext, *own_tiles, *pull_rims, expand),
             )
             ext = None
             kept.append(current)

time: 48.1 us -> 40.3 us (0.84)
  starting transfers between devices: 17.7 us -> 13.8 us
  waiting for transfers between devices: 6.32 us -> 5.25 us
  Pallas kernels: 6.46 us -> 5.46 us
  blocking collectives: 14.5 us -> 13.7 us
  local copies, waits for them, and re-layouts: 1.93 us -> 1.17 us
    ppermute x4 -> x3, starting transfers between devices: 5.8 us -> 1.86 us  [beside(): return lax.ppermute(x, ('tm', 'space'), route)]
    ppermute x4, waiting for transfers between devices: 6.31 us -> 5.25 us  [hop(): return lax.ppermute(x, ('tm', 'space'), route)]
    pallas_call x8 -> x9, Pallas kernels: 6.46 us -> 5.46 us  [call(): pl.pallas_call(kernel, out_shape=shapes, in_specs=[pl.BlockSpec(memory_sp...]
    all_to_all x1, blocking collectives: 14.5 us -> 13.7 us  [shards(): grams = lax.all_to_all(every, 'space', 0, 0)]
    unnamed x8, local copies, waits for them, and re-layouts: 1.82 us -> 1.14 us
  transfers between devices with their start and end apart: 8 -> 7, of which waited for: 3 -> 2; matrix products, arithmetic and copies ran while one was open for 0% -> 0% of each run, Pallas kernels for 5% -> 6%
where the time goes in v2:
time: 40.3 us; the launch traced here: 40.1 us
  starting transfers between devices  13.8 us (34%)
  blocking collectives  13.7 us (34%)
  Pallas kernels  5.46 us (14%)
  waiting for transfers between devices  5.25 us (13%)
  local copies, waits for them, and re-layouts  1.17 us (3%)
  between operations  0.78 us (2%)
    all_to_all x1, blocking collectives, shards(): grams = lax.all_to_all(every, 'space', 0, 0)  13.7 us
    ppermute x4, starting transfers between devices, hop(): return lax.ppermute(x, ('tm', 'space'), route)  11.9 us
    pallas_call x9, Pallas kernels, call(): pl.pallas_call(kernel, out_shape=shapes, in_specs=[pl.BlockSpec(memory_sp...  5.46 us
    ppermute x4, waiting for transfers between devices, hop(): return lax.ppermute(x, ('tm', 'space'), route)  5.25 us
    ppermute x3, starting transfers between devices, beside(): return lax.ppermute(x, ('tm', 'space'), route)  1.86 us
    unnamed x8, local copies, waits for them, and re-layouts  1.14 us
  transfers between devices with their start and end apart: 7, of which 2 were waited for; matrix products, arithmetic and copies ran while one was open for 0% of the time, Pallas kernels for 6%

profile of v2, /device:TPU:0, one launch (start us, length us, event | category | flops | bytes accessed | tf_op | source)
XLA Modules:
  0.0 40.1 jit_solution(12269007870531710780)
XLA Ops:
  0.6 0.0 copy-start.1
  0.6 0.0 copy-start
  0.7 0.0 copy-start.3
  0.7 0.8 %copy-done.1 = f32[32,512]{1,0:T(8,128)S(1)} copy-done((f32[32,512]{1,0:T(8,128)S(1)}, f32[32,512]{1,0:T(8,128)}, u32[]{:S(2)}) %copy-start.1) | copy-done | bytes 65560
  1.5 0.3 copy-done
  1.8 0.0 copy-done.3
  1.8 0.0 copy-start.2
  1.8 0.2 shard_map.60
  2.1 0.5 %collective-permute-start.1 = (f32[864,128]{1,0:T(8,128)S(1)}, f32[864,128]{1,0:T(8,128)S(1)}, u32[]{:S(2)}, u32[]{:S(2)}) collective-permute-start(f32[864,128]{1,0:T(8,128)S(1)} %get-tuple-element.33), channel_id=1, source_target_pairs={{0,1},{1,0},{2,3},{3,2},{4,5},{5,4},{6,7},{7,6},{8,9},{9,8},{10,11... | collective-permute-start | bytes 1327112 | tf_op jit(solution)/shard_map/ppermute | solution.py:412
  2.6 0.7 %collective-permute-start.5 = (f32[864,128]{1,0:T(8,128)S(1)}, f32[864,128]{1,0:T(8,128)S(1)}, u32[]{:S(2)}, u32[]{:S(2)}) collective-permute-start(f32[864,128]{1,0:T(8,128)S(1)} %get-tuple-element.34), channel_id=1, source_target_pairs={{16,16},{17,18},{18,17},{19,20},{20,19},{21,22},{22,21},{23,24},{2... | collective-permute-start | bytes 1327112 | tf_op jit(solution)/shard_map/ppermute | solution.py:412
  3.3 0.7 %collective-permute-start = (f32[224,128]{1,0:T(8,128)S(1)}, f32[224,128]{1,0:T(8,128)S(1)}, u32[]{:S(2)}, u32[]{:S(2)}) collective-permute-start(f32[224,128]{1,0:T(8,128)S(1)} %get-tuple-element.32), channel_id=1, source_target_pairs={{0,0},{1,2},{2,1},{3,4},{4,3},{5,6},{6,5},{7,8},{8,7},{9,10},{10,9... | collective-permute-start | bytes 344072 | tf_op jit(solution)/shard_map/ppermute | solution.py:412
  3.9 0.0 copy-done.2
  3.9 1.2 %shard_map.61 = (bf16[512,256]{1,0:T(8,128)(2,1)S(1)}, bf16[512,256]{1,0:T(8,128)(2,1)S(1)}, bf16[512,256]{1,0:T(8,128)(2,1)S(1)}, bf16[512,256]{1,0:T(8,128)(2,1)S(1)}, f32[16,128]{1,0:T(8,128)S(1)}) custom-call(f32[2,3,8,4096]{3,2,1,0:T(8,128)S(1)} %bitcast.5, s32[3,2,8]{2,1,0:T(2,128)S(1)} %bitcast.7, f32[2,4,8,8]{3,2,1,0:T(8,128)S(1)} %copy-done.2), custom_call_target="tpu_custom_call" | custom-call | flops 1000000 | bytes 100000 | tf_op jit(solution)/shard_map/pallas_call | solution.py:30
  5.2 0.0 collective-permute-done.near_b
  5.2 0.0 collective-permute-done.1.near_a.far_a
  5.2 1.0 %shard_map.62 = (f32[32,640]{1,0:T(8,128)S(1)}, f32[32,384]{1,0:T(8,128)S(1)}, f32[32,384]{1,0:T(8,128)S(1)}, f32[32,128]{1,0:T(8,128)S(1)}) custom-call(f32[32,128]{1,0:T(8,128)S(1)} %broadcast_in_dim.15.old, f32[32,128]{1,0:T(8,128)S(1)} %slice.12.edge_b, f32[32,512]{1,0:T(8,128)S(1)} %copy-done.1, f32[32,128]{1,0:T(8,128)S(1)} %slice.13.edge_a, ...), custom_call_target="tpu_custom_call" | custom-call | flops 1000000 | bytes 100000 | tf_op jit(solution)/shard_map/pallas_call | solution.py:30
  6.2 2.1 %collective-permute-start.3 = (f32[32,640]{1,0:T(8,128)S(1)}, f32[32,640]{1,0:T(8,128)S(1)}, u32[]{:S(2)}, u32[]{:S(2)}) collective-permute-start(f32[32,640]{1,0:T(8,128)S(1)} %get-tuple-element.45.refs_0_), channel_id=1, source_target_pairs={{0,16},{1,17},{2,18},{3,19},{4,20},{5,21},{6,22},{7,23},{8,24},{9,... | collective-permute-start | bytes 245768 | tf_op jit(solution)/shard_map/ppermute | solution.py:418
  8.3 0.1 collective-permute-start.2
  8.3 5.9 %collective-permute-start.4 = (f32[32,384]{1,0:T(8,128)S(1)}, f32[32,384]{1,0:T(8,128)S(1)}, u32[]{:S(2)}, u32[]{:S(2)}) collective-permute-start(f32[32,384]{1,0:T(8,128)S(1)} %get-tuple-element.46), channel_id=1, source_target_pairs={{0,17},{1,16},{2,19},{3,18},{4,21},{5,20},{6,23},{7,22},{8,25},{9,... | collective-permute-start | bytes 147464 | tf_op jit(solution)/shard_map/ppermute | solution.py:418
  14.2 0.0 collective-permute-done.5.far_b
  14.2 0.0 collective-permute-done.2.edge_b
  14.2 2.3 %collective-permute-done.4.edge_a = f32[32,384]{1,0:T(8,128)S(1)} collective-permute-done((f32[32,384]{1,0:T(8,128)S(1)}, f32[32,384]{1,0:T(8,128)S(1)}, u32[]{:S(2)}, u32[]{:S(2)}) %collective-permute-start.4) | collective-permute-done | bytes 49184 | tf_op jit(solution)/shard_map/ppermute | solution.py:418
  16.5 0.0 collective-permute-done.3.main
  16.5 3.9 %collective-permute-start.6 = (f32[32,896]{1,0:T(8,128)S(1)}, f32[32,896]{1,0:T(8,128)S(1)}, u32[]{:S(2)}, u32[]{:S(2)}) collective-permute-start(f32[32,896]{1,0:T(8,128)S(1)} %get-tuple-element.52.refs_2_), channel_id=1, source_target_pairs={{0,16},{1,17},{2,18},{3,19},{4,20},{5,21},{6,22},{7,23},{8,24},{9,... | collective-permute-start | bytes 344072 | tf_op jit(solution)/shard_map/ppermute | solution.py:418
  20.4 0.2 shard_map.65
  20.6 3.0 %collective-permute-done.6.ext = f32[32,896]{1,0:T(8,128)S(1)} collective-permute-done((f32[32,896]{1,0:T(8,128)S(1)}, f32[32,896]{1,0:T(8,128)S(1)}, u32[]{:S(2)}, u32[]{:S(2)}) %collective-permute-start.6) | collective-permute-done | bytes 114720 | tf_op jit(solution)/shard_map/ppermute | solution.py:418
  23.6 0.8 %shard_map.66 = (f32[32,512]{1,0:T(8,128)S(1)}, f32[32,128]{1,0:T(8,128)S(1)}) custom-call(f32[32,128]{1,0:T(8,128)S(1)} %get-tuple-element.51.old, f32[32,896]{1,0:T(8,128)S(1)} %collective-permute-done.6.ext, bf16[512,256]{1,0:T(8,128)(2,1)S(1)} %get-tuple-element.38.a_hi, bf16[512,256]{1,0:T(8,128)(2,1)S(1)} %get-tuple-element.39.a_lo, ...), custom_call_target="tpu_custom_call" | custom-call | flops 1000000 | bytes 100000 | tf_op jit(solution)/shard_map/pallas_call | solution.py:30
  24.4 13.7 %all_to_all.5.grams = f32[16,8,128]{2,1,0:T(8,128)S(1)} all-to-all(f32[16,8,128]{2,1,0:T(8,128)S(1)} %broadcast_in_dim.16), channel_id=1, replica_groups=mesh['tm'=2,'space'=16] {'space'}, dimensions={0} | all-to-all | bytes 131072 | tf_op jit(solution)/shard_map/all_to_all | solution.py:501
  38.0 2.1 %shard_map.67 = (f32[32,512]{1,0:T(8,128)}, f32[32,512]{1,0:T(8,128)}) custom-call(f32[16,8,128]{2,1,0:T(8,128)S(1)} %all_to_all.5.grams, f32[32,128]{1,0:T(8,128)S(1)} %get-tuple-element.57.meta, f32[32,640]{1,0:T(8,128)S(1)} %get-tuple-element.45.refs_0_, f32[32,512]{1,0:T(8,128)S(1)} %get-tuple-element.58.refs_1_, ...), custom_call_target="tpu_custom_call" | custom-call | flops 1000000 | bytes 100000 | tf_op jit(solution)/shard_map/pallas_call | solution.py:30
  (8 shorter events, 0.0 us)
Async XLA Ops:
  0.6 0.8 %copy-start.1 = (f32[32,512]{1,0:T(8,128)S(1)}, f32[32,512]{1,0:T(8,128)}, u32[]{:S(2)}) copy-start(f32[32,512]{1,0:T(8,128)} %main.1) | copy-start | bytes 196612
  0.6 1.2 %copy-start = (f32[2,8,3,4096]{3,1,2,0:T(8,128)S(1)}, f32[2,8,3,4096]{3,1,2,0:T(8,128)}, u32[]{:S(2)}) copy-start(f32[2,8,3,4096]{3,1,2,0:T(8,128)} %param.5) | copy-start | bytes 2359300
  0.7 1.1 %copy-start.3 = (s32[2,8,3]{1,0,2:T(2,128)S(1)}, s32[2,8,3]{1,0,2:T(2,128)}, u32[]{:S(2)}) copy-start(s32[2,8,3]{1,0,2:T(2,128)} %param.6) | copy-start | bytes 580
  1.8 2.1 %copy-start.2 = (f32[2,4,8,8]{3,2,1,0:T(8,128)S(1)}, f32[2,4,8,8]{3,2,1,0:T(8,128)}, u32[]{:S(2)}) copy-start(f32[2,4,8,8]{3,2,1,0:T(8,128)} %mixing) | copy-start | bytes 6148
  2.1 3.1 %collective-permute-start.1 = (f32[864,128]{1,0:T(8,128)S(1)}, f32[864,128]{1,0:T(8,128)S(1)}, u32[]{:S(2)}, u32[]{:S(2)}) collective-permute-start(f32[864,128]{1,0:T(8,128)S(1)} %get-tuple-element.33), channel_id=1, source_target_pairs={{0,1},{1,0},{2,3},{3,2},{4,5},{5,4},{6,7},{7,6},{8,9},{9,8},{10,11... | collective-permute-start | bytes 1327112 | tf_op jit(solution)/shard_map/ppermute | solution.py:412
  2.6 11.6 %collective-permute-start.5 = (f32[864,128]{1,0:T(8,128)S(1)}, f32[864,128]{1,0:T(8,128)S(1)}, u32[]{:S(2)}, u32[]{:S(2)}) collective-permute-start(f32[864,128]{1,0:T(8,128)S(1)} %get-tuple-element.34), channel_id=1, source_target_pairs={{16,16},{17,18},{18,17},{19,20},{20,19},{21,22},{22,21},{23,24},{2... | collective-permute-start | bytes 1327112 | tf_op jit(solution)/shard_map/ppermute | solution.py:412
  3.3 1.9 %collective-permute-start = (f32[224,128]{1,0:T(8,128)S(1)}, f32[224,128]{1,0:T(8,128)S(1)}, u32[]{:S(2)}, u32[]{:S(2)}) collective-permute-start(f32[224,128]{1,0:T(8,128)S(1)} %get-tuple-element.32), channel_id=1, source_target_pairs={{0,0},{1,2},{2,1},{3,4},{4,3},{5,6},{6,5},{7,8},{8,7},{9,10},{10,9... | collective-permute-start | bytes 344072 | tf_op jit(solution)/shard_map/ppermute | solution.py:412
  6.2 10.3 %collective-permute-start.3 = (f32[32,640]{1,0:T(8,128)S(1)}, f32[32,640]{1,0:T(8,128)S(1)}, u32[]{:S(2)}, u32[]{:S(2)}) collective-permute-start(f32[32,640]{1,0:T(8,128)S(1)} %get-tuple-element.45.refs_0_), channel_id=1, source_target_pairs={{0,16},{1,17},{2,18},{3,19},{4,20},{5,21},{6,22},{7,23},{8,24},{9,... | collective-permute-start | bytes 245768 | tf_op jit(solution)/shard_map/ppermute | solution.py:418
  8.3 5.9 %collective-permute-start.2 = (f32[32,384]{1,0:T(8,128)S(1)}, f32[32,384]{1,0:T(8,128)S(1)}, u32[]{:S(2)}, u32[]{:S(2)}) collective-permute-start(f32[32,384]{1,0:T(8,128)S(1)} %get-tuple-element.44), channel_id=1, source_target_pairs={{0,16},{1,18},{2,17},{3,20},{4,19},{5,22},{6,21},{7,24},{8,23},{9,... | collective-permute-start | bytes 147464 | tf_op jit(solution)/shard_map/ppermute | solution.py:418
  8.3 8.2 %collective-permute-start.4 = (f32[32,384]{1,0:T(8,128)S(1)}, f32[32,384]{1,0:T(8,128)S(1)}, u32[]{:S(2)}, u32[]{:S(2)}) collective-permute-start(f32[32,384]{1,0:T(8,128)S(1)} %get-tuple-element.46), channel_id=1, source_target_pairs={{0,17},{1,16},{2,19},{3,18},{4,21},{5,20},{6,23},{7,22},{8,25},{9,... | collective-permute-start | bytes 147464 | tf_op jit(solution)/shard_map/ppermute | solution.py:418
  16.5 7.1 %collective-permute-start.6 = (f32[32,896]{1,0:T(8,128)S(1)}, f32[32,896]{1,0:T(8,128)S(1)}, u32[]{:S(2)}, u32[]{:S(2)}) collective-permute-start(f32[32,896]{1,0:T(8,128)S(1)} %get-tuple-element.52.refs_2_), channel_id=1, source_target_pairs={{0,16},{1,17},{2,18},{3,19},{4,20},{5,21},{6,22},{7,23},{8,24},{9,... | collective-permute-start | bytes 344072 | tf_op jit(solution)/shard_map/ppermute | solution.py:418

commit v3 on v2

--- a/solution.py
+++ b/solution.py
@@ -13,8 +13,10 @@
 ROWS = COLS * PANELS
 RUN = 2
 GROUP = 4
-RIM_A = 5
-RIM_B = 4
+RIM_A, RIM_B = 5, 4
+FAR_A, FAR_B = 3, 2
+PUSH = 10**9
+ASIDE_1, ASIDE_2 = 3 * 10**8, 5 * 10**8
 DOWN = 2.0**-16
 BF = jnp.bfloat16
 F32 = jnp.float32
@@ -95,17 +97,17 @@
 
     @pl.when(turns)
     def _():
-        even = parity() == 0
+        even, odd = parity() == 0, parity() == 1
         keep = inside()
-        for t, rows, start in ((0, RIM_A, 0), (1, RIM_B, 96 * RIM_A)):
+        for t, deep, start_a, wide, start_b in ((0, RIM_A, 0, FAR_A, 0), (1, RIM_B, 96 * RIM_A, FAR_B, 96 * FAR_A)):
             column = [jnp.broadcast_to(presence(mask, t, j, nb), (nb, 128)) for j in range(3)]
             for r in range(32):
                 for j in range(3):
                     y = blocks[t, j, :, r * 128 : (r + 1) * 128] * column[j]
-                    to = pl.ds(start + j * 32 + r, rows, stride=96)
-                    head, tail = y[:rows], y[nb - rows :]
-                    to_a[to, :] = jnp.where(even, tail, head)
-                    far_b[0][to, :] = jnp.where(even, head, tail) * keep
+                    for dst, rows, start, tail_if in ((to_a, deep, start_a, even), (far_b[0], wide, start_b, odd)):
+                        to = pl.ds(start + j * 32 + r, rows, stride=96)
+                        dst[to, :] = jnp.where(tail_if, y[nb - rows :], y[:rows])
+        far_b[0][...] = far_b[0][...] * keep
 
 
 def banded(y, p):
@@ -183,29 +185,41 @@
 
 
 def rim_kernel(turning, far_b, far_a, a_hi, a_lo, b_hi, b_lo, wide_a, wide_b):
+    none = jnp.zeros((32, 128), F32)
+
     @pl.when(lax.axis_index("tm") == turning)
     def _():
-        for dst, depth, start, odd in ((wide_a, RIM_A, 0, 1), (wide_b, RIM_B, 96 * RIM_A, 0)):
-            for i in range(depth):
+        for dst, deep, start_a, wide, start_b, odd in (
+            (wide_a, RIM_A, 0, FAR_A, 0, 1),
+            (wide_b, RIM_B, 96 * RIM_A, FAR_B, 96 * FAR_A, 0),
+        ):
+            for i in range(deep):
                 for left in (True, False):
-                    y = [taken(far_a, far_b, left, start + i * 96 + j * 32) for j in range(3)]
-                    place = i - depth if left else i
-                    rim_row(dst, i if left else depth + i, place % 2 == odd, y)
+                    k = i - (deep - wide) if left else i
+                    y = []
+                    for j in range(3):
+                        n, m = start_a + i * 96 + j * 32, start_b + k * 96 + j * 32
+                        from_b = far_b[m : m + 32, :] if 0 <= k < wide else none
+                        y.append(jnp.where((parity() == 0) == left, from_b, far_a[n : n + 32, :]))
+                    place = i - deep if left else i
+                    rim_row(dst, i if left else deep + i, place % 2 == odd, y)
         split_halves(wide_a, 0, a_hi, a_lo)
         split_halves(wide_b, 0, b_hi, b_lo)
 
 
-def pull_rim_kernel(near_a, near_b, a_hi, a_lo, b_hi, b_lo, wide_a, wide_b):
-    edge_rows(near_a, near_b, wide_a)
-    none = jnp.zeros((32, 128), F32)
-    left = [taken(near_a, near_b, True, (4 + i) * 32) for i in range(3)]
-    right = [taken(near_a, near_b, False, (4 + i) * 32) for i in range(3)]
-    rim_row(wide_b, 0, True, [none, none, left[0]])
-    rim_row(wide_b, 1, False, [none, left[1], left[2]])
-    rim_row(wide_b, 2, True, [right[0], right[1], none])
-    rim_row(wide_b, 3, False, [right[2], none, none])
-    split_halves(wide_a, 0, a_hi, a_lo)
-    split_halves(wide_b, 0, b_hi, b_lo)
+def pull_rim_kernel(turning, near_a, near_b, a_hi, a_lo, b_hi, b_lo, wide_a, wide_b):
+    @pl.when(lax.axis_index("tm") != turning)
+    def _():
+        edge_rows(near_a, near_b, wide_a)
+        none = jnp.zeros((32, 128), F32)
+        left = [taken(near_a, near_b, True, (4 + i) * 32) for i in range(3)]
+        right = [taken(near_a, near_b, False, (4 + i) * 32) for i in range(3)]
+        rim_row(wide_b, 0, True, [none, none, left[0]])
+        rim_row(wide_b, 1, False, [none, left[1], left[2]])
+        rim_row(wide_b, 2, True, [right[0], right[1], none])
+        rim_row(wide_b, 3, False, [right[2], none, none])
+        split_halves(wide_a, 0, a_hi, a_lo)
+        split_halves(wide_b, 0, b_hi, b_lo)
 
 
 def pair_tile(own, rim, depth, nb, b):
@@ -251,13 +265,14 @@
 
 
 def gram(u):
-    u1, u2, u3 = split3(u)
-    stack = jnp.concatenate([u3, u2, u1], axis=0)
-    total = None
-    for part in (u3, u2, u1):
-        g = lax.dot_general(stack, jnp.concatenate([part] * 4, axis=0), NT, preferred_element_type=F32)
-        g = (g[:ROWS] + g[ROWS : 2 * ROWS]) + g[2 * ROWS :]
-        total = g if total is None else total + g
+    high, low = split2(u)
+    o = lax.dot_general(
+        jnp.concatenate([low, high], axis=0),
+        jnp.concatenate([low] * 4 + [high] * 4, axis=0),
+        NT,
+        preferred_element_type=F32,
+    )
+    total = (o[:ROWS, :128] + o[:ROWS, 128:] + o[ROWS:, :128]) + o[ROWS:, 128:]
     panel = lax.rem(iota((COLS, 128), 1), ROWS) // COLS
     out = jnp.zeros((COLS, 128), F32)
     for p in range(PANELS):
@@ -265,11 +280,9 @@
     return out
 
 
-def noted(meta, slot, g, e):
+def noted(g, e, slot, new_g, new_e):
     mine = (iota((COLS, 128), 1) // ROWS) == slot
-    return jnp.concatenate(
-        [jnp.where(mine, g, meta[:COLS]), jnp.where(mine, e, meta[COLS : 2 * COLS]), meta[2 * COLS :]], axis=0
-    )
+    return jnp.where(mine, new_g, g), jnp.where(mine, new_e, e)
 
 
 def by_side(e_a, e_b):
@@ -277,39 +290,43 @@
     return jnp.where(even, e_b, e_a), jnp.where(even, e_a, e_b)
 
 
-def push_kernel(nb, owner, slot, reach, old, edge_b, main, edge_a, near_b, near_a, a_hi, a_lo, b_hi, b_lo, expand,
-                out, out_a, out_b, meta, wide):
+def aside_kernel(edge, *refs):
+    out = refs[-1]
+    width, wanted = edge.shape[1], out.shape[1]
+    if width == wanted:
+        out[...] = edge[...]
+        return
+    none = jnp.zeros((ROWS, wanted - width), F32)
+    left = jnp.concatenate([none, edge[...]], axis=1)
+    right = jnp.concatenate([edge[...], none], axis=1)
+    out[...] = jnp.where(parity() == 0, left, right)
+
+
+def push_kernel(nb, owner, edge_b, main, edge_a, near_b, near_a, a_hi, a_lo, b_hi, b_lo, out, out_b, out_a, wide):
     own = nb * BLOCK
-
-    @pl.when(lax.axis_index("tm") != owner)
-    def _():
-        meta[...] = old[...]
 
     @pl.when(lax.axis_index("tm") == owner)
     def _():
         edge_rows(near_a, near_b, wide)
         rim_hi, rim_lo = split2(jnp.concatenate([wide[0], wide[1]], axis=1))
-        w_edge = edge_a.shape[1]
         left, right = by_side(edge_a[...], edge_b[...])
-        v = jnp.concatenate([left[:, w_edge - 128 :], main[:, :own], right[:, :128]], axis=1)
+        v = jnp.concatenate([left, main[:, :own], right], axis=1)
         w = push(v, tiles_of((a_hi, a_lo, rim_hi, rim_lo), 1, nb, -1, nb))
         u = push(w, tiles_of((b_hi, b_lo, None, None), 0, nb, 0, nb))
-        known = old[...] if main.shape[1] == own else main[:, own:]
-        now = noted(known, slot, gram(u), expand[:COLS])
-        out[:, :own] = u
-        out[:, own:] = now
-        meta[...] = now
-        low, high = u[:, :reach], u[:, own - reach :]
-        out_b[...], out_a[...] = by_side(high, low)
-
-
-def turn_kernel(nb, owner, slot, old, edge_b, main, edge_a, a_hi, a_lo, b_hi, b_lo, ra_hi, ra_lo, rb_hi, rb_lo,
-                expand, first_out, out, meta):
+        out[...] = u
+        wide_b, wide_a = out_b.shape[1], out_a.shape[1]
+        out_b[...] = by_side(u[:, :wide_b], u[:, own - wide_b :])[1]
+        out_a[...] = by_side(u[:, own - wide_a :], u[:, :wide_a])[1]
+
+
+def turn_kernel(nb, owner, slot, edge_b, main, edge_a, a_hi, a_lo, b_hi, b_lo, ra_hi, ra_lo, rb_hi, rb_lo,
+                old, expand, first, out, out_b):
     own = nb * BLOCK
+    end = own + 128
 
     @pl.when(lax.axis_index("tm") != owner)
     def _():
-        meta[...] = old[...]
+        out[: 2 * COLS, end:] = old[...]
 
     @pl.when(lax.axis_index("tm") == owner)
     def _():
@@ -319,49 +336,57 @@
         tiles_b = tiles_of((b_hi, b_lo, rb_hi, rb_lo), RIM_B, nb, -RIM_B, nb + RIM_B)
         u = push(push(v, tiles_a), tiles_b)
         u_own = u[:, 256 : 256 + own]
-        first_out[...] = u_own
+        first[...] = u_own
         back = pull(pull(u * DOWN, tiles_b), tiles_a[1:-1])
-        now = noted(main[:, own:], slot, gram(u_own), expand[:COLS])
-        now = noted(now, slot + 1, gram(back[:, 128 : 128 + own]), expand[COLS:] * (1.0 / DOWN))
-        out[:, : own + 256] = back
-        out[:, own + 256 :] = now
-        meta[...] = now
-
-
-def pull_kernel(nb, owner, slot, old, ext, a_hi, a_lo, b_hi, b_lo, ra_hi, ra_lo, rb_hi, rb_lo, expand, out, meta):
+        back_own = back[:, 128 : 128 + own]
+        out[:, :own] = back_own
+        out[:, own:end] = by_side(back[:, end:], back[:, :128])[1]
+        out_b[...] = by_side(back[:, 128:256], back[:, own:end])[1]
+        g, e = noted(old[:COLS], old[COLS:], slot, gram(u_own), expand[:COLS])
+        g, e = noted(g, e, slot + 1, gram(back_own), expand[COLS:] * (1.0 / DOWN))
+        out[: 2 * COLS, end:] = jnp.concatenate([g, e], axis=0)
+
+
+def pull_kernel(nb, owner, edge_b, main, edge_a, a_hi, a_lo, b_hi, b_lo, ra_hi, ra_lo, rb_hi, rb_lo, out):
     own = nb * BLOCK
 
+    @pl.when(lax.axis_index("tm") == owner)
+    def _():
+        left, right = by_side(edge_a[...], edge_b[...])
+        v = jnp.concatenate([left, main[:, :own], right], axis=1)
+        y = pull(v, tiles_of((b_hi, b_lo, rb_hi, rb_lo), 2, nb, -2, nb + 2))
+        out[...] = pull(y, tiles_of((a_hi, a_lo, ra_hi, ra_lo), 1, nb, -1, nb + 1))
+
+
+def note_kernel(nb, owner, slot, forward, u, old, expand, out):
     @pl.when(lax.axis_index("tm") != owner)
     def _():
-        meta[...] = old[...]
+        out[...] = old[...]
 
     @pl.when(lax.axis_index("tm") == owner)
     def _():
-        y = pull(ext[:, : own + 256], tiles_of((b_hi, b_lo, rb_hi, rb_lo), 2, nb, -2, nb + 2))
-        u = pull(y, tiles_of((a_hi, a_lo, ra_hi, ra_lo), 1, nb, -1, nb + 1))
-        out[...] = u
-        meta[...] = noted(ext[:, own + 256 :], slot, gram(u), expand[COLS:])
+        e = expand[:COLS] if forward else expand[COLS:]
+        out[:COLS], out[COLS:] = noted(old[:COLS], old[COLS:], slot, gram(u[:, : nb * BLOCK]), e)
 
 
 def exact(x, y):
-    width = y.shape[1]
-    xs, ys = split3(x), split3(y)
+    m = x.shape[0]
     o = lax.dot_general(
-        jnp.concatenate(xs, axis=0), jnp.concatenate(ys, axis=1), NN, preferred_element_type=F32
+        jnp.concatenate(split3(x), axis=0), jnp.concatenate(split3(y), axis=1), NN, preferred_element_type=F32
     )
-    piece = [[o[i * ROWS : (i + 1) * ROWS, j * width : (j + 1) * width] for j in range(3)] for i in range(3)]
+    piece = [[o[i * m : (i + 1) * m, j * 128 : (j + 1) * 128] for j in range(3)] for i in range(3)]
     small = (piece[0][2] + piece[2][0]) + piece[1][1]
     return (small + (piece[0][1] + piece[1][0])) + piece[0][0]
 
 
-def scale_kernel(stages, boxes, offsets, grams, meta, *refs):
+def scale_kernel(stages, boxes, grams, meta, *refs):
     panels, (out_f, out_a) = refs[: len(stages)], refs[len(stages) :]
     own = out_f.shape[1]
     parts = [grams[i] for i in range(grams.shape[0])]
     while len(parts) > 1:
         parts = [a + b for a, b in zip(parts[::2], parts[1::2])] + parts[len(parts) // 2 * 2 :]
     total = parts[0] * (1.0 / boxes)
-    growth = meta[COLS : 2 * COLS, :]
+    growth = meta[COLS:, :]
     row, lane = iota((ROWS, 128), 0), iota((ROWS, 128), 1)
     same = (row // COLS) == (lax.rem(lane, ROWS) // COLS)
     me = lax.axis_index("tm")
@@ -374,13 +399,18 @@
             spread = jnp.where(group == k, turns[k], spread)
         return jnp.where(same, jnp.concatenate([spread] * PANELS, axis=0), 0.0)
 
-    back, select = None, {True: None, False: None}
+    count = len(stages)
+    h = full(growth, 0)
+    stack = jnp.concatenate([h, exact(jnp.concatenate([full(total, n)[:, :ROWS] for n in range(count)], axis=0), h)])
+    select = {True: None, False: None}
     for n, (owner, forward) in enumerate(stages):
-        e = full(growth, n)
-        h = e if back is None else exact(back[:, :ROWS], e)
-        square = jnp.sum(h * exact(full(total, n)[:, :ROWS], h), axis=0, keepdims=True)
-        back = h * lax.rsqrt(jnp.maximum(square, 0.0) + 1e-06)
-        u = panels[n][:, offsets[n] : offsets[n] + own]
+        if n:
+            stack = exact(stack[:, :ROWS], full(growth, n))
+        square = jnp.sum(stack[:ROWS] * stack[ROWS : 2 * ROWS], axis=0, keepdims=True)
+        scale = lax.rsqrt(jnp.maximum(square, 0.0) + 1e-06)
+        later = [stack[2 * ROWS :]] if n + 1 < count else []
+        stack = jnp.concatenate([stack[:ROWS]] + later, axis=0) * scale
+        back, u = stack[:ROWS], panels[n][:, :own]
         old = select[forward]
         select[forward] = (back, u) if old is None else (
             jnp.where(me == owner, back, old[0]), jnp.where(me == owner, u, old[1])
@@ -389,8 +419,10 @@
         if select[forward] is None:
             out[...] = jnp.zeros_like(out)
         else:
-            b, u = select[forward]
-            out[...] = exact(b[:, :ROWS].T, u)
+            back, u = select[forward]
+            left = jnp.concatenate(split2(back[:, :ROWS].T), axis=0)
+            o = lax.dot_general(left, jnp.concatenate(split2(u), axis=1), NN, preferred_element_type=F32)
+            out[...] = (o[ROWS:, own:] + o[ROWS:, :own] + o[:ROWS, own:]) + o[:ROWS, :own]
 
 
 def shards(panels_in, blocks, block_mask, mixing):
@@ -411,19 +443,22 @@
         route = [(t * count + s, t * count + to(s)) for t in (only or range(owners)) for s in range(count)]
         return lax.ppermute(x, ("tm", "space"), route)
 
-    def hop(x, shift, to):
-        route = [
-            (t * count + s, (t + shift) % owners * count + to(s)) for t in range(owners) for s in range(count)
-        ]
-        return lax.ppermute(x, ("tm", "space"), route)
+    def hop(x, t, o, to):
+        pairs = [(t, o), (o, t)] if t != o else [(t, t)]
+        return lax.ppermute(x, ("tm", "space"), [(i * count + s, k * count + to(s)) for i, k in pairs for s in range(count)])
+
+    def edges_of(x, wide_b, wide_a):
+        return (
+            jnp.where(even, x[:, :wide_b], x[:, own - wide_b : own]),
+            jnp.where(even, x[:, own - wide_a : own], x[:, :wide_a]),
+        )
 
     rows, mask = blocks.transpose(0, 2, 1, 3), block_mask.transpose(2, 0, 1)
     vm = lambda *s: pltpu.VMEM(s, F32)
     turn = owners % GROUP != 0
     turning = owners - 1 if turn else owners
     begin = call(first_kernel, [f32(8, 128)], (), flops=10**9)
-    far_rows = 96 * (RIM_A + RIM_B)
-    sizes = [224, far_rows, far_rows] if turn else [224, 224]
+    sizes = [224, 96 * (RIM_A + RIM_B), 96 * (FAR_A + FAR_B)] if turn else [224, 224]
     edges = call(
         functools.partial(edge_kernel, nb, turning),
         [f32(n, 128) for n in sizes],
@@ -445,64 +480,58 @@
         outs, scratch = [bf(deep_a, 256)] * 2 + [bf(deep_b, 256)] * 2, [vm(2, deep_a, 128), vm(2, deep_b, 128)]
         return call(kernel, outs, args, scratch)
 
-    pull_rims = rim_call(pull_rim_kernel, 1, 2, (near_a, near_b))
+    pull_rims = rim_call(functools.partial(pull_rim_kernel, turning), 1, 2, (near_a, near_b))
     if turn:
         turn_rims = rim_call(functools.partial(rim_kernel, turning), RIM_A, RIM_B, (far_b, near_a))
 
-    meta = jnp.zeros((ROWS, 128), F32)
+    meta = jnp.zeros((2 * COLS, 128), F32)
     main, edge_a, edge_b = panels_in, near_a[96:128], near_b[96:128]
-    ext = None
     stages = 2 * owners
     owner_of = [k if k < owners else stages - 1 - k for k in range(stages)]
-    result = None
-    kept, offsets = [], []
-    k = 0
+    kept, result, k = [], None, 0
     while k < stages:
-        turning = k == owners - 1 and (k + 1) % GROUP != 0
         owner, slot = owner_of[k], k % GROUP
-        if turning:
-            first, ext, meta = call(
+        turns_here, turns_next = turn and k == owners - 1, turn and k + 1 == owners - 1
+        if turns_here:
+            first, main, send_b = call(
                 functools.partial(turn_kernel, nb, owner, slot),
-                [f32(ROWS, own), f32(ROWS, own + 384), f32(ROWS, 128)],
-                (meta, edge_b, main, edge_a, *own_tiles, *turn_rims, expand),
+                [f32(ROWS, own), f32(ROWS, own + 256), f32(ROWS, 128)],
+                (edge_b, main, edge_a, *own_tiles, *turn_rims, meta, expand),
             )
-            kept += [first, ext]
-            offsets += [0, 128]
-            current = ext[:, 128 : 128 + own]
+            kept += [first, main]
+            meta = main[: 2 * COLS, own + 128 :]
             k += 2
-        elif k < owners:
-            reach = 384 if k + 1 == owners - 1 and (k + 2) % GROUP != 0 else 128
-            main, edge_a, edge_b, meta = call(
-                functools.partial(push_kernel, nb, owner, slot, reach),
-                [f32(ROWS, own + 128), f32(ROWS, reach), f32(ROWS, reach), f32(ROWS, 128)],
-                (meta, edge_b, main, edge_a, near_b, near_a, *own_tiles, expand),
-                [pltpu.VMEM((2, 2 * BLOCK, 128), F32)],
+        else:
+            if k < owners:
+                main, send_b, send_a = call(
+                    functools.partial(push_kernel, nb, owner),
+                    [f32(ROWS, own)] + [f32(ROWS, w) for w in ((256, 384) if turns_next else (128, 128))],
+                    (edge_b, main, edge_a, near_b, near_a, *own_tiles),
+                    [vm(2, 2 * BLOCK, 128)],
+                    flops=PUSH,
+                )
+            else:
+                (main,) = call(
+                    functools.partial(pull_kernel, nb, owner),
+                    [f32(ROWS, own)],
+                    (edge_b, main, edge_a, *own_tiles, *pull_rims),
+                )
+                send_b, send_a = edges_of(main, 128, 128)
+            (meta,) = call(
+                functools.partial(note_kernel, nb, owner, slot, k < owners),
+                [f32(2 * COLS, 128)],
+                (main, meta, expand),
             )
             kept.append(main)
-            offsets.append(0)
-            current = main[:, :own]
             k += 1
-        else:
-            current, meta = call(
-                functools.partial(pull_kernel, nb, owner, slot),
-                [f32(ROWS, own), f32(ROWS, 128)],
-                (meta, ext, *own_tiles, *pull_rims, expand),
-            )
-            ext = None
-            kept.append(current)
-            offsets.append(0)
-            k += 1
-
-        fresh = False
+        share = not (turns_next and slot == 0)
+
         if k % GROUP == 0 or k == stages:
-            start = k - len(kept)
-            todo = [(owner_of[i], i < owners) for i in range(start, k)]
+            todo = [(owner_of[i], i < owners) for i in range(k - len(kept), k)]
             every = jnp.broadcast_to(meta[None, :COLS], (count, COLS, 128))
             grams = lax.all_to_all(every, "space", 0, 0)
             pair = call(
-                functools.partial(scale_kernel, todo, count * own, offsets),
-                [f32(ROWS, own)] * 2,
-                (grams, meta, *kept),
+                functools.partial(scale_kernel, todo, count * own), [f32(ROWS, own)] * 2, (grams, meta, *kept)
             )
             if result is None:
                 result = pair
@@ -512,27 +541,29 @@
                     for way in (True, False)
                 ]
                 result = [jnp.where(c, new, old) for c, new, old in zip(live, pair, result)]
-            current = pair[0 if k - 1 < owners else 1]
-            meta, ext, fresh = jnp.zeros((ROWS, 128), F32), None, True
-            kept, offsets = [], []
+            main = pair[0 if k - 1 < owners else 1]
+            send_b, send_a = edges_of(main, *((256, 384) if turn and k == owners - 1 else (128, 128)))
+            meta, kept, share = jnp.zeros((2 * COLS, 128), F32), [], False
         if k == stages:
             break
 
-        shift = owner_of[k] - owner_of[k - 1]
-        if ext is not None:
-            ext = hop(ext, shift, lambda s: s)
-            continue
-        turns_next = k == owners - 1 and (k + 1) % GROUP != 0
-        reach = 384 if turns_next else 128
-        if fresh or k > owners or main.shape[1] == own:
-            main = jnp.concatenate([current, meta], axis=1)
-            low, high = current[:, :reach], current[:, own - reach :]
-            edge_a, edge_b = jnp.where(even, high, low), jnp.where(even, low, high)
-        main = hop(main, shift, lambda s: s)
-        edge_a, edge_b = hop(edge_a, shift, partner_a), hop(edge_b, shift, partner_b)
-        if k >= owners:
-            left, right = jnp.where(even, edge_b, edge_a), jnp.where(even, edge_a, edge_b)
-            ext = jnp.concatenate([left, main[:, :own], right, main[:, own:]], axis=1)
+        before, after = owner_of[k - 1], owner_of[k]
+        if after != before:
+            main = hop(main, before, after, lambda s: s)
+        into_turn = turn and k == owners - 1
+        (edge_b,) = call(
+            aside_kernel,
+            [f32(ROWS, 384 if into_turn else 128)],
+            (hop(send_b, before, after, partner_b),) + ((turn_rims[0],) if into_turn else ()),
+            flops=ASIDE_1 if into_turn else ASIDE_2,
+        )
+        if main.shape[1] > own:
+            edge_a = main[:, own : own + 128]
+            meta = meta + main[: 2 * COLS, own + 128 :]
+        else:
+            edge_a = hop(send_a, before, after, partner_a)
+            if share and after != before:
+                meta = meta + hop(meta, before, after, lambda s: s)
     return result[0][None], result[1][None]
 
 

time: 40.3 us -> 39.4 us (0.978)
  starting transfers between devices: 13.8 us -> 13.2 us
  Pallas kernels: 5.46 us -> 4.9 us
    ppermute x4 -> x5, starting transfers between devices: 11.9 us -> 11.3 us  [hop(): lax.ppermute(x, ('tm', 'space'), [(i * count + s, k * count + to(s)) for...]
    pallas_call x9 -> x13, Pallas kernels: 5.46 us -> 4.9 us  [call(): pl.pallas_call(kernel, out_shape=shapes, in_specs=[pl.BlockSpec(memory_sp...]
    ppermute x4 -> x5, waiting for transfers between devices: 5.25 us -> 5.32 us  [hop(): lax.ppermute(x, ('tm', 'space'), [(i * count + s, k * count + to(s)) for...]
  transfers between devices with their start and end apart: 7 -> 8, of which waited for: 2 -> 2; matrix products, arithmetic and copies ran while one was open for 0% -> 0% of each run, Pallas kernels for 6% -> 6%
where the time goes in v3:
time: 39.4 us; the launch traced here: 39.2 us
  blocking collectives  13.8 us (35%)
  starting transfers between devices  13.2 us (34%)
  waiting for transfers between devices  5.33 us (14%)
  Pallas kernels  4.9 us (12%)
  local copies, waits for them, and re-layouts  1.13 us (3%)
  between operations  0.82 us (2%)
    all_to_all x1, blocking collectives, shards(): grams = lax.all_to_all(every, 'space', 0, 0)  13.8 us
    ppermute x5, starting transfers between devices, hop(): lax.ppermute(x, ('tm', 'space'), [(i * count + s, k * count + to(s)) for...  11.3 us
    ppermute x5, waiting for transfers between devices, hop(): lax.ppermute(x, ('tm', 'space'), [(i * count + s, k * count + to(s)) for...  5.32 us
    pallas_call x13, Pallas kernels, call(): pl.pallas_call(kernel, out_shape=shapes, in_specs=[pl.BlockSpec(memory_sp...  4.9 us
    ppermute x3, starting transfers between devices, beside(): return lax.ppermute(x, ('tm', 'space'), route)  1.84 us
    unnamed x8, local copies, waits for them, and re-layouts  1.11 us
  transfers between devices with their start and end apart: 8, of which 2 were waited for; matrix products, arithmetic and copies ran while one was open for 0% of the time, Pallas kernels for 6%

profile of v3, /device:TPU:0, one launch (start us, length us, event | category | flops | bytes accessed | tf_op | source)
XLA Modules:
  0.0 39.2 jit_solution(7200223315050699941)
XLA Ops:
  0.6 0.0 copy-start
  0.6 0.0 copy-start.1
  0.7 0.0 copy-start.3
  0.7 1.1 %copy-done = f32[2,8,3,4096]{3,1,2,0:T(8,128)S(1)} copy-done((f32[2,8,3,4096]{3,1,2,0:T(8,128)S(1)}, f32[2,8,3,4096]{3,1,2,0:T(8,128)}, u32[]{:S(2)}) %copy-start) | copy-done | bytes 786456
  1.8 0.0 copy-done.1
  1.8 0.0 copy-done.3
  1.8 0.0 copy-start.2
  1.8 0.2 shard_map.60
  2.0 0.5 %collective-permute-start.1 = (f32[864,128]{1,0:T(8,128)S(1)}, f32[864,128]{1,0:T(8,128)S(1)}, u32[]{:S(2)}, u32[]{:S(2)}) collective-permute-start(f32[864,128]{1,0:T(8,128)S(1)} %get-tuple-element.30), channel_id=1, source_target_pairs={{0,1},{1,0},{2,3},{3,2},{4,5},{5,4},{6,7},{7,6},{8,9},{9,8},{10,11... | collective-permute-start | bytes 1327112 | tf_op jit(solution)/shard_map/ppermute | solution.py:444
  2.5 0.7 %collective-permute-start = (f32[224,128]{1,0:T(8,128)S(1)}, f32[224,128]{1,0:T(8,128)S(1)}, u32[]{:S(2)}, u32[]{:S(2)}) collective-permute-start(f32[224,128]{1,0:T(8,128)S(1)} %get-tuple-element.29), channel_id=1, source_target_pairs={{0,0},{1,2},{2,1},{3,4},{4,3},{5,6},{6,5},{7,8},{8,7},{9,10},{10,9... | collective-permute-start | bytes 344072 | tf_op jit(solution)/shard_map/ppermute | solution.py:444
  3.2 0.7 %collective-permute-start.3 = (f32[480,128]{1,0:T(8,128)S(1)}, f32[480,128]{1,0:T(8,128)S(1)}, u32[]{:S(2)}, u32[]{:S(2)}) collective-permute-start(f32[480,128]{1,0:T(8,128)S(1)} %get-tuple-element.31), channel_id=1, source_target_pairs={{16,16},{17,18},{18,17},{19,20},{20,19},{21,22},{22,21},{23,24},{2... | collective-permute-start | bytes 737288 | tf_op jit(solution)/shard_map/ppermute | solution.py:444
  3.9 0.0 copy-done.2
  3.9 1.2 %shard_map.61 = (bf16[512,256]{1,0:T(8,128)(2,1)S(1)}, bf16[512,256]{1,0:T(8,128)(2,1)S(1)}, bf16[512,256]{1,0:T(8,128)(2,1)S(1)}, bf16[512,256]{1,0:T(8,128)(2,1)S(1)}, f32[16,128]{1,0:T(8,128)S(1)}) custom-call(f32[2,3,8,4096]{3,2,1,0:T(8,128)S(1)} %bitcast.5, s32[3,2,8]{2,1,0:T(2,128)S(1)} %bitcast.7, f32[2,4,8,8]{3,2,1,0:T(8,128)S(1)} %copy-done.2), custom_call_target="tpu_custom_call" | custom-call | flops 1000000 | bytes 100000 | tf_op jit(solution)/shard_map/pallas_call | solution.py:32
  5.1 0.0 collective-permute-done.near_b
  5.1 0.0 collective-permute-done.1.near_a.far_a
  5.1 0.6 %shard_map.62 = (f32[32,512]{1,0:T(8,128)S(1)}, f32[32,256]{1,0:T(8,128)S(1)}, f32[32,384]{1,0:T(8,128)S(1)}) custom-call(f32[32,128]{1,0:T(8,128)S(1)} %slice.24.edge_b, f32[32,512]{1,0:T(8,128)S(1)} %copy-done.1, f32[32,128]{1,0:T(8,128)S(1)} %slice.25.edge_a, f32[224,128]{1,0:T(8,128)S(1)} %collective-permute-done.near_b, ...), custom_call_target="tpu_custom_call" | custom-call | flops 1000000000 | bytes 100000 | tf_op jit(solution)/shard_map/pallas_call | solution.py:32
  5.7 2.5 %collective-permute-start.4 = (f32[32,512]{1,0:T(8,128)S(1)}, f32[32,512]{1,0:T(8,128)S(1)}, u32[]{:S(2)}, u32[]{:S(2)}) collective-permute-start(f32[32,512]{1,0:T(8,128)S(1)} %get-tuple-element.41.u.refs_0_), channel_id=1, source_target_pairs={{0,16},{1,17},{2,18},{3,19},{4,20},{5,21},{6,22},{7,23},{8,24},{9,... | collective-permute-start | bytes 196616 | tf_op jit(solution)/shard_map/ppermute | solution.py:448
  8.3 0.1 collective-permute-start.2
  8.4 4.8 %collective-permute-start.5 = (f32[32,384]{1,0:T(8,128)S(1)}, f32[32,384]{1,0:T(8,128)S(1)}, u32[]{:S(2)}, u32[]{:S(2)}) collective-permute-start(f32[32,384]{1,0:T(8,128)S(1)} %get-tuple-element.42), channel_id=1, source_target_pairs={{0,17},{1,16},{2,19},{3,18},{4,21},{5,20},{6,23},{7,22},{8,25},{9,... | collective-permute-start | bytes 147464 | tf_op jit(solution)/shard_map/ppermute | solution.py:448
  13.1 0.2 shard_map.65.old
  13.3 0.0 collective-permute-done.3.far_b
  13.4 0.0 collective-permute-done.2.edge
  13.4 1.8 %collective-permute-done.5.edge_a = f32[32,384]{1,0:T(8,128)S(1)} collective-permute-done((f32[32,384]{1,0:T(8,128)S(1)}, f32[32,384]{1,0:T(8,128)S(1)}, u32[]{:S(2)}, u32[]{:S(2)}) %collective-permute-start.5) | collective-permute-done | bytes 49184 | tf_op jit(solution)/shard_map/ppermute | solution.py:448
  15.2 0.0 collective-permute-done.4.main
  15.3 3.9 %collective-permute-start.7 = (f32[32,768]{1,0:T(8,128)S(1)}, f32[32,768]{1,0:T(8,128)S(1)}, u32[]{:S(2)}, u32[]{:S(2)}) collective-permute-start(f32[32,768]{1,0:T(8,128)S(1)} %get-tuple-element.48.refs_2_), channel_id=1, source_target_pairs={{16,0},{17,1},{18,2},{19,3},{20,4},{21,5},{22,6},{23,7},{24,8},{25... | collective-permute-start | bytes 294920 | tf_op jit(solution)/shard_map/ppermute | solution.py:448
  19.1 0.1 collective-permute-start.6
  19.2 0.2 shard_map.68
  19.4 3.5 %collective-permute-done.6.edge = f32[32,128]{1,0:T(8,128)S(1)} collective-permute-done((f32[32,128]{1,0:T(8,128)S(1)}, f32[32,128]{1,0:T(8,128)S(1)}, u32[]{:S(2)}, u32[]{:S(2)}) %collective-permute-start.6) | collective-permute-done | bytes 16416 | tf_op jit(solution)/shard_map/ppermute | solution.py:448
  22.9 0.0 collective-permute-done.7.main
  22.9 0.4 shard_map.69.u.refs_3_
  23.3 0.2 shard_map.70.meta
  23.5 13.8 %all_to_all.5.grams = f32[16,8,128]{2,1,0:T(8,128)S(1)} all-to-all(f32[16,8,128]{2,1,0:T(8,128)S(1)} %broadcast_in_dim.16), channel_id=1, replica_groups=mesh['tm'=2,'space'=16] {'space'}, dimensions={0} | all-to-all | bytes 131072 | tf_op jit(solution)/shard_map/all_to_all | solution.py:532
  37.4 1.8 %shard_map.71 = (f32[32,512]{1,0:T(8,128)}, f32[32,512]{1,0:T(8,128)}) custom-call(f32[16,8,128]{2,1,0:T(8,128)S(1)} %all_to_all.5.grams, f32[16,128]{1,0:T(8,128)S(1)} %shard_map.70.meta, f32[32,512]{1,0:T(8,128)S(1)} %get-tuple-element.41.u.refs_0_, f32[32,512]{1,0:T(8,128)S(1)} %get-tuple-element.53.refs_1_, f32[32,768]{1,0:T(8,128)S(1)} %get-tuple-element.48.refs_2_, ...), custom_call_target="tpu_custom_call" | custom-call | flops 1000000 | bytes 100000 | tf_op jit(solution)/shard_map/pallas_call | solution.py:32
  (12 shorter events, 0.1 us)
Async XLA Ops:
  0.6 1.1 %copy-start = (f32[2,8,3,4096]{3,1,2,0:T(8,128)S(1)}, f32[2,8,3,4096]{3,1,2,0:T(8,128)}, u32[]{:S(2)}) copy-start(f32[2,8,3,4096]{3,1,2,0:T(8,128)} %param.5) | copy-start | bytes 2359300
  0.6 1.1 %copy-start.1 = (f32[32,512]{1,0:T(8,128)S(1)}, f32[32,512]{1,0:T(8,128)}, u32[]{:S(2)}) copy-start(f32[32,512]{1,0:T(8,128)} %main.1) | copy-start | bytes 196612
  0.7 1.1 %copy-start.3 = (s32[2,8,3]{1,0,2:T(2,128)S(1)}, s32[2,8,3]{1,0,2:T(2,128)}, u32[]{:S(2)}) copy-start(s32[2,8,3]{1,0,2:T(2,128)} %param.6) | copy-start | bytes 580
  1.8 2.1 %copy-start.2 = (f32[2,4,8,8]{3,2,1,0:T(8,128)S(1)}, f32[2,4,8,8]{3,2,1,0:T(8,128)}, u32[]{:S(2)}) copy-start(f32[2,4,8,8]{3,2,1,0:T(8,128)} %mixing) | copy-start | bytes 6148
  2.0 3.1 %collective-permute-start.1 = (f32[864,128]{1,0:T(8,128)S(1)}, f32[864,128]{1,0:T(8,128)S(1)}, u32[]{:S(2)}, u32[]{:S(2)}) collective-permute-start(f32[864,128]{1,0:T(8,128)S(1)} %get-tuple-element.30), channel_id=1, source_target_pairs={{0,1},{1,0},{2,3},{3,2},{4,5},{5,4},{6,7},{7,6},{8,9},{9,8},{10,11... | collective-permute-start | bytes 1327112 | tf_op jit(solution)/shard_map/ppermute | solution.py:444
  2.5 2.6 %collective-permute-start = (f32[224,128]{1,0:T(8,128)S(1)}, f32[224,128]{1,0:T(8,128)S(1)}, u32[]{:S(2)}, u32[]{:S(2)}) collective-permute-start(f32[224,128]{1,0:T(8,128)S(1)} %get-tuple-element.29), channel_id=1, source_target_pairs={{0,0},{1,2},{2,1},{3,4},{4,3},{5,6},{6,5},{7,8},{8,7},{9,10},{10,9... | collective-permute-start | bytes 344072 | tf_op jit(solution)/shard_map/ppermute | solution.py:444
  3.2 10.1 %collective-permute-start.3 = (f32[480,128]{1,0:T(8,128)S(1)}, f32[480,128]{1,0:T(8,128)S(1)}, u32[]{:S(2)}, u32[]{:S(2)}) collective-permute-start(f32[480,128]{1,0:T(8,128)S(1)} %get-tuple-element.31), channel_id=1, source_target_pairs={{16,16},{17,18},{18,17},{19,20},{20,19},{21,22},{22,21},{23,24},{2... | collective-permute-start | bytes 737288 | tf_op jit(solution)/shard_map/ppermute | solution.py:444
  5.7 9.5 %collective-permute-start.4 = (f32[32,512]{1,0:T(8,128)S(1)}, f32[32,512]{1,0:T(8,128)S(1)}, u32[]{:S(2)}, u32[]{:S(2)}) collective-permute-start(f32[32,512]{1,0:T(8,128)S(1)} %get-tuple-element.41.u.refs_0_), channel_id=1, source_target_pairs={{0,16},{1,17},{2,18},{3,19},{4,20},{5,21},{6,22},{7,23},{8,24},{9,... | collective-permute-start | bytes 196616 | tf_op jit(solution)/shard_map/ppermute | solution.py:448
  8.3 5.1 %collective-permute-start.2 = (f32[32,256]{1,0:T(8,128)S(1)}, f32[32,256]{1,0:T(8,128)S(1)}, u32[]{:S(2)}, u32[]{:S(2)}) collective-permute-start(f32[32,256]{1,0:T(8,128)S(1)} %get-tuple-element.39), channel_id=1, source_target_pairs={{0,16},{1,18},{2,17},{3,20},{4,19},{5,22},{6,21},{7,24},{8,23},{9,... | collective-permute-start | bytes 98312 | tf_op jit(solution)/shard_map/ppermute | solution.py:448
  8.4 6.9 %collective-permute-start.5 = (f32[32,384]{1,0:T(8,128)S(1)}, f32[32,384]{1,0:T(8,128)S(1)}, u32[]{:S(2)}, u32[]{:S(2)}) collective-permute-start(f32[32,384]{1,0:T(8,128)S(1)} %get-tuple-element.42), channel_id=1, source_target_pairs={{0,17},{1,16},{2,19},{3,18},{4,21},{5,20},{6,23},{7,22},{8,25},{9,... | collective-permute-start | bytes 147464 | tf_op jit(solution)/shard_map/ppermute | solution.py:448
  15.3 7.6 %collective-permute-start.7 = (f32[32,768]{1,0:T(8,128)S(1)}, f32[32,768]{1,0:T(8,128)S(1)}, u32[]{:S(2)}, u32[]{:S(2)}) collective-permute-start(f32[32,768]{1,0:T(8,128)S(1)} %get-tuple-element.48.refs_2_), channel_id=1, source_target_pairs={{16,0},{17,1},{18,2},{19,3},{20,4},{21,5},{22,6},{23,7},{24,8},{25... | collective-permute-start | bytes 294920 | tf_op jit(solution)/shard_map/ppermute | solution.py:448
  19.1 3.7 %collective-permute-start.6 = (f32[32,128]{1,0:T(8,128)S(1)}, f32[32,128]{1,0:T(8,128)S(1)}, u32[]{:S(2)}, u32[]{:S(2)}) collective-permute-start(f32[32,128]{1,0:T(8,128)S(1)} %get-tuple-element.47), channel_id=1, source_target_pairs={{16,0},{17,2},{18,1},{19,4},{20,3},{21,6},{22,5},{23,8},{24,7},{25... | collective-permute-start | bytes 49160 | tf_op jit(solution)/shard_map/ppermute | solution.py:448

commit v4 on v3

--- a/solution.py
+++ b/solution.py
@@ -15,8 +15,8 @@
 GROUP = 4
 RIM_A, RIM_B = 5, 4
 FAR_A, FAR_B = 3, 2
-PUSH = 10**9
-ASIDE_1, ASIDE_2 = 3 * 10**8, 5 * 10**8
+PUSH = 3 * 10**9
+ASIDE_1, ASIDE_2 = 7 * 10**8, 5 * 10**8
 DOWN = 2.0**-16
 BF = jnp.bfloat16
 F32 = jnp.float32
@@ -69,19 +69,20 @@
     out[...] = jnp.zeros_like(out)
 
 
-def edge_kernel(nb, turning, _, blocks, mask, panels, near_b, to_a, *far_b):
+def edge_kernel(nb, turning, _, blocks, mask, panels, near_b, late_b, to_a, *far_b):
     width = panels.shape[1]
     turns = lax.axis_index("tm") == turning
 
-    def near(dst, low_side, column, keep=1.0):
+    def near(dst, later, at, low_side, column, keep=1.0):
         edge = 0 if low_side else nb - 1
         inner = 1 if low_side else nb - 2
         rest = [(edge, 0), (edge, 1), (inner, 0)] if low_side else [(inner, 2), (edge, 1), (edge, 2)]
-        slots = [(0, edge, j, j) for j in range(3)] + [(1, b, j, 4 + i) for i, (b, j) in enumerate(rest)]
-        for t, b, j, slot in slots:
+        slots = [(dst, 0, edge, j, j * 32) for j in range(3)]
+        slots += [(later, 1, b, j, at + i * 32) for i, (b, j) in enumerate(rest)]
+        for ref, t, b, j, start in slots:
             line = blocks[t, j, b : b + 1, :] * (column[t][j][b : b + 1, :] * keep)
             for r in range(32):
-                dst[slot * 32 + r : slot * 32 + r + 1, :] = line[:, r * 128 : (r + 1) * 128]
+                ref[start + r : start + r + 1, :] = line[:, r * 128 : (r + 1) * 128]
         dst[96:128, :] = panels[:, :128] if low_side else panels[:, width - 128 :]
 
     for side in range(2):
@@ -89,8 +90,8 @@
         @pl.when((parity() == side) & jnp.logical_not(turns))
         def _():
             column = [[presence(mask, t, j, nb) for j in range(3)] for t in range(RUN)]
-            near(near_b, side == 0, column, inside())
-            near(to_a, side == 1, column)
+            near(near_b, late_b, 0, side == 0, column, inside())
+            near(to_a, to_a, 128, side == 1, column)
 
     if not far_b:
         return
@@ -167,9 +168,10 @@
         )
 
 
-def taken(from_a, from_b, left, start):
+def taken(from_a, from_b, left, at_a, at_b=None):
     use_b = (parity() == 0) == left
-    return jnp.where(use_b, from_b[start : start + 32, :], from_a[start : start + 32, :])
+    at_b = at_a if at_b is None else at_b
+    return jnp.where(use_b, from_b[at_b : at_b + 32, :], from_a[at_a : at_a + 32, :])
 
 
 def rim_row(dst, index, first, y):
@@ -207,13 +209,13 @@
         split_halves(wide_b, 0, b_hi, b_lo)
 
 
-def pull_rim_kernel(turning, near_a, near_b, a_hi, a_lo, b_hi, b_lo, wide_a, wide_b):
+def pull_rim_kernel(turning, near_a, near_b, late_b, a_hi, a_lo, b_hi, b_lo, wide_a, wide_b):
     @pl.when(lax.axis_index("tm") != turning)
     def _():
         edge_rows(near_a, near_b, wide_a)
         none = jnp.zeros((32, 128), F32)
-        left = [taken(near_a, near_b, True, (4 + i) * 32) for i in range(3)]
-        right = [taken(near_a, near_b, False, (4 + i) * 32) for i in range(3)]
+        left = [taken(near_a, late_b, True, 128 + i * 32, i * 32) for i in range(3)]
+        right = [taken(near_a, late_b, False, 128 + i * 32, i * 32) for i in range(3)]
         rim_row(wide_b, 0, True, [none, none, left[0]])
         rim_row(wide_b, 1, False, [none, left[1], left[2]])
         rim_row(wide_b, 2, True, [right[0], right[1], none])
@@ -285,6 +287,12 @@
     return jnp.where(mine, new_g, g), jnp.where(mine, new_e, e)
 
 
+def panels_of(ref, own):
+    if ref.shape[0] == ROWS:
+        return ref[:, :own]
+    return jnp.concatenate([ref[i * ROWS : (i + 1) * ROWS, :] for i in range(own // 128)], axis=1)
+
+
 def by_side(e_a, e_b):
     even = parity() == 0
     return jnp.where(even, e_b, e_a), jnp.where(even, e_a, e_b)
@@ -323,10 +331,12 @@
                 old, expand, first, out, out_b):
     own = nb * BLOCK
     end = own + 128
+    pieces = own // 128
+    record = slice((pieces + 1) * ROWS, (pieces + 1) * ROWS + 2 * COLS)
 
     @pl.when(lax.axis_index("tm") != owner)
     def _():
-        out[: 2 * COLS, end:] = old[...]
+        out[record, :] = old[...]
 
     @pl.when(lax.axis_index("tm") == owner)
     def _():
@@ -339,12 +349,13 @@
         first[...] = u_own
         back = pull(pull(u * DOWN, tiles_b), tiles_a[1:-1])
         back_own = back[:, 128 : 128 + own]
-        out[:, :own] = back_own
-        out[:, own:end] = by_side(back[:, end:], back[:, :128])[1]
+        for i in range(pieces):
+            out[i * ROWS : (i + 1) * ROWS, :] = back_own[:, i * 128 : (i + 1) * 128]
+        out[pieces * ROWS : (pieces + 1) * ROWS, :] = by_side(back[:, end:], back[:, :128])[1]
         out_b[...] = by_side(back[:, 128:256], back[:, own:end])[1]
         g, e = noted(old[:COLS], old[COLS:], slot, gram(u_own), expand[:COLS])
         g, e = noted(g, e, slot + 1, gram(back_own), expand[COLS:] * (1.0 / DOWN))
-        out[: 2 * COLS, end:] = jnp.concatenate([g, e], axis=0)
+        out[record, :] = jnp.concatenate([g, e], axis=0)
 
 
 def pull_kernel(nb, owner, edge_b, main, edge_a, a_hi, a_lo, b_hi, b_lo, ra_hi, ra_lo, rb_hi, rb_lo, out):
@@ -353,7 +364,7 @@
     @pl.when(lax.axis_index("tm") == owner)
     def _():
         left, right = by_side(edge_a[...], edge_b[...])
-        v = jnp.concatenate([left, main[:, :own], right], axis=1)
+        v = jnp.concatenate([left, panels_of(main, own), right], axis=1)
         y = pull(v, tiles_of((b_hi, b_lo, rb_hi, rb_lo), 2, nb, -2, nb + 2))
         out[...] = pull(y, tiles_of((a_hi, a_lo, ra_hi, ra_lo), 1, nb, -1, nb + 1))
 
@@ -410,7 +421,7 @@
         scale = lax.rsqrt(jnp.maximum(square, 0.0) + 1e-06)
         later = [stack[2 * ROWS :]] if n + 1 < count else []
         stack = jnp.concatenate([stack[:ROWS]] + later, axis=0) * scale
-        back, u = stack[:ROWS], panels[n][:, :own]
+        back, u = stack[:ROWS], panels_of(panels[n], own)
         old = select[forward]
         select[forward] = (back, u) if old is None else (
             jnp.where(me == owner, back, old[0]), jnp.where(me == owner, u, old[1])
@@ -458,15 +469,15 @@
     turn = owners % GROUP != 0
     turning = owners - 1 if turn else owners
     begin = call(first_kernel, [f32(8, 128)], (), flops=10**9)
-    sizes = [224, 96 * (RIM_A + RIM_B), 96 * (FAR_A + FAR_B)] if turn else [224, 224]
+    sizes = [128, 96] + ([96 * (RIM_A + RIM_B), 96 * (FAR_A + FAR_B)] if turn else [224])
     edges = call(
         functools.partial(edge_kernel, nb, turning),
         [f32(n, 128) for n in sizes],
         (*begin, rows, mask, panels_in),
     )
-    near_b, near_a = beside(edges[0], partner_b, range(turning)), beside(edges[1], partner_a)
+    near_b, near_a = beside(edges[0], partner_b, range(turning)), beside(edges[2], partner_a)
     if turn:
-        far_b = beside(edges[2], partner_b, [turning])
+        far_b = beside(edges[3], partner_b, [turning])
     rows, mask, mixing, _ = lax.optimization_barrier((rows, mask, mixing, edges))
     *own_tiles, expand = call(
         functools.partial(own_kernel, nb),
@@ -480,7 +491,12 @@
         outs, scratch = [bf(deep_a, 256)] * 2 + [bf(deep_b, 256)] * 2, [vm(2, deep_a, 128), vm(2, deep_b, 128)]
         return call(kernel, outs, args, scratch)
 
-    pull_rims = rim_call(functools.partial(pull_rim_kernel, turning), 1, 2, (near_a, near_b))
+    def late_rims(after):
+        late, _ = lax.optimization_barrier((edges[1], after))
+        args = (near_a, near_b, beside(late, partner_b, range(turning)))
+        return rim_call(functools.partial(pull_rim_kernel, turning), 1, 2, args)
+
+    pull_rims = None
     if turn:
         turn_rims = rim_call(functools.partial(rim_kernel, turning), RIM_A, RIM_B, (far_b, near_a))
 
@@ -489,17 +505,19 @@
     stages = 2 * owners
     owner_of = [k if k < owners else stages - 1 - k for k in range(stages)]
     kept, result, k = [], None, 0
+    record = ROWS * (own // 128 + 1)
     while k < stages:
-        owner, slot = owner_of[k], k % GROUP
+        owner, slot, turned = owner_of[k], k % GROUP, False
         turns_here, turns_next = turn and k == owners - 1, turn and k + 1 == owners - 1
         if turns_here:
             first, main, send_b = call(
                 functools.partial(turn_kernel, nb, owner, slot),
-                [f32(ROWS, own), f32(ROWS, own + 256), f32(ROWS, 128)],
+                [f32(ROWS, own), f32(record + 2 * COLS, 128), f32(ROWS, 128)],
                 (edge_b, main, edge_a, *own_tiles, *turn_rims, meta, expand),
             )
             kept += [first, main]
-            meta = main[: 2 * COLS, own + 128 :]
+            turned = True
+            meta = main[record:]
             k += 2
         else:
             if k < owners:
@@ -510,6 +528,8 @@
                     [vm(2, 2 * BLOCK, 128)],
                     flops=PUSH,
                 )
+                if pull_rims is None:
+                    pull_rims = late_rims(send_b)
             else:
                 (main,) = call(
                     functools.partial(pull_kernel, nb, owner),
@@ -543,7 +563,7 @@
                 result = [jnp.where(c, new, old) for c, new, old in zip(live, pair, result)]
             main = pair[0 if k - 1 < owners else 1]
             send_b, send_a = edges_of(main, *((256, 384) if turn and k == owners - 1 else (128, 128)))
-            meta, kept, share = jnp.zeros((2 * COLS, 128), F32), [], False
+            meta, kept, share, turned = jnp.zeros((2 * COLS, 128), F32), [], False, False
         if k == stages:
             break
 
@@ -551,15 +571,16 @@
         if after != before:
             main = hop(main, before, after, lambda s: s)
         into_turn = turn and k == owners - 1
+        wide_a = 384 if into_turn else 128
         (edge_b,) = call(
             aside_kernel,
-            [f32(ROWS, 384 if into_turn else 128)],
+            [f32(ROWS, wide_a)],
             (hop(send_b, before, after, partner_b),) + ((turn_rims[0],) if into_turn else ()),
             flops=ASIDE_1 if into_turn else ASIDE_2,
         )
-        if main.shape[1] > own:
-            edge_a = main[:, own : own + 128]
-            meta = meta + main[: 2 * COLS, own + 128 :]
+        if turned:
+            edge_a = main[record - ROWS : record]
+            meta = meta + main[record:]
         else:
             edge_a = hop(send_a, before, after, partner_a)
             if share and after != before:

time: 39.4 us -> 38.7 us (0.982)
  blocking collectives: 13.8 us -> 13.2 us
    ppermute x5, starting transfers between devices: 11.3 us -> 10.6 us  [hop(): lax.ppermute(x, ('tm', 'space'), [(i * count + s, k * count + to(s)) for...]
    ppermute x3 -> x4, starting transfers between devices: 1.84 us -> 2.49 us  [beside(): return lax.ppermute(x, ('tm', 'space'), route)]
    all_to_all x1, blocking collectives: 13.8 us -> 13.2 us  [shards(): grams = lax.all_to_all(every, 'space', 0, 0)]
  transfers between devices with their start and end apart: 8 -> 9, of which waited for: 2 -> 2; matrix products, arithmetic and copies ran while one was open for 0% -> 0% of each run, Pallas kernels for 6% -> 6%
where the time goes in v4:
time: 38.7 us; the launch traced here: 38.5 us
  blocking collectives  13.2 us (34%)
  starting transfers between devices  13.1 us (34%)
  waiting for transfers between devices  5.31 us (14%)
  Pallas kernels  4.92 us (13%)
  local copies, waits for them, and re-layouts  1.13 us (3%)
  between operations  0.84 us (2%)
    all_to_all x1, blocking collectives, shards(): grams = lax.all_to_all(every, 'space', 0, 0)  13.2 us
    ppermute x5, starting transfers between devices, hop(): lax.ppermute(x, ('tm', 'space'), [(i * count + s, k * count + to(s)) for...  10.6 us
    ppermute x5, waiting for transfers between devices, hop(): lax.ppermute(x, ('tm', 'space'), [(i * count + s, k * count + to(s)) for...  5.3 us
    pallas_call x13, Pallas kernels, call(): pl.pallas_call(kernel, out_shape=shapes, in_specs=[pl.BlockSpec(memory_sp...  4.92 us
    ppermute x4, starting transfers between devices, beside(): return lax.ppermute(x, ('tm', 'space'), route)  2.49 us
    unnamed x8, local copies, waits for them, and re-layouts  1.11 us
  transfers between devices with their start and end apart: 9, of which 2 were waited for; matrix products, arithmetic and copies ran while one was open for 0% of the time, Pallas kernels for 6%

profile of v4, /device:TPU:0, one launch (start us, length us, event | category | flops | bytes accessed | tf_op | source)
XLA Modules:
  0.0 38.5 jit_solution(5233444535892066316)
XLA Ops:
  0.6 0.0 copy-start
  0.6 0.0 copy-start.1
  0.7 0.0 copy-start.3
  0.7 1.1 %copy-done = f32[2,8,3,4096]{3,1,2,0:T(8,128)S(1)} copy-done((f32[2,8,3,4096]{3,1,2,0:T(8,128)S(1)}, f32[2,8,3,4096]{3,1,2,0:T(8,128)}, u32[]{:S(2)}) %copy-start) | copy-done | bytes 786456
  1.8 0.0 copy-done.1
  1.8 0.0 copy-done.3
  1.8 0.0 copy-start.2
  1.8 0.2 shard_map.60
  2.0 0.5 %collective-permute-start.1 = (f32[864,128]{1,0:T(8,128)S(1)}, f32[864,128]{1,0:T(8,128)S(1)}, u32[]{:S(2)}, u32[]{:S(2)}) collective-permute-start(f32[864,128]{1,0:T(8,128)S(1)} %get-tuple-element.32), channel_id=1, source_target_pairs={{0,1},{1,0},{2,3},{3,2},{4,5},{5,4},{6,7},{7,6},{8,9},{9,8},{10,11... | collective-permute-start | bytes 1327112 | tf_op jit(solution)/shard_map/ppermute | solution.py:455
  2.5 0.7 %collective-permute-start = (f32[128,128]{1,0:T(8,128)S(1)}, f32[128,128]{1,0:T(8,128)S(1)}, u32[]{:S(2)}, u32[]{:S(2)}) collective-permute-start(f32[128,128]{1,0:T(8,128)S(1)} %get-tuple-element.31), channel_id=1, source_target_pairs={{0,0},{1,2},{2,1},{3,4},{4,3},{5,6},{6,5},{7,8},{8,7},{9,10},{10,9... | collective-permute-start | bytes 196616 | tf_op jit(solution)/shard_map/ppermute | solution.py:455
  3.2 0.7 %collective-permute-start.3 = (f32[480,128]{1,0:T(8,128)S(1)}, f32[480,128]{1,0:T(8,128)S(1)}, u32[]{:S(2)}, u32[]{:S(2)}) collective-permute-start(f32[480,128]{1,0:T(8,128)S(1)} %get-tuple-element.34), channel_id=1, source_target_pairs={{16,16},{17,18},{18,17},{19,20},{20,19},{21,22},{22,21},{23,24},{2... | collective-permute-start | bytes 737288 | tf_op jit(solution)/shard_map/ppermute | solution.py:455
  3.9 0.0 copy-done.2
  3.9 1.2 %shard_map.61 = (bf16[512,256]{1,0:T(8,128)(2,1)S(1)}, bf16[512,256]{1,0:T(8,128)(2,1)S(1)}, bf16[512,256]{1,0:T(8,128)(2,1)S(1)}, bf16[512,256]{1,0:T(8,128)(2,1)S(1)}, f32[16,128]{1,0:T(8,128)S(1)}) custom-call(f32[2,3,8,4096]{3,2,1,0:T(8,128)S(1)} %bitcast.5, s32[3,2,8]{2,1,0:T(2,128)S(1)} %bitcast.7, f32[2,4,8,8]{3,2,1,0:T(8,128)S(1)} %copy-done.2), custom_call_target="tpu_custom_call" | custom-call | flops 1000000 | bytes 100000 | tf_op jit(solution)/shard_map/pallas_call | solution.py:32
  5.1 0.0 collective-permute-done.near_b
  5.1 0.0 collective-permute-done.1.near_a.far_a
  5.1 0.6 %shard_map.62 = (f32[32,512]{1,0:T(8,128)S(1)}, f32[32,256]{1,0:T(8,128)S(1)}, f32[32,384]{1,0:T(8,128)S(1)}) custom-call(f32[32,128]{1,0:T(8,128)S(1)} %slice.24.edge_b, f32[32,512]{1,0:T(8,128)S(1)} %copy-done.1, f32[32,128]{1,0:T(8,128)S(1)} %slice.25.edge_a, f32[128,128]{1,0:T(8,128)S(1)} %collective-permute-done.near_b, ...), custom_call_target="tpu_custom_call" | custom-call | flops 3000000000 | bytes 100000 | tf_op jit(solution)/shard_map/pallas_call | solution.py:32
  5.7 2.5 %collective-permute-start.2 = (f32[32,256]{1,0:T(8,128)S(1)}, f32[32,256]{1,0:T(8,128)S(1)}, u32[]{:S(2)}, u32[]{:S(2)}) collective-permute-start(f32[32,256]{1,0:T(8,128)S(1)} %get-tuple-element.42), channel_id=1, source_target_pairs={{0,16},{1,18},{2,17},{3,20},{4,19},{5,22},{6,21},{7,24},{8,23},{9,... | collective-permute-start | bytes 98312 | tf_op jit(solution)/shard_map/ppermute | solution.py:459
  8.3 0.1 collective-permute-start.4
  8.4 4.2 %collective-permute-start.5 = (f32[32,384]{1,0:T(8,128)S(1)}, f32[32,384]{1,0:T(8,128)S(1)}, u32[]{:S(2)}, u32[]{:S(2)}) collective-permute-start(f32[32,384]{1,0:T(8,128)S(1)} %get-tuple-element.45), channel_id=1, source_target_pairs={{0,17},{1,16},{2,19},{3,18},{4,21},{5,20},{6,23},{7,22},{8,25},{9,... | collective-permute-start | bytes 147464 | tf_op jit(solution)/shard_map/ppermute | solution.py:459
  12.6 0.7 %collective-permute-start.8 = (f32[96,128]{1,0:T(8,128)S(1)}, f32[96,128]{1,0:T(8,128)S(1)}, u32[]{:S(2)}, u32[]{:S(2)}) collective-permute-start(f32[96,128]{1,0:T(8,128)S(1)} %get-tuple-element.52), channel_id=1, source_target_pairs={{0,0},{1,2},{2,1},{3,4},{4,3},{5,6},{6,5},{7,8},{8,7},{9,10},{10,9... | collective-permute-start | bytes 147464 | tf_op jit(solution)/shard_map/ppermute | solution.py:455
  13.2 0.2 shard_map.65.old
  13.4 0.0 collective-permute-done.3.far_b
  13.5 0.0 collective-permute-done.2.edge
  13.5 1.8 %collective-permute-done.5.edge_a = f32[32,384]{1,0:T(8,128)S(1)} collective-permute-done((f32[32,384]{1,0:T(8,128)S(1)}, f32[32,384]{1,0:T(8,128)S(1)}, u32[]{:S(2)}, u32[]{:S(2)}) %collective-permute-start.5) | collective-permute-done | bytes 49184 | tf_op jit(solution)/shard_map/ppermute | solution.py:459
  15.3 0.0 collective-permute-done.4.main
  15.3 3.7 %collective-permute-start.7 = (f32[176,128]{1,0:T(8,128)S(1)}, f32[176,128]{1,0:T(8,128)S(1)}, u32[]{:S(2)}, u32[]{:S(2)}) collective-permute-start(f32[176,128]{1,0:T(8,128)S(1)} %get-tuple-element.51.refs_2_), channel_id=1, source_target_pairs={{16,0},{17,1},{18,2},{19,3},{20,4},{21,5},{22,6},{23,7},{24,8},{25... | collective-permute-start | bytes 270344 | tf_op jit(solution)/shard_map/ppermute | solution.py:459
  19.0 0.1 collective-permute-start.6
  19.1 0.0 collective-permute-done.8.late_b
  19.1 0.2 shard_map.68
  19.3 3.5 %collective-permute-done.6.edge = f32[32,128]{1,0:T(8,128)S(1)} collective-permute-done((f32[32,128]{1,0:T(8,128)S(1)}, f32[32,128]{1,0:T(8,128)S(1)}, u32[]{:S(2)}, u32[]{:S(2)}) %collective-permute-start.6) | collective-permute-done | bytes 16416 | tf_op jit(solution)/shard_map/ppermute | solution.py:459
  22.8 0.0 collective-permute-done.7.main
  22.8 0.4 %shard_map.69.u.refs_3_ = f32[32,512]{1,0:T(8,128)S(1)} custom-call(f32[32,128]{1,0:T(8,128)S(1)} %shard_map.67.edge_b, f32[176,128]{1,0:T(8,128)S(1)} %collective-permute-done.7.main, f32[32,128]{1,0:T(8,128)S(1)} %slice.26.edge_a, bf16[512,256]{1,0:T(8,128)(2,1)S(1)} %get-tuple-element.38.a_hi, bf16[512,256]{1,0:T(8,128)(2,1)S(1)} %get-tuple-element.39.a_lo, ...), custom_call_target="tpu_custom_call" | custom-call | flops 1000000 | bytes 100000 | tf_op jit(solution)/shard_map/pallas_call | solution.py:32
  23.2 0.2 shard_map.70.meta
  23.4 13.2 %all_to_all.5.grams = f32[16,8,128]{2,1,0:T(8,128)S(1)} all-to-all(f32[16,8,128]{2,1,0:T(8,128)S(1)} %broadcast_in_dim.16), channel_id=1, replica_groups=mesh['tm'=2,'space'=16] {'space'}, dimensions={0} | all-to-all | bytes 131072 | tf_op jit(solution)/shard_map/all_to_all | solution.py:552
  36.7 1.8 %shard_map.71 = (f32[32,512]{1,0:T(8,128)}, f32[32,512]{1,0:T(8,128)}) custom-call(f32[16,8,128]{2,1,0:T(8,128)S(1)} %all_to_all.5.grams, f32[16,128]{1,0:T(8,128)S(1)} %shard_map.70.meta, f32[32,512]{1,0:T(8,128)S(1)} %get-tuple-element.44.u.refs_0_, f32[32,512]{1,0:T(8,128)S(1)} %get-tuple-element.57.refs_1_, f32[176,128]{1,0:T(8,128)S(1)} %get-tuple-element.51.refs_2_, ...), custom_call_target="tpu_custom_call" | custom-call | flops 1000000 | bytes 100000 | tf_op jit(solution)/shard_map/pallas_call | solution.py:32
  (12 shorter events, 0.1 us)
Async XLA Ops:
  0.6 1.1 %copy-start = (f32[2,8,3,4096]{3,1,2,0:T(8,128)S(1)}, f32[2,8,3,4096]{3,1,2,0:T(8,128)}, u32[]{:S(2)}) copy-start(f32[2,8,3,4096]{3,1,2,0:T(8,128)} %param.5) | copy-start | bytes 2359300
  0.6 1.1 %copy-start.1 = (f32[32,512]{1,0:T(8,128)S(1)}, f32[32,512]{1,0:T(8,128)}, u32[]{:S(2)}) copy-start(f32[32,512]{1,0:T(8,128)} %main.1) | copy-start | bytes 196612
  0.7 1.1 %copy-start.3 = (s32[2,8,3]{1,0,2:T(2,128)S(1)}, s32[2,8,3]{1,0,2:T(2,128)}, u32[]{:S(2)}) copy-start(s32[2,8,3]{1,0,2:T(2,128)} %param.6) | copy-start | bytes 580
  1.8 2.1 %copy-start.2 = (f32[2,4,8,8]{3,2,1,0:T(8,128)S(1)}, f32[2,4,8,8]{3,2,1,0:T(8,128)}, u32[]{:S(2)}) copy-start(f32[2,4,8,8]{3,2,1,0:T(8,128)} %mixing) | copy-start | bytes 6148
  2.0 3.1 %collective-permute-start.1 = (f32[864,128]{1,0:T(8,128)S(1)}, f32[864,128]{1,0:T(8,128)S(1)}, u32[]{:S(2)}, u32[]{:S(2)}) collective-permute-start(f32[864,128]{1,0:T(8,128)S(1)} %get-tuple-element.32), channel_id=1, source_target_pairs={{0,1},{1,0},{2,3},{3,2},{4,5},{5,4},{6,7},{7,6},{8,9},{9,8},{10,11... | collective-permute-start | bytes 1327112 | tf_op jit(solution)/shard_map/ppermute | solution.py:455
  2.5 2.6 %collective-permute-start = (f32[128,128]{1,0:T(8,128)S(1)}, f32[128,128]{1,0:T(8,128)S(1)}, u32[]{:S(2)}, u32[]{:S(2)}) collective-permute-start(f32[128,128]{1,0:T(8,128)S(1)} %get-tuple-element.31), channel_id=1, source_target_pairs={{0,0},{1,2},{2,1},{3,4},{4,3},{5,6},{6,5},{7,8},{8,7},{9,10},{10,9... | collective-permute-start | bytes 196616 | tf_op jit(solution)/shard_map/ppermute | solution.py:455
  3.2 10.2 %collective-permute-start.3 = (f32[480,128]{1,0:T(8,128)S(1)}, f32[480,128]{1,0:T(8,128)S(1)}, u32[]{:S(2)}, u32[]{:S(2)}) collective-permute-start(f32[480,128]{1,0:T(8,128)S(1)} %get-tuple-element.34), channel_id=1, source_target_pairs={{16,16},{17,18},{18,17},{19,20},{20,19},{21,22},{22,21},{23,24},{2... | collective-permute-start | bytes 737288 | tf_op jit(solution)/shard_map/ppermute | solution.py:455
  5.7 7.7 %collective-permute-start.2 = (f32[32,256]{1,0:T(8,128)S(1)}, f32[32,256]{1,0:T(8,128)S(1)}, u32[]{:S(2)}, u32[]{:S(2)}) collective-permute-start(f32[32,256]{1,0:T(8,128)S(1)} %get-tuple-element.42), channel_id=1, source_target_pairs={{0,16},{1,18},{2,17},{3,20},{4,19},{5,22},{6,21},{7,24},{8,23},{9,... | collective-permute-start | bytes 98312 | tf_op jit(solution)/shard_map/ppermute | solution.py:459
  8.3 7.1 %collective-permute-start.4 = (f32[32,512]{1,0:T(8,128)S(1)}, f32[32,512]{1,0:T(8,128)S(1)}, u32[]{:S(2)}, u32[]{:S(2)}) collective-permute-start(f32[32,512]{1,0:T(8,128)S(1)} %get-tuple-element.44.u.refs_0_), channel_id=1, source_target_pairs={{0,16},{1,17},{2,18},{3,19},{4,20},{5,21},{6,22},{7,23},{8,24},{9,... | collective-permute-start | bytes 196616 | tf_op jit(solution)/shard_map/ppermute | solution.py:459
  8.4 7.0 %collective-permute-start.5 = (f32[32,384]{1,0:T(8,128)S(1)}, f32[32,384]{1,0:T(8,128)S(1)}, u32[]{:S(2)}, u32[]{:S(2)}) collective-permute-start(f32[32,384]{1,0:T(8,128)S(1)} %get-tuple-element.45), channel_id=1, source_target_pairs={{0,17},{1,16},{2,19},{3,18},{4,21},{5,20},{6,23},{7,22},{8,25},{9,... | collective-permute-start | bytes 147464 | tf_op jit(solution)/shard_map/ppermute | solution.py:459
  12.6 6.6 %collective-permute-start.8 = (f32[96,128]{1,0:T(8,128)S(1)}, f32[96,128]{1,0:T(8,128)S(1)}, u32[]{:S(2)}, u32[]{:S(2)}) collective-permute-start(f32[96,128]{1,0:T(8,128)S(1)} %get-tuple-element.52), channel_id=1, source_target_pairs={{0,0},{1,2},{2,1},{3,4},{4,3},{5,6},{6,5},{7,8},{8,7},{9,10},{10,9... | collective-permute-start | bytes 147464 | tf_op jit(solution)/shard_map/ppermute | solution.py:455
  15.3 7.4 %collective-permute-start.7 = (f32[176,128]{1,0:T(8,128)S(1)}, f32[176,128]{1,0:T(8,128)S(1)}, u32[]{:S(2)}, u32[]{:S(2)}) collective-permute-start(f32[176,128]{1,0:T(8,128)S(1)} %get-tuple-element.51.refs_2_), channel_id=1, source_target_pairs={{16,0},{17,1},{18,2},{19,3},{20,4},{21,5},{22,6},{23,7},{24,8},{25... | collective-permute-start | bytes 270344 | tf_op jit(solution)/shard_map/ppermute | solution.py:459
  19.0 3.7 %collective-permute-start.6 = (f32[32,128]{1,0:T(8,128)S(1)}, f32[32,128]{1,0:T(8,128)S(1)}, u32[]{:S(2)}, u32[]{:S(2)}) collective-permute-start(f32[32,128]{1,0:T(8,128)S(1)} %get-tuple-element.50), channel_id=1, source_target_pairs={{16,0},{17,2},{18,1},{19,4},{20,3},{21,6},{22,5},{23,8},{24,7},{25... | collective-permute-start | bytes 49160 | tf_op jit(solution)/shard_map/ppermute | solution.py:459

commit v5 on v4

--- a/solution.py
+++ b/solution.py
@@ -16,6 +16,7 @@
 RIM_A, RIM_B = 5, 4
 FAR_A, FAR_B = 3, 2
 PUSH = 3 * 10**9
+ASIDE_0 = 10**10
 ASIDE_1, ASIDE_2 = 7 * 10**8, 5 * 10**8
 DOWN = 2.0**-16
 BF = jnp.bfloat16
@@ -69,46 +70,46 @@
     out[...] = jnp.zeros_like(out)
 
 
+def block_of(blocks, column, t, j, b, nb):
+    return blocks[t, j, pl.ds(b, BLOCK // 2, stride=nb), :] * column[t][j][b : b + 1, :]
+
+
 def edge_kernel(nb, turning, _, blocks, mask, panels, near_b, late_b, to_a, *far_b):
     width = panels.shape[1]
     turns = lax.axis_index("tm") == turning
-
-    def near(dst, later, at, low_side, column, keep=1.0):
+    column = [[presence(mask, t, j, nb) for j in range(3)] for t in range(RUN)]
+
+    def near(dst, later, at, low_side, keep=1.0):
         edge = 0 if low_side else nb - 1
         inner = 1 if low_side else nb - 2
+        for j in range(3):
+            dst[j * 32 : (j + 1) * 32, :] = block_of(blocks, column, 0, j, edge, nb) * keep
+        dst[96:128, :] = panels[:, :128] if low_side else panels[:, width - 128 :]
         rest = [(edge, 0), (edge, 1), (inner, 0)] if low_side else [(inner, 2), (edge, 1), (edge, 2)]
-        slots = [(dst, 0, edge, j, j * 32) for j in range(3)]
-        slots += [(later, 1, b, j, at + i * 32) for i, (b, j) in enumerate(rest)]
-        for ref, t, b, j, start in slots:
-            line = blocks[t, j, b : b + 1, :] * (column[t][j][b : b + 1, :] * keep)
-            for r in range(32):
-                ref[start + r : start + r + 1, :] = line[:, r * 128 : (r + 1) * 128]
-        dst[96:128, :] = panels[:, :128] if low_side else panels[:, width - 128 :]
+        for i, (b, j) in enumerate(rest):
+            later[at + i * 32 : at + (i + 1) * 32, :] = block_of(blocks, column, 1, j, b, nb) * keep
+
+    def far(dst, deep_a, deep_b, low_side, keep=1.0):
+        at = 0
+        for t, deep in ((0, deep_a), (1, deep_b)):
+            for b in range(deep) if low_side else range(nb - deep, nb):
+                for j in range(3):
+                    dst[at : at + 32, :] = block_of(blocks, column, t, j, b, nb) * keep
+                    at += 32
 
     for side in range(2):
 
         @pl.when((parity() == side) & jnp.logical_not(turns))
         def _():
-            column = [[presence(mask, t, j, nb) for j in range(3)] for t in range(RUN)]
-            near(near_b, late_b, 0, side == 0, column, inside())
-            near(to_a, to_a, 128, side == 1, column)
-
-    if not far_b:
-        return
-
-    @pl.when(turns)
-    def _():
-        even, odd = parity() == 0, parity() == 1
-        keep = inside()
-        for t, deep, start_a, wide, start_b in ((0, RIM_A, 0, FAR_A, 0), (1, RIM_B, 96 * RIM_A, FAR_B, 96 * FAR_A)):
-            column = [jnp.broadcast_to(presence(mask, t, j, nb), (nb, 128)) for j in range(3)]
-            for r in range(32):
-                for j in range(3):
-                    y = blocks[t, j, :, r * 128 : (r + 1) * 128] * column[j]
-                    for dst, rows, start, tail_if in ((to_a, deep, start_a, even), (far_b[0], wide, start_b, odd)):
-                        to = pl.ds(start + j * 32 + r, rows, stride=96)
-                        dst[to, :] = jnp.where(tail_if, y[nb - rows :], y[:rows])
-        far_b[0][...] = far_b[0][...] * keep
+            near(near_b, late_b, 0, side == 0, inside())
+            near(to_a, to_a, 128, side == 1)
+
+        if far_b:
+
+            @pl.when((parity() == side) & turns)
+            def _():
+                far(far_b[0], FAR_A, FAR_B, side == 0, inside())
+                far(to_a, RIM_A, RIM_B, side == 1)
 
 
 def banded(y, p):
@@ -139,20 +140,12 @@
         hi[:, lanes], lo[:, lanes] = split2(wide[at + half])
 
 
-def own_kernel(nb, blocks, mask, mixing, a_hi, a_lo, b_hi, b_lo, expand, wide):
+def own_kernel(nb, blocks, mask, mixing, a_hi, a_lo, b_hi, b_lo, expand, *wide):
+    column = [[presence(mask, t, j, nb) for j in range(3)] for t in range(RUN)]
     for t, hi, lo in ((0, a_hi, a_lo), (1, b_hi, b_lo)):
-        is_first = lax.rem(iota((nb, 128), 0), 2) == (1 - t)
-        column = [jnp.broadcast_to(presence(mask, t, j, nb), (nb, 128)) for j in range(3)]
-        for r in range(32):
-            lanes = slice(r * 128, (r + 1) * 128)
-            y = [blocks[t, j, :, lanes] * column[j] for j in range(3)]
-            for p in range(2):
-                first, second = banded(y, p)
-                for half in range(2):
-                    wide[2 * t + half, pl.ds(2 * r + p, nb, stride=BLOCK), :] = jnp.where(
-                        is_first, first[half], second[half]
-                    )
-        split_halves(wide, 2 * t, hi, lo)
+        for b in range(nb):
+            rim_row(wide[t], b, b % 2 == 1 - t, [block_of(blocks, column, t, j, b, nb) for j in range(3)])
+        split_halves(wide[t], 0, hi, lo)
     pick = (lax.rem(iota((COLS, 128), 1), COLS) == iota((COLS, 128), 0)).astype(F32)
     row, lane = iota((ROWS, 128), 0), lax.rem(iota((ROWS, 128), 1), ROWS)
     same = (row // COLS) == (lane // COLS)
@@ -358,34 +351,47 @@
         out[record, :] = jnp.concatenate([g, e], axis=0)
 
 
-def pull_kernel(nb, owner, edge_b, main, edge_a, a_hi, a_lo, b_hi, b_lo, ra_hi, ra_lo, rb_hi, rb_lo, out):
+def pull_kernel(nb, owner, slot, edge_b, main, edge_a, a_hi, a_lo, b_hi, b_lo, ra_hi, ra_lo, rb_hi, rb_lo,
+                old, expand, out, record, *every):
     own = nb * BLOCK
+
+    @pl.when(lax.axis_index("tm") != owner)
+    def _():
+        record[...] = old[...]
 
     @pl.when(lax.axis_index("tm") == owner)
     def _():
         left, right = by_side(edge_a[...], edge_b[...])
         v = jnp.concatenate([left, panels_of(main, own), right], axis=1)
         y = pull(v, tiles_of((b_hi, b_lo, rb_hi, rb_lo), 2, nb, -2, nb + 2))
-        out[...] = pull(y, tiles_of((a_hi, a_lo, ra_hi, ra_lo), 1, nb, -1, nb + 1))
-
-
-def note_kernel(nb, owner, slot, forward, u, old, expand, out):
+        u = pull(y, tiles_of((a_hi, a_lo, ra_hi, ra_lo), 1, nb, -1, nb + 1))
+        out[...] = u
+        record[:COLS], record[COLS:] = noted(old[:COLS], old[COLS:], slot, gram(u), expand[COLS:])
+
+    for ref in every:
+        for i in range(ref.shape[0]):
+            ref[i] = record[:COLS]
+
+
+def note_kernel(nb, owner, slot, u, old, expand, out):
     @pl.when(lax.axis_index("tm") != owner)
     def _():
         out[...] = old[...]
 
     @pl.when(lax.axis_index("tm") == owner)
     def _():
-        e = expand[:COLS] if forward else expand[COLS:]
-        out[:COLS], out[COLS:] = noted(old[:COLS], old[COLS:], slot, gram(u[:, : nb * BLOCK]), e)
+        out[:COLS], out[COLS:] = noted(old[:COLS], old[COLS:], slot, gram(u[:, : nb * BLOCK]), expand[:COLS])
 
 
 def exact(x, y):
-    m = x.shape[0]
+    rows = x.shape[0]
+    m = -(-rows // 16) * 16
+    if m > rows:
+        x = jnp.concatenate([x, jnp.zeros((m - rows, x.shape[1]), F32)], axis=0)
     o = lax.dot_general(
         jnp.concatenate(split3(x), axis=0), jnp.concatenate(split3(y), axis=1), NN, preferred_element_type=F32
     )
-    piece = [[o[i * m : (i + 1) * m, j * 128 : (j + 1) * 128] for j in range(3)] for i in range(3)]
+    piece = [[o[i * m : i * m + rows, j * 128 : (j + 1) * 128] for j in range(3)] for i in range(3)]
     small = (piece[0][2] + piece[2][0]) + piece[1][1]
     return (small + (piece[0][1] + piece[1][0])) + piece[0][0]
 
@@ -400,28 +406,32 @@
     growth = meta[COLS:, :]
     row, lane = iota((ROWS, 128), 0), iota((ROWS, 128), 1)
     same = (row // COLS) == (lax.rem(lane, ROWS) // COLS)
+    group = lane[:COLS] // ROWS
     me = lax.axis_index("tm")
 
-    def full(x, n):
+    def spread(x, n):
         turns = [x if k == n else pltpu.roll(x, ((k - n) % 4) * ROWS, 1) for k in range(4)]
-        group = lane[:COLS] // ROWS
-        spread = turns[0]
+        out = turns[0]
         for k in range(1, 4):
-            spread = jnp.where(group == k, turns[k], spread)
-        return jnp.where(same, jnp.concatenate([spread] * PANELS, axis=0), 0.0)
+            out = jnp.where(group == k, turns[k], out)
+        return out
+
+    def full(x):
+        return jnp.where(same, jnp.concatenate([x] * PANELS, axis=0), 0.0)
 
     count = len(stages)
-    h = full(growth, 0)
-    stack = jnp.concatenate([h, exact(jnp.concatenate([full(total, n)[:, :ROWS] for n in range(count)], axis=0), h)])
+    grow = [spread(growth, n) for n in range(count)]
+    products = jnp.concatenate([spread(total, n)[:, :ROWS] for n in range(count)], axis=0)
+    stack = jnp.concatenate([grow[0], exact(products, full(grow[0]))], axis=0)
     select = {True: None, False: None}
     for n, (owner, forward) in enumerate(stages):
         if n:
-            stack = exact(stack[:, :ROWS], full(growth, n))
-        square = jnp.sum(stack[:ROWS] * stack[ROWS : 2 * ROWS], axis=0, keepdims=True)
+            stack = exact(stack[:, :ROWS], full(grow[n]))
+        square = jnp.sum(stack[:COLS] * stack[COLS : 2 * COLS], axis=0, keepdims=True)
         scale = lax.rsqrt(jnp.maximum(square, 0.0) + 1e-06)
-        later = [stack[2 * ROWS :]] if n + 1 < count else []
-        stack = jnp.concatenate([stack[:ROWS]] + later, axis=0) * scale
-        back, u = stack[:ROWS], panels_of(panels[n], own)
+        later = [stack[2 * COLS :]] if n + 1 < count else []
+        stack = jnp.concatenate([stack[:COLS]] + later, axis=0) * scale
+        back, u = stack[:COLS], panels_of(panels[n], own)
         old = select[forward]
         select[forward] = (back, u) if old is None else (
             jnp.where(me == owner, back, old[0]), jnp.where(me == owner, u, old[1])
@@ -431,7 +441,7 @@
             out[...] = jnp.zeros_like(out)
         else:
             back, u = select[forward]
-            left = jnp.concatenate(split2(back[:, :ROWS].T), axis=0)
+            left = jnp.concatenate(split2(full(back)[:, :ROWS].T), axis=0)
             o = lax.dot_general(left, jnp.concatenate(split2(u), axis=1), NN, preferred_element_type=F32)
             out[...] = (o[ROWS:, own:] + o[ROWS:, :own] + o[:ROWS, own:]) + o[:ROWS, :own]
 
@@ -464,7 +474,8 @@
             jnp.where(even, x[:, own - wide_a : own], x[:, :wide_a]),
         )
 
-    rows, mask = blocks.transpose(0, 2, 1, 3), block_mask.transpose(2, 0, 1)
+    rows = blocks.reshape(RUN, nb, 3, BLOCK // 2, 2 * BLOCK).transpose(0, 2, 3, 1, 4)
+    rows, mask = rows.reshape(RUN, 3, BLOCK // 2 * nb, 2 * BLOCK), block_mask.transpose(2, 0, 1)
     vm = lambda *s: pltpu.VMEM(s, F32)
     turn = owners % GROUP != 0
     turning = owners - 1 if turn else owners
@@ -476,6 +487,7 @@
         (*begin, rows, mask, panels_in),
     )
     near_b, near_a = beside(edges[0], partner_b, range(turning)), beside(edges[2], partner_a)
+    (near_b,) = call(aside_kernel, [f32(*near_b.shape)], (near_b,), flops=ASIDE_0)
     if turn:
         far_b = beside(edges[3], partner_b, [turning])
     rows, mask, mixing, _ = lax.optimization_barrier((rows, mask, mixing, edges))
@@ -483,7 +495,7 @@
         functools.partial(own_kernel, nb),
         [bf(own, 256)] * 4 + [f32(2 * COLS, 128)],
         (rows, mask, mixing),
-        [vm(2 * RUN, own, 128)],
+        [vm(2, own, 128)] * RUN,
     )
 
     def rim_call(kernel, deep_a, deep_b, args):
@@ -507,7 +519,7 @@
     kept, result, k = [], None, 0
     record = ROWS * (own // 128 + 1)
     while k < stages:
-        owner, slot, turned = owner_of[k], k % GROUP, False
+        owner, slot, turned, sums = owner_of[k], k % GROUP, False, []
         turns_here, turns_next = turn and k == owners - 1, turn and k + 1 == owners - 1
         if turns_here:
             first, main, send_b = call(
@@ -530,25 +542,26 @@
                 )
                 if pull_rims is None:
                     pull_rims = late_rims(send_b)
+                (meta,) = call(
+                    functools.partial(note_kernel, nb, owner, slot),
+                    [f32(2 * COLS, 128)],
+                    (main, meta, expand),
+                )
             else:
-                (main,) = call(
-                    functools.partial(pull_kernel, nb, owner),
-                    [f32(ROWS, own)],
-                    (edge_b, main, edge_a, *own_tiles, *pull_rims),
+                ends = (k + 1) % GROUP == 0 or k + 1 == stages
+                main, meta, *sums = call(
+                    functools.partial(pull_kernel, nb, owner, slot),
+                    [f32(ROWS, own), f32(2 * COLS, 128)] + [f32(count, COLS, 128)] * ends,
+                    (edge_b, main, edge_a, *own_tiles, *pull_rims, meta, expand),
                 )
                 send_b, send_a = edges_of(main, 128, 128)
-            (meta,) = call(
-                functools.partial(note_kernel, nb, owner, slot, k < owners),
-                [f32(2 * COLS, 128)],
-                (main, meta, expand),
-            )
             kept.append(main)
             k += 1
         share = not (turns_next and slot == 0)
 
         if k % GROUP == 0 or k == stages:
             todo = [(owner_of[i], i < owners) for i in range(k - len(kept), k)]
-            every = jnp.broadcast_to(meta[None, :COLS], (count, COLS, 128))
+            every = sums[0] if sums else jnp.broadcast_to(meta[None, :COLS], (count, COLS, 128))
             grams = lax.all_to_all(every, "space", 0, 0)
             pair = call(
                 functools.partial(scale_kernel, todo, count * own), [f32(ROWS, own)] * 2, (grams, meta, *kept)

time: 38.7 us -> 37.8 us (0.977)
  Pallas kernels: 4.92 us -> 3.92 us
  blocking collectives: 13.2 us -> 12.7 us
    ppermute x4, starting transfers between devices: 2.49 us -> 6.37 us  [beside(): return lax.ppermute(x, ('tm', 'space'), route)]
    ppermute x5, starting transfers between devices: 10.6 us -> 7.07 us  [hop(): lax.ppermute(x, ('tm', 'space'), [(i * count + s, k * count + to(s)) for...]
    pallas_call x13, Pallas kernels: 4.92 us -> 3.92 us  [call(): pl.pallas_call(kernel, out_shape=shapes, in_specs=[pl.BlockSpec(memory_sp...]
    all_to_all x1, blocking collectives: 13.2 us -> 12.7 us  [shards(): grams = lax.all_to_all(every, 'space', 0, 0)]
  transfers between devices with their start and end apart: 9 -> 9, of which waited for: 2 -> 3; matrix products, arithmetic and copies ran while one was open for 0% -> 0% of each run, Pallas kernels for 6% -> 4%
where the time goes in v5:
time: 37.8 us; the launch traced here: 37.6 us
  starting transfers between devices  13.4 us (35%)
  blocking collectives  12.7 us (34%)
  waiting for transfers between devices  5.59 us (15%)
  Pallas kernels  3.92 us (10%)
  local copies, waits for them, and re-layouts  1.12 us (3%)
  between operations  0.82 us (2%)
    all_to_all x1, blocking collectives, shards(): grams = lax.all_to_all(every, 'space', 0, 0)  12.7 us
    ppermute x5, starting transfers between devices, hop(): lax.ppermute(x, ('tm', 'space'), [(i * count + s, k * count + to(s)) for...  7.07 us
    ppermute x4, starting transfers between devices, beside(): return lax.ppermute(x, ('tm', 'space'), route)  6.37 us
    ppermute x5, waiting for transfers between devices, hop(): lax.ppermute(x, ('tm', 'space'), [(i * count + s, k * count + to(s)) for...  5.38 us
    pallas_call x13, Pallas kernels, call(): pl.pallas_call(kernel, out_shape=shapes, in_specs=[pl.BlockSpec(memory_sp...  3.92 us
    unnamed x8, local copies, waits for them, and re-layouts  1.11 us
  transfers between devices with their start and end apart: 9, of which 3 were waited for; matrix products, arithmetic and copies ran while one was open for 0% of the time, Pallas kernels for 4%

profile of v5, /device:TPU:0, one launch (start us, length us, event | category | flops | bytes accessed | tf_op | source)
XLA Modules:
  0.0 37.6 jit_solution(16901580171875911642)
XLA Ops:
  0.6 0.0 copy-start
  0.6 0.0 copy-start.1
  0.7 0.0 copy-start.3
  0.7 1.1 %copy-done = f32[2,8,3,4096]{3,1,2,0:T(8,128)S(1)} copy-done((f32[2,8,3,4096]{3,1,2,0:T(8,128)S(1)}, f32[2,8,3,4096]{3,1,2,0:T(8,128)}, u32[]{:S(2)}) %copy-start) | copy-done | bytes 786456
  1.8 0.0 copy-done.1
  1.8 0.0 copy-done.3
  1.8 0.0 copy-start.2
  1.8 0.1 shard_map.60
  1.9 0.7 %collective-permute-start = (f32[128,128]{1,0:T(8,128)S(1)}, f32[128,128]{1,0:T(8,128)S(1)}, u32[]{:S(2)}, u32[]{:S(2)}) collective-permute-start(f32[128,128]{1,0:T(8,128)S(1)} %get-tuple-element.34), channel_id=1, source_target_pairs={{0,0},{1,2},{2,1},{3,4},{4,3},{5,6},{6,5},{7,8},{8,7},{9,10},{10,9... | collective-permute-start | bytes 196616 | tf_op jit(solution)/shard_map/ppermute | solution.py:465
  2.6 4.4 %collective-permute-start.1 = (f32[864,128]{1,0:T(8,128)S(1)}, f32[864,128]{1,0:T(8,128)S(1)}, u32[]{:S(2)}, u32[]{:S(2)}) collective-permute-start(f32[864,128]{1,0:T(8,128)S(1)} %get-tuple-element.35), channel_id=1, source_target_pairs={{0,1},{1,0},{2,3},{3,2},{4,5},{5,4},{6,7},{7,6},{8,9},{9,8},{10,11... | collective-permute-start | bytes 1327112 | tf_op jit(solution)/shard_map/ppermute | solution.py:465
  7.0 0.7 %collective-permute-start.3 = (f32[480,128]{1,0:T(8,128)S(1)}, f32[480,128]{1,0:T(8,128)S(1)}, u32[]{:S(2)}, u32[]{:S(2)}) collective-permute-start(f32[480,128]{1,0:T(8,128)S(1)} %get-tuple-element.37), channel_id=1, source_target_pairs={{16,16},{17,18},{18,17},{19,20},{20,19},{21,22},{22,21},{23,24},{2... | collective-permute-start | bytes 737288 | tf_op jit(solution)/shard_map/ppermute | solution.py:465
  7.7 0.0 copy-done.2
  7.7 0.5 %shard_map.62 = (bf16[512,256]{1,0:T(8,128)(2,1)S(1)}, bf16[512,256]{1,0:T(8,128)(2,1)S(1)}, bf16[512,256]{1,0:T(8,128)(2,1)S(1)}, bf16[512,256]{1,0:T(8,128)(2,1)S(1)}, f32[16,128]{1,0:T(8,128)S(1)}) custom-call(f32[2,3,256,128]{3,2,1,0:T(8,128)S(1)} %bitcast.9, s32[3,2,8]{2,1,0:T(2,128)S(1)} %bitcast.11, f32[2,4,8,8]{3,2,1,0:T(8,128)S(1)} %copy-done.2), custom_call_target="tpu_custom_call" | custom-call | flops 1000000 | bytes 100000 | tf_op jit(solution)/shard_map/pallas_call | solution.py:33
  8.2 0.0 collective-permute-done.edge
  8.2 0.2 collective-permute-done.1.near_a.far_a
  8.4 0.6 %shard_map.63 = (f32[32,512]{1,0:T(8,128)S(1)}, f32[32,256]{1,0:T(8,128)S(1)}, f32[32,384]{1,0:T(8,128)S(1)}) custom-call(f32[32,128]{1,0:T(8,128)S(1)} %slice.20.edge_b, f32[32,512]{1,0:T(8,128)S(1)} %copy-done.1, f32[32,128]{1,0:T(8,128)S(1)} %slice.21.edge_a, f32[128,128]{1,0:T(8,128)S(1)} %shard_map.61.near_b, ...), custom_call_target="tpu_custom_call" | custom-call | flops 3000000000 | bytes 100000 | tf_op jit(solution)/shard_map/pallas_call | solution.py:33
  9.0 0.1 collective-permute-start.2
  9.1 2.0 %collective-permute-start.4 = (f32[32,512]{1,0:T(8,128)S(1)}, f32[32,512]{1,0:T(8,128)S(1)}, u32[]{:S(2)}, u32[]{:S(2)}) collective-permute-start(f32[32,512]{1,0:T(8,128)S(1)} %get-tuple-element.47.u.refs_0_), channel_id=1, source_target_pairs={{0,16},{1,17},{2,18},{3,19},{4,20},{5,21},{6,22},{7,23},{8,24},{9,... | collective-permute-start | bytes 196616 | tf_op jit(solution)/shard_map/ppermute | solution.py:469
  11.1 1.3 %collective-permute-start.5 = (f32[32,384]{1,0:T(8,128)S(1)}, f32[32,384]{1,0:T(8,128)S(1)}, u32[]{:S(2)}, u32[]{:S(2)}) collective-permute-start(f32[32,384]{1,0:T(8,128)S(1)} %get-tuple-element.48), channel_id=1, source_target_pairs={{0,17},{1,16},{2,19},{3,18},{4,21},{5,20},{6,23},{7,22},{8,25},{9,... | collective-permute-start | bytes 147464 | tf_op jit(solution)/shard_map/ppermute | solution.py:469
  12.4 0.7 %collective-permute-start.8 = (f32[96,128]{1,0:T(8,128)S(1)}, f32[96,128]{1,0:T(8,128)S(1)}, u32[]{:S(2)}, u32[]{:S(2)}) collective-permute-start(f32[96,128]{1,0:T(8,128)S(1)} %get-tuple-element.55), channel_id=1, source_target_pairs={{0,0},{1,2},{2,1},{3,4},{4,3},{5,6},{6,5},{7,8},{8,7},{9,10},{10,9... | collective-permute-start | bytes 147464 | tf_op jit(solution)/shard_map/ppermute | solution.py:465
  13.1 0.2 shard_map.66.old
  13.3 0.0 collective-permute-done.3.far_b
  13.3 0.0 collective-permute-done.2.edge
  13.4 1.9 %collective-permute-done.5.edge_a = f32[32,384]{1,0:T(8,128)S(1)} collective-permute-done((f32[32,384]{1,0:T(8,128)S(1)}, f32[32,384]{1,0:T(8,128)S(1)}, u32[]{:S(2)}, u32[]{:S(2)}) %collective-permute-start.5) | collective-permute-done | bytes 49184 | tf_op jit(solution)/shard_map/ppermute | solution.py:469
  15.3 0.0 collective-permute-done.4.main
  15.3 3.6 %collective-permute-start.7 = (f32[176,128]{1,0:T(8,128)S(1)}, f32[176,128]{1,0:T(8,128)S(1)}, u32[]{:S(2)}, u32[]{:S(2)}) collective-permute-start(f32[176,128]{1,0:T(8,128)S(1)} %get-tuple-element.54.refs_2_), channel_id=1, source_target_pairs={{16,0},{17,1},{18,2},{19,3},{20,4},{21,5},{22,6},{23,7},{24,8},{25... | collective-permute-start | bytes 270344 | tf_op jit(solution)/shard_map/ppermute | solution.py:469
  18.9 0.1 collective-permute-start.6
  18.9 0.0 collective-permute-done.8.late_b
  18.9 0.2 shard_map.69
  19.1 3.5 %collective-permute-done.6.edge = f32[32,128]{1,0:T(8,128)S(1)} collective-permute-done((f32[32,128]{1,0:T(8,128)S(1)}, f32[32,128]{1,0:T(8,128)S(1)}, u32[]{:S(2)}, u32[]{:S(2)}) %collective-permute-start.6) | collective-permute-done | bytes 16416 | tf_op jit(solution)/shard_map/ppermute | solution.py:469
  22.6 0.0 collective-permute-done.7.main
  22.6 0.7 %shard_map.70 = (f32[32,512]{1,0:T(8,128)S(1)}, f32[16,128]{1,0:T(8,128)S(1)}, f32[16,8,128]{2,1,0:T(8,128)S(1)}) custom-call(f32[32,128]{1,0:T(8,128)S(1)} %shard_map.68.edge_b, f32[176,128]{1,0:T(8,128)S(1)} %collective-permute-done.7.main, f32[32,128]{1,0:T(8,128)S(1)} %slice.22.edge_a, bf16[512,256]{1,0:T(8,128)(2,1)S(1)} %get-tuple-element.41.a_hi, ...), custom_call_target="tpu_custom_call" | custom-call | flops 1000000 | bytes 100000 | tf_op jit(solution)/shard_map/pallas_call | solution.py:33
  23.3 12.7 %all_to_all.5.grams = f32[16,8,128]{2,1,0:T(8,128)S(1)} all-to-all(f32[16,8,128]{2,1,0:T(8,128)S(1)} %get-tuple-element.60), channel_id=1, replica_groups=mesh['tm'=2,'space'=16] {'space'}, dimensions={0} | all-to-all | bytes 131072 | tf_op jit(solution)/shard_map/all_to_all | solution.py:565
  36.0 1.6 %shard_map.71 = (f32[32,512]{1,0:T(8,128)}, f32[32,512]{1,0:T(8,128)}) custom-call(f32[16,8,128]{2,1,0:T(8,128)S(1)} %all_to_all.5.grams, f32[16,128]{1,0:T(8,128)S(1)} %get-tuple-element.61.meta, f32[32,512]{1,0:T(8,128)S(1)} %get-tuple-element.47.u.refs_0_, f32[32,512]{1,0:T(8,128)S(1)} %get-tuple-element.62.refs_1_, ...), custom_call_target="tpu_custom_call" | custom-call | flops 1000000 | bytes 100000 | tf_op jit(solution)/shard_map/pallas_call | solution.py:33
  (11 shorter events, 0.1 us)
Async XLA Ops:
  0.6 1.1 %copy-start = (f32[2,8,3,4096]{3,1,2,0:T(8,128)S(1)}, f32[2,8,3,4096]{3,1,2,0:T(8,128)}, u32[]{:S(2)}) copy-start(f32[2,8,3,4096]{3,1,2,0:T(8,128)} %param.5) | copy-start | bytes 2359300
  0.6 1.1 %copy-start.1 = (f32[32,512]{1,0:T(8,128)S(1)}, f32[32,512]{1,0:T(8,128)}, u32[]{:S(2)}) copy-start(f32[32,512]{1,0:T(8,128)} %main.1) | copy-start | bytes 196612
  0.7 1.1 %copy-start.3 = (s32[2,8,3]{1,0,2:T(2,128)S(1)}, s32[2,8,3]{1,0,2:T(2,128)}, u32[]{:S(2)}) copy-start(s32[2,8,3]{1,0,2:T(2,128)} %param.6) | copy-start | bytes 580
  1.8 5.9 %copy-start.2 = (f32[2,4,8,8]{3,2,1,0:T(8,128)S(1)}, f32[2,4,8,8]{3,2,1,0:T(8,128)}, u32[]{:S(2)}) copy-start(f32[2,4,8,8]{3,2,1,0:T(8,128)} %mixing) | copy-start | bytes 6148
  1.9 6.3 %collective-permute-start = (f32[128,128]{1,0:T(8,128)S(1)}, f32[128,128]{1,0:T(8,128)S(1)}, u32[]{:S(2)}, u32[]{:S(2)}) collective-permute-start(f32[128,128]{1,0:T(8,128)S(1)} %get-tuple-element.34), channel_id=1, source_target_pairs={{0,0},{1,2},{2,1},{3,4},{4,3},{5,6},{6,5},{7,8},{8,7},{9,10},{10,9... | collective-permute-start | bytes 196616 | tf_op jit(solution)/shard_map/ppermute | solution.py:465
  2.6 5.8 %collective-permute-start.1 = (f32[864,128]{1,0:T(8,128)S(1)}, f32[864,128]{1,0:T(8,128)S(1)}, u32[]{:S(2)}, u32[]{:S(2)}) collective-permute-start(f32[864,128]{1,0:T(8,128)S(1)} %get-tuple-element.35), channel_id=1, source_target_pairs={{0,1},{1,0},{2,3},{3,2},{4,5},{5,4},{6,7},{7,6},{8,9},{9,8},{10,11... | collective-permute-start | bytes 1327112 | tf_op jit(solution)/shard_map/ppermute | solution.py:465
  7.0 6.3 %collective-permute-start.3 = (f32[480,128]{1,0:T(8,128)S(1)}, f32[480,128]{1,0:T(8,128)S(1)}, u32[]{:S(2)}, u32[]{:S(2)}) collective-permute-start(f32[480,128]{1,0:T(8,128)S(1)} %get-tuple-element.37), channel_id=1, source_target_pairs={{16,16},{17,18},{18,17},{19,20},{20,19},{21,22},{22,21},{23,24},{2... | collective-permute-start | bytes 737288 | tf_op jit(solution)/shard_map/ppermute | solution.py:465
  9.0 4.3 %collective-permute-start.2 = (f32[32,256]{1,0:T(8,128)S(1)}, f32[32,256]{1,0:T(8,128)S(1)}, u32[]{:S(2)}, u32[]{:S(2)}) collective-permute-start(f32[32,256]{1,0:T(8,128)S(1)} %get-tuple-element.45), channel_id=1, source_target_pairs={{0,16},{1,18},{2,17},{3,20},{4,19},{5,22},{6,21},{7,24},{8,23},{9,... | collective-permute-start | bytes 98312 | tf_op jit(solution)/shard_map/ppermute | solution.py:469
  9.1 6.2 %collective-permute-start.4 = (f32[32,512]{1,0:T(8,128)S(1)}, f32[32,512]{1,0:T(8,128)S(1)}, u32[]{:S(2)}, u32[]{:S(2)}) collective-permute-start(f32[32,512]{1,0:T(8,128)S(1)} %get-tuple-element.47.u.refs_0_), channel_id=1, source_target_pairs={{0,16},{1,17},{2,18},{3,19},{4,20},{5,21},{6,22},{7,23},{8,24},{9,... | collective-permute-start | bytes 196616 | tf_op jit(solution)/shard_map/ppermute | solution.py:469
  11.1 4.2 %collective-permute-start.5 = (f32[32,384]{1,0:T(8,128)S(1)}, f32[32,384]{1,0:T(8,128)S(1)}, u32[]{:S(2)}, u32[]{:S(2)}) collective-permute-start(f32[32,384]{1,0:T(8,128)S(1)} %get-tuple-element.48), channel_id=1, source_target_pairs={{0,17},{1,16},{2,19},{3,18},{4,21},{5,20},{6,23},{7,22},{8,25},{9,... | collective-permute-start | bytes 147464 | tf_op jit(solution)/shard_map/ppermute | solution.py:469
  12.4 6.6 %collective-permute-start.8 = (f32[96,128]{1,0:T(8,128)S(1)}, f32[96,128]{1,0:T(8,128)S(1)}, u32[]{:S(2)}, u32[]{:S(2)}) collective-permute-start(f32[96,128]{1,0:T(8,128)S(1)} %get-tuple-element.55), channel_id=1, source_target_pairs={{0,0},{1,2},{2,1},{3,4},{4,3},{5,6},{6,5},{7,8},{8,7},{9,10},{10,9... | collective-permute-start | bytes 147464 | tf_op jit(solution)/shard_map/ppermute | solution.py:465
  15.3 7.4 %collective-permute-start.7 = (f32[176,128]{1,0:T(8,128)S(1)}, f32[176,128]{1,0:T(8,128)S(1)}, u32[]{:S(2)}, u32[]{:S(2)}) collective-permute-start(f32[176,128]{1,0:T(8,128)S(1)} %get-tuple-element.54.refs_2_), channel_id=1, source_target_pairs={{16,0},{17,1},{18,2},{19,3},{20,4},{21,5},{22,6},{23,7},{24,8},{25... | collective-permute-start | bytes 270344 | tf_op jit(solution)/shard_map/ppermute | solution.py:469
  18.9 3.7 %collective-permute-start.6 = (f32[32,128]{1,0:T(8,128)S(1)}, f32[32,128]{1,0:T(8,128)S(1)}, u32[]{:S(2)}, u32[]{:S(2)}) collective-permute-start(f32[32,128]{1,0:T(8,128)S(1)} %get-tuple-element.53), channel_id=1, source_target_pairs={{16,0},{17,2},{18,1},{19,4},{20,3},{21,6},{22,5},{23,8},{24,7},{25... | collective-permute-start | bytes 49160 | tf_op jit(solution)/shard_map/ppermute | solution.py:469

commit v6 on v5

--- a/solution.py
+++ b/solution.py
@@ -127,13 +127,6 @@
     return high, (x - high.astype(F32)).astype(BF)
 
 
-def split3(x):
-    first = x.astype(BF)
-    x = x - first.astype(F32)
-    second = x.astype(BF)
-    return first, second, (x - second.astype(F32)).astype(BF)
-
-
 def split_halves(wide, at, hi, lo):
     for half in range(2):
         lanes = slice(half * 128, half * 128 + 128)
@@ -292,15 +285,7 @@
 
 
 def aside_kernel(edge, *refs):
-    out = refs[-1]
-    width, wanted = edge.shape[1], out.shape[1]
-    if width == wanted:
-        out[...] = edge[...]
-        return
-    none = jnp.zeros((ROWS, wanted - width), F32)
-    left = jnp.concatenate([none, edge[...]], axis=1)
-    right = jnp.concatenate([edge[...], none], axis=1)
-    out[...] = jnp.where(parity() == 0, left, right)
+    refs[-1][...] = edge[...]
 
 
 def push_kernel(nb, owner, edge_b, main, edge_a, near_b, near_a, a_hi, a_lo, b_hi, b_lo, out, out_b, out_a, wide):
@@ -323,7 +308,6 @@
 def turn_kernel(nb, owner, slot, edge_b, main, edge_a, a_hi, a_lo, b_hi, b_lo, ra_hi, ra_lo, rb_hi, rb_lo,
                 old, expand, first, out, out_b):
     own = nb * BLOCK
-    end = own + 128
     pieces = own // 128
     record = slice((pieces + 1) * ROWS, (pieces + 1) * ROWS + 2 * COLS)
 
@@ -331,24 +315,28 @@
     def _():
         out[record, :] = old[...]
 
-    @pl.when(lax.axis_index("tm") == owner)
-    def _():
-        left, right = by_side(edge_a[...], edge_b[...])
-        v = jnp.concatenate([left, main[:, :own], right], axis=1)
-        tiles_a = tiles_of((a_hi, a_lo, ra_hi, ra_lo), RIM_A, nb, -RIM_A, nb + RIM_A)
-        tiles_b = tiles_of((b_hi, b_lo, rb_hi, rb_lo), RIM_B, nb, -RIM_B, nb + RIM_B)
+    def turn(low, edges):
+        a0, a1 = (RIM_A, FAR_A) if low else (FAR_A, RIM_A)
+        b0, b1 = (RIM_B, FAR_B) if low else (FAR_B, RIM_B)
+        v = jnp.concatenate([edges[0], main[:, :own], edges[1]], axis=1)
+        tiles_a = tiles_of((a_hi, a_lo, ra_hi, ra_lo), RIM_A, nb, -a0, nb + a1)
+        tiles_b = tiles_of((b_hi, b_lo, rb_hi, rb_lo), RIM_B, nb, -b0, nb + b1)
         u = push(push(v, tiles_a), tiles_b)
-        u_own = u[:, 256 : 256 + own]
+        u_own = u[:, b0 * BLOCK : b0 * BLOCK + own]
         first[...] = u_own
         back = pull(pull(u * DOWN, tiles_b), tiles_a[1:-1])
-        back_own = back[:, 128 : 128 + own]
+        back_own, beyond = (back[:, 128:], back[:, :128]) if low else (back[:, :own], back[:, own:])
         for i in range(pieces):
             out[i * ROWS : (i + 1) * ROWS, :] = back_own[:, i * 128 : (i + 1) * 128]
-        out[pieces * ROWS : (pieces + 1) * ROWS, :] = by_side(back[:, end:], back[:, :128])[1]
-        out_b[...] = by_side(back[:, 128:256], back[:, own:end])[1]
+        out[pieces * ROWS : (pieces + 1) * ROWS, :] = beyond
+        out_b[...] = back_own[:, own - 128 :] if low else back_own[:, :128]
         g, e = noted(old[:COLS], old[COLS:], slot, gram(u_own), expand[:COLS])
         g, e = noted(g, e, slot + 1, gram(back_own), expand[COLS:] * (1.0 / DOWN))
         out[record, :] = jnp.concatenate([g, e], axis=0)
+
+    mine = lax.axis_index("tm") == owner
+    pl.when(mine & (parity() == 0))(lambda: turn(False, (edge_b[...], edge_a[...])))
+    pl.when(mine & (parity() == 1))(lambda: turn(True, (edge_a[...], edge_b[...])))
 
 
 def pull_kernel(nb, owner, slot, edge_b, main, edge_a, a_hi, a_lo, b_hi, b_lo, ra_hi, ra_lo, rb_hi, rb_lo,
@@ -389,11 +377,10 @@
     if m > rows:
         x = jnp.concatenate([x, jnp.zeros((m - rows, x.shape[1]), F32)], axis=0)
     o = lax.dot_general(
-        jnp.concatenate(split3(x), axis=0), jnp.concatenate(split3(y), axis=1), NN, preferred_element_type=F32
+        jnp.concatenate(split2(x), axis=0), jnp.concatenate(split2(y), axis=1), NN, preferred_element_type=F32
     )
-    piece = [[o[i * m : i * m + rows, j * 128 : (j + 1) * 128] for j in range(3)] for i in range(3)]
-    small = (piece[0][2] + piece[2][0]) + piece[1][1]
-    return (small + (piece[0][1] + piece[1][0])) + piece[0][0]
+    o = (o[m:, 128:] + o[m:, :128] + o[:m, 128:]) + o[:m, :128]
+    return o[:rows]
 
 
 def scale_kernel(stages, boxes, grams, meta, *refs):
@@ -584,10 +571,9 @@
         if after != before:
             main = hop(main, before, after, lambda s: s)
         into_turn = turn and k == owners - 1
-        wide_a = 384 if into_turn else 128
         (edge_b,) = call(
             aside_kernel,
-            [f32(ROWS, wide_a)],
+            [f32(*send_b.shape)],
             (hop(send_b, before, after, partner_b),) + ((turn_rims[0],) if into_turn else ()),
             flops=ASIDE_1 if into_turn else ASIDE_2,
         )

time: 37.8 us -> 37.7 us (level)
  no operation moved by 1% of the time
where the time goes in v6:
time: 37.7 us; the launch traced here: 37.4 us
  starting transfers between devices  13.3 us (35%)
  blocking collectives  12.7 us (34%)
  waiting for transfers between devices  5.6 us (15%)
  Pallas kernels  3.85 us (10%)
  local copies, waits for them, and re-layouts  1.12 us (3%)
  between operations  0.82 us (2%)
    all_to_all x1, blocking collectives, shards(): grams = lax.all_to_all(every, 'space', 0, 0)  12.7 us
    ppermute x5, starting transfers between devices, hop(): lax.ppermute(x, ('tm', 'space'), [(i * count + s, k * count + to(s)) for...  6.97 us
    ppermute x4, starting transfers between devices, beside(): return lax.ppermute(x, ('tm', 'space'), route)  6.37 us
    ppermute x5, waiting for transfers between devices, hop(): lax.ppermute(x, ('tm', 'space'), [(i * count + s, k * count + to(s)) for...  5.4 us
    pallas_call x13, Pallas kernels, call(): pl.pallas_call(kernel, out_shape=shapes, in_specs=[pl.BlockSpec(memory_sp...  3.85 us
    unnamed x8, local copies, waits for them, and re-layouts  1.11 us
  transfers between devices with their start and end apart: 9, of which 3 were waited for; matrix products, arithmetic and copies ran while one was open for 0% of the time, Pallas kernels for 4%

profile of v6, /device:TPU:0, one launch (start us, length us, event | category | flops | bytes accessed | tf_op | source)
XLA Modules:
  0.0 37.4 jit_solution(5503387098954113388)
XLA Ops:
  0.6 0.0 copy-start
  0.6 0.0 copy-start.1
  0.7 0.0 copy-start.3
  0.7 1.1 %copy-done = f32[2,8,3,4096]{3,1,2,0:T(8,128)S(1)} copy-done((f32[2,8,3,4096]{3,1,2,0:T(8,128)S(1)}, f32[2,8,3,4096]{3,1,2,0:T(8,128)}, u32[]{:S(2)}) %copy-start) | copy-done | bytes 786456
  1.8 0.0 copy-done.1
  1.8 0.0 copy-done.3
  1.8 0.0 copy-start.2
  1.8 0.1 shard_map.60
  1.9 0.7 %collective-permute-start = (f32[128,128]{1,0:T(8,128)S(1)}, f32[128,128]{1,0:T(8,128)S(1)}, u32[]{:S(2)}, u32[]{:S(2)}) collective-permute-start(f32[128,128]{1,0:T(8,128)S(1)} %get-tuple-element.34), channel_id=1, source_target_pairs={{0,0},{1,2},{2,1},{3,4},{4,3},{5,6},{6,5},{7,8},{8,7},{9,10},{10,9... | collective-permute-start | bytes 196616 | tf_op jit(solution)/shard_map/ppermute | solution.py:452
  2.6 4.4 %collective-permute-start.1 = (f32[864,128]{1,0:T(8,128)S(1)}, f32[864,128]{1,0:T(8,128)S(1)}, u32[]{:S(2)}, u32[]{:S(2)}) collective-permute-start(f32[864,128]{1,0:T(8,128)S(1)} %get-tuple-element.35), channel_id=1, source_target_pairs={{0,1},{1,0},{2,3},{3,2},{4,5},{5,4},{6,7},{7,6},{8,9},{9,8},{10,11... | collective-permute-start | bytes 1327112 | tf_op jit(solution)/shard_map/ppermute | solution.py:452
  7.0 0.7 %collective-permute-start.3 = (f32[480,128]{1,0:T(8,128)S(1)}, f32[480,128]{1,0:T(8,128)S(1)}, u32[]{:S(2)}, u32[]{:S(2)}) collective-permute-start(f32[480,128]{1,0:T(8,128)S(1)} %get-tuple-element.37), channel_id=1, source_target_pairs={{16,16},{17,18},{18,17},{19,20},{20,19},{21,22},{22,21},{23,24},{2... | collective-permute-start | bytes 737288 | tf_op jit(solution)/shard_map/ppermute | solution.py:452
  7.7 0.0 copy-done.2
  7.7 0.5 %shard_map.62 = (bf16[512,256]{1,0:T(8,128)(2,1)S(1)}, bf16[512,256]{1,0:T(8,128)(2,1)S(1)}, bf16[512,256]{1,0:T(8,128)(2,1)S(1)}, bf16[512,256]{1,0:T(8,128)(2,1)S(1)}, f32[16,128]{1,0:T(8,128)S(1)}) custom-call(f32[2,3,256,128]{3,2,1,0:T(8,128)S(1)} %bitcast.9, s32[3,2,8]{2,1,0:T(2,128)S(1)} %bitcast.11, f32[2,4,8,8]{3,2,1,0:T(8,128)S(1)} %copy-done.2), custom_call_target="tpu_custom_call" | custom-call | flops 1000000 | bytes 100000 | tf_op jit(solution)/shard_map/pallas_call | solution.py:33
  8.2 0.0 collective-permute-done.edge
  8.2 0.2 collective-permute-done.1.near_a.far_a
  8.4 0.6 %shard_map.63 = (f32[32,512]{1,0:T(8,128)S(1)}, f32[32,256]{1,0:T(8,128)S(1)}, f32[32,384]{1,0:T(8,128)S(1)}) custom-call(f32[32,128]{1,0:T(8,128)S(1)} %slice.20.edge_b, f32[32,512]{1,0:T(8,128)S(1)} %copy-done.1, f32[32,128]{1,0:T(8,128)S(1)} %slice.21.edge_a, f32[128,128]{1,0:T(8,128)S(1)} %shard_map.61.near_b, ...), custom_call_target="tpu_custom_call" | custom-call | flops 3000000000 | bytes 100000 | tf_op jit(solution)/shard_map/pallas_call | solution.py:33
  9.0 0.1 collective-permute-start.2
  9.1 2.0 %collective-permute-start.4 = (f32[32,512]{1,0:T(8,128)S(1)}, f32[32,512]{1,0:T(8,128)S(1)}, u32[]{:S(2)}, u32[]{:S(2)}) collective-permute-start(f32[32,512]{1,0:T(8,128)S(1)} %get-tuple-element.47.u.refs_0_), channel_id=1, source_target_pairs={{0,16},{1,17},{2,18},{3,19},{4,20},{5,21},{6,22},{7,23},{8,24},{9,... | collective-permute-start | bytes 196616 | tf_op jit(solution)/shard_map/ppermute | solution.py:456
  11.1 1.3 %collective-permute-start.5 = (f32[32,384]{1,0:T(8,128)S(1)}, f32[32,384]{1,0:T(8,128)S(1)}, u32[]{:S(2)}, u32[]{:S(2)}) collective-permute-start(f32[32,384]{1,0:T(8,128)S(1)} %get-tuple-element.48), channel_id=1, source_target_pairs={{0,17},{1,16},{2,19},{3,18},{4,21},{5,20},{6,23},{7,22},{8,25},{9,... | collective-permute-start | bytes 147464 | tf_op jit(solution)/shard_map/ppermute | solution.py:456
  12.4 0.7 %collective-permute-start.8 = (f32[96,128]{1,0:T(8,128)S(1)}, f32[96,128]{1,0:T(8,128)S(1)}, u32[]{:S(2)}, u32[]{:S(2)}) collective-permute-start(f32[96,128]{1,0:T(8,128)S(1)} %get-tuple-element.55), channel_id=1, source_target_pairs={{0,0},{1,2},{2,1},{3,4},{4,3},{5,6},{6,5},{7,8},{8,7},{9,10},{10,9... | collective-permute-start | bytes 147464 | tf_op jit(solution)/shard_map/ppermute | solution.py:452
  13.1 0.2 shard_map.66.old
  13.3 0.0 collective-permute-done.3.far_b
  13.3 0.0 collective-permute-done.2.edge
  13.3 1.9 %collective-permute-done.5.edge_a = f32[32,384]{1,0:T(8,128)S(1)} collective-permute-done((f32[32,384]{1,0:T(8,128)S(1)}, f32[32,384]{1,0:T(8,128)S(1)}, u32[]{:S(2)}, u32[]{:S(2)}) %collective-permute-start.5) | collective-permute-done | bytes 49184 | tf_op jit(solution)/shard_map/ppermute | solution.py:456
  15.3 0.0 collective-permute-done.4.main
  15.3 3.5 %collective-permute-start.7 = (f32[176,128]{1,0:T(8,128)S(1)}, f32[176,128]{1,0:T(8,128)S(1)}, u32[]{:S(2)}, u32[]{:S(2)}) collective-permute-start(f32[176,128]{1,0:T(8,128)S(1)} %get-tuple-element.54.refs_2_), channel_id=1, source_target_pairs={{16,0},{17,1},{18,2},{19,3},{20,4},{21,5},{22,6},{23,7},{24,8},{25... | collective-permute-start | bytes 270344 | tf_op jit(solution)/shard_map/ppermute | solution.py:456
  18.8 0.1 collective-permute-start.6
  18.8 0.0 collective-permute-done.8.late_b
  18.8 0.2 shard_map.69
  19.0 3.5 %collective-permute-done.6.edge = f32[32,128]{1,0:T(8,128)S(1)} collective-permute-done((f32[32,128]{1,0:T(8,128)S(1)}, f32[32,128]{1,0:T(8,128)S(1)}, u32[]{:S(2)}, u32[]{:S(2)}) %collective-permute-start.6) | collective-permute-done | bytes 16416 | tf_op jit(solution)/shard_map/ppermute | solution.py:456
  22.5 0.0 collective-permute-done.7.main
  22.5 0.7 %shard_map.70 = (f32[32,512]{1,0:T(8,128)S(1)}, f32[16,128]{1,0:T(8,128)S(1)}, f32[16,8,128]{2,1,0:T(8,128)S(1)}) custom-call(f32[32,128]{1,0:T(8,128)S(1)} %shard_map.68.edge_b, f32[176,128]{1,0:T(8,128)S(1)} %collective-permute-done.7.main, f32[32,128]{1,0:T(8,128)S(1)} %slice.22.edge_a, bf16[512,256]{1,0:T(8,128)(2,1)S(1)} %get-tuple-element.41.a_hi, ...), custom_call_target="tpu_custom_call" | custom-call | flops 1000000 | bytes 100000 | tf_op jit(solution)/shard_map/pallas_call | solution.py:33
  23.2 12.7 %all_to_all.5.grams = f32[16,8,128]{2,1,0:T(8,128)S(1)} all-to-all(f32[16,8,128]{2,1,0:T(8,128)S(1)} %get-tuple-element.60), channel_id=1, replica_groups=mesh['tm'=2,'space'=16] {'space'}, dimensions={0} | all-to-all | bytes 131072 | tf_op jit(solution)/shard_map/all_to_all | solution.py:552
  35.9 1.5 %shard_map.71 = (f32[32,512]{1,0:T(8,128)}, f32[32,512]{1,0:T(8,128)}) custom-call(f32[16,8,128]{2,1,0:T(8,128)S(1)} %all_to_all.5.grams, f32[16,128]{1,0:T(8,128)S(1)} %get-tuple-element.61.meta, f32[32,512]{1,0:T(8,128)S(1)} %get-tuple-element.47.u.refs_0_, f32[32,512]{1,0:T(8,128)S(1)} %get-tuple-element.62.refs_1_, ...), custom_call_target="tpu_custom_call" | custom-call | flops 1000000 | bytes 100000 | tf_op jit(solution)/shard_map/pallas_call | solution.py:33
  (11 shorter events, 0.0 us)
Async XLA Ops:
  0.6 1.1 %copy-start = (f32[2,8,3,4096]{3,1,2,0:T(8,128)S(1)}, f32[2,8,3,4096]{3,1,2,0:T(8,128)}, u32[]{:S(2)}) copy-start(f32[2,8,3,4096]{3,1,2,0:T(8,128)} %param.5) | copy-start | bytes 2359300
  0.6 1.1 %copy-start.1 = (f32[32,512]{1,0:T(8,128)S(1)}, f32[32,512]{1,0:T(8,128)}, u32[]{:S(2)}) copy-start(f32[32,512]{1,0:T(8,128)} %main.1) | copy-start | bytes 196612
  0.7 1.1 %copy-start.3 = (s32[2,8,3]{1,0,2:T(2,128)S(1)}, s32[2,8,3]{1,0,2:T(2,128)}, u32[]{:S(2)}) copy-start(s32[2,8,3]{1,0,2:T(2,128)} %param.6) | copy-start | bytes 580
  1.8 5.9 %copy-start.2 = (f32[2,4,8,8]{3,2,1,0:T(8,128)S(1)}, f32[2,4,8,8]{3,2,1,0:T(8,128)}, u32[]{:S(2)}) copy-start(f32[2,4,8,8]{3,2,1,0:T(8,128)} %mixing) | copy-start | bytes 6148
  1.9 6.3 %collective-permute-start = (f32[128,128]{1,0:T(8,128)S(1)}, f32[128,128]{1,0:T(8,128)S(1)}, u32[]{:S(2)}, u32[]{:S(2)}) collective-permute-start(f32[128,128]{1,0:T(8,128)S(1)} %get-tuple-element.34), channel_id=1, source_target_pairs={{0,0},{1,2},{2,1},{3,4},{4,3},{5,6},{6,5},{7,8},{8,7},{9,10},{10,9... | collective-permute-start | bytes 196616 | tf_op jit(solution)/shard_map/ppermute | solution.py:452
  2.6 5.8 %collective-permute-start.1 = (f32[864,128]{1,0:T(8,128)S(1)}, f32[864,128]{1,0:T(8,128)S(1)}, u32[]{:S(2)}, u32[]{:S(2)}) collective-permute-start(f32[864,128]{1,0:T(8,128)S(1)} %get-tuple-element.35), channel_id=1, source_target_pairs={{0,1},{1,0},{2,3},{3,2},{4,5},{5,4},{6,7},{7,6},{8,9},{9,8},{10,11... | collective-permute-start | bytes 1327112 | tf_op jit(solution)/shard_map/ppermute | solution.py:452
  7.0 6.3 %collective-permute-start.3 = (f32[480,128]{1,0:T(8,128)S(1)}, f32[480,128]{1,0:T(8,128)S(1)}, u32[]{:S(2)}, u32[]{:S(2)}) collective-permute-start(f32[480,128]{1,0:T(8,128)S(1)} %get-tuple-element.37), channel_id=1, source_target_pairs={{16,16},{17,18},{18,17},{19,20},{20,19},{21,22},{22,21},{23,24},{2... | collective-permute-start | bytes 737288 | tf_op jit(solution)/shard_map/ppermute | solution.py:452
  9.0 4.3 %collective-permute-start.2 = (f32[32,256]{1,0:T(8,128)S(1)}, f32[32,256]{1,0:T(8,128)S(1)}, u32[]{:S(2)}, u32[]{:S(2)}) collective-permute-start(f32[32,256]{1,0:T(8,128)S(1)} %get-tuple-element.45), channel_id=1, source_target_pairs={{0,16},{1,18},{2,17},{3,20},{4,19},{5,22},{6,21},{7,24},{8,23},{9,... | collective-permute-start | bytes 98312 | tf_op jit(solution)/shard_map/ppermute | solution.py:456
  9.1 6.2 %collective-permute-start.4 = (f32[32,512]{1,0:T(8,128)S(1)}, f32[32,512]{1,0:T(8,128)S(1)}, u32[]{:S(2)}, u32[]{:S(2)}) collective-permute-start(f32[32,512]{1,0:T(8,128)S(1)} %get-tuple-element.47.u.refs_0_), channel_id=1, source_target_pairs={{0,16},{1,17},{2,18},{3,19},{4,20},{5,21},{6,22},{7,23},{8,24},{9,... | collective-permute-start | bytes 196616 | tf_op jit(solution)/shard_map/ppermute | solution.py:456
  11.1 4.2 %collective-permute-start.5 = (f32[32,384]{1,0:T(8,128)S(1)}, f32[32,384]{1,0:T(8,128)S(1)}, u32[]{:S(2)}, u32[]{:S(2)}) collective-permute-start(f32[32,384]{1,0:T(8,128)S(1)} %get-tuple-element.48), channel_id=1, source_target_pairs={{0,17},{1,16},{2,19},{3,18},{4,21},{5,20},{6,23},{7,22},{8,25},{9,... | collective-permute-start | bytes 147464 | tf_op jit(solution)/shard_map/ppermute | solution.py:456
  12.4 6.5 %collective-permute-start.8 = (f32[96,128]{1,0:T(8,128)S(1)}, f32[96,128]{1,0:T(8,128)S(1)}, u32[]{:S(2)}, u32[]{:S(2)}) collective-permute-start(f32[96,128]{1,0:T(8,128)S(1)} %get-tuple-element.55), channel_id=1, source_target_pairs={{0,0},{1,2},{2,1},{3,4},{4,3},{5,6},{6,5},{7,8},{8,7},{9,10},{10,9... | collective-permute-start | bytes 147464 | tf_op jit(solution)/shard_map/ppermute | solution.py:452
  15.3 7.3 %collective-permute-start.7 = (f32[176,128]{1,0:T(8,128)S(1)}, f32[176,128]{1,0:T(8,128)S(1)}, u32[]{:S(2)}, u32[]{:S(2)}) collective-permute-start(f32[176,128]{1,0:T(8,128)S(1)} %get-tuple-element.54.refs_2_), channel_id=1, source_target_pairs={{16,0},{17,1},{18,2},{19,3},{20,4},{21,5},{22,6},{23,7},{24,8},{25... | collective-permute-start | bytes 270344 | tf_op jit(solution)/shard_map/ppermute | solution.py:456
  18.8 3.7 %collective-permute-start.6 = (f32[32,128]{1,0:T(8,128)S(1)}, f32[32,128]{1,0:T(8,128)S(1)}, u32[]{:S(2)}, u32[]{:S(2)}) collective-permute-start(f32[32,128]{1,0:T(8,128)S(1)} %get-tuple-element.53), channel_id=1, source_target_pairs={{16,0},{17,2},{18,1},{19,4},{20,3},{21,6},{22,5},{23,8},{24,7},{25... | collective-permute-start | bytes 49160 | tf_op jit(solution)/shard_map/ppermute | solution.py:456

commit v7 on v6

--- a/solution.py
+++ b/solution.py
@@ -127,6 +127,13 @@
     return high, (x - high.astype(F32)).astype(BF)
 
 
+def split3(x):
+    first = x.astype(BF)
+    x = x - first.astype(F32)
+    second = x.astype(BF)
+    return first, second, (x - second.astype(F32)).astype(BF)
+
+
 def split_halves(wide, at, hi, lo):
     for half in range(2):
         lanes = slice(half * 128, half * 128 + 128)
@@ -220,13 +227,23 @@
     return jnp.concatenate([row(b), row(b + 1)], axis=0)
 
 
+def pieces_sum(o, m, n, skip=0):
+    rows, cols = o.shape[0] // m, o.shape[1] // n
+    order = sorted(((i, j) for i in range(rows) for j in range(cols)), key=lambda p: -sum(p))
+    total = None
+    for i, j in order[skip:]:
+        piece = o[i * m : (i + 1) * m, j * n : (j + 1) * n]
+        total = piece if total is None else total + piece
+    return total
+
+
 def product(x, w, dims):
     o = lax.dot_general(x, w, dims, preferred_element_type=F32)
-    return (o[ROWS:, 128:] + o[ROWS:, :128] + o[:ROWS, 128:]) + o[:ROWS, :128]
+    return pieces_sum(o, ROWS, 128)
 
 
 def push(v, tiles):
-    x = jnp.concatenate(split2(v), axis=0)
+    x = jnp.concatenate(split3(v), axis=0)
     outs = []
     for i, (hi, lo) in enumerate(tiles):
         outs.append(product(x[:, i * 128 : i * 128 + 256], jnp.concatenate([hi, lo], axis=0), NT))
@@ -234,7 +251,7 @@
 
 
 def pull(v, tiles):
-    x = jnp.concatenate(split2(v), axis=0)
+    x = jnp.concatenate(split3(v), axis=0)
     outs = []
     for i in range(len(tiles) - 1):
         parts = [
@@ -253,14 +270,11 @@
 
 
 def gram(u):
-    high, low = split2(u)
-    o = lax.dot_general(
-        jnp.concatenate([low, high], axis=0),
-        jnp.concatenate([low] * 4 + [high] * 4, axis=0),
-        NT,
-        preferred_element_type=F32,
-    )
-    total = (o[:ROWS, :128] + o[:ROWS, 128:] + o[ROWS:, :128]) + o[ROWS:, 128:]
+    first = lax.rem(iota(u.shape, 0), COLS) == 0
+    parts = split3(u - jnp.where(first, 0.0, pltpu.roll(u, 1, 0)))
+    wide = jnp.concatenate([x for x in parts for _ in range(4)], axis=0)
+    o = lax.dot_general(jnp.concatenate(parts, axis=0), wide, NT, preferred_element_type=F32)
+    total = pieces_sum(o, ROWS, 128)
     panel = lax.rem(iota((COLS, 128), 1), ROWS) // COLS
     out = jnp.zeros((COLS, 128), F32)
     for p in range(PANELS):
@@ -377,10 +391,9 @@
     if m > rows:
         x = jnp.concatenate([x, jnp.zeros((m - rows, x.shape[1]), F32)], axis=0)
     o = lax.dot_general(
-        jnp.concatenate(split2(x), axis=0), jnp.concatenate(split2(y), axis=1), NN, preferred_element_type=F32
+        jnp.concatenate(split3(x), axis=0), jnp.concatenate(split3(y), axis=1), NN, preferred_element_type=F32
     )
-    o = (o[m:, 128:] + o[m:, :128] + o[:m, 128:]) + o[:m, :128]
-    return o[:rows]
+    return pieces_sum(o, m, 128, 3)[:rows]
 
 
 def scale_kernel(stages, boxes, grams, meta, *refs):
@@ -408,16 +421,20 @@
 
     count = len(stages)
     grow = [spread(growth, n) for n in range(count)]
+    sums = [grow[0][COLS - 1 :]]
+    for i in range(COLS - 2, -1, -1):
+        sums.insert(0, sums[0] + grow[0][i : i + 1])
+    sums = jnp.concatenate(sums, axis=0)
     products = jnp.concatenate([spread(total, n)[:, :ROWS] for n in range(count)], axis=0)
-    stack = jnp.concatenate([grow[0], exact(products, full(grow[0]))], axis=0)
+    stack = jnp.concatenate([grow[0], sums, exact(products, full(sums))], axis=0)
     select = {True: None, False: None}
     for n, (owner, forward) in enumerate(stages):
         if n:
             stack = exact(stack[:, :ROWS], full(grow[n]))
-        square = jnp.sum(stack[:COLS] * stack[COLS : 2 * COLS], axis=0, keepdims=True)
+        square = jnp.sum(stack[COLS : 2 * COLS] * stack[2 * COLS : 3 * COLS], axis=0, keepdims=True)
         scale = lax.rsqrt(jnp.maximum(square, 0.0) + 1e-06)
-        later = [stack[2 * COLS :]] if n + 1 < count else []
-        stack = jnp.concatenate([stack[:COLS]] + later, axis=0) * scale
+        later = [stack[3 * COLS :]] if n + 1 < count else []
+        stack = jnp.concatenate([stack[: 2 * COLS]] + later, axis=0) * scale
         back, u = stack[:COLS], panels_of(panels[n], own)
         old = select[forward]
         select[forward] = (back, u) if old is None else (
@@ -428,9 +445,9 @@
             out[...] = jnp.zeros_like(out)
         else:
             back, u = select[forward]
-            left = jnp.concatenate(split2(full(back)[:, :ROWS].T), axis=0)
-            o = lax.dot_general(left, jnp.concatenate(split2(u), axis=1), NN, preferred_element_type=F32)
-            out[...] = (o[ROWS:, own:] + o[ROWS:, :own] + o[:ROWS, own:]) + o[:ROWS, :own]
+            left = jnp.concatenate(split3(full(back)[:, :ROWS].T), axis=0)
+            o = lax.dot_general(left, jnp.concatenate(split3(u), axis=1), NN, preferred_element_type=F32)
+            out[...] = pieces_sum(o, ROWS, own, 3)
 
 
 def shards(panels_in, blocks, block_mask, mixing):

time: 37.7 us -> 38 us (level)
  no operation moved by 1% of the time
where the time goes in v7:
time: 38 us; the launch traced here: 37.7 us
  starting transfers between devices  13.5 us (36%)
  blocking collectives  12.7 us (33%)
  waiting for transfers between devices  5.51 us (14%)
  Pallas kernels  4.11 us (11%)
  local copies, waits for them, and re-layouts  1.12 us (3%)
  between operations  0.83 us (2%)
    all_to_all x1, blocking collectives, shards(): grams = lax.all_to_all(every, 'space', 0, 0)  12.7 us
    ppermute x5, starting transfers between devices, hop(): lax.ppermute(x, ('tm', 'space'), [(i * count + s, k * count + to(s)) for...  7.08 us
    ppermute x4, starting transfers between devices, beside(): return lax.ppermute(x, ('tm', 'space'), route)  6.37 us
    ppermute x5, waiting for transfers between devices, hop(): lax.ppermute(x, ('tm', 'space'), [(i * count + s, k * count + to(s)) for...  5.31 us
    pallas_call x13, Pallas kernels, call(): pl.pallas_call(kernel, out_shape=shapes, in_specs=[pl.BlockSpec(memory_sp...  4.11 us
    unnamed x8, local copies, waits for them, and re-layouts  1.11 us
  transfers between devices with their start and end apart: 9, of which 3 were waited for; matrix products, arithmetic and copies ran while one was open for 0% of the time, Pallas kernels for 4%

profile of v7, /device:TPU:0, one launch (start us, length us, event | category | flops | bytes accessed | tf_op | source)
XLA Modules:
  0.0 37.7 jit_solution(3392544296902274470)
XLA Ops:
  0.6 0.0 copy-start
  0.6 0.0 copy-start.1
  0.7 0.0 copy-start.3
  0.7 1.1 %copy-done = f32[2,8,3,4096]{3,1,2,0:T(8,128)S(1)} copy-done((f32[2,8,3,4096]{3,1,2,0:T(8,128)S(1)}, f32[2,8,3,4096]{3,1,2,0:T(8,128)}, u32[]{:S(2)}) %copy-start) | copy-done | bytes 786456
  1.8 0.0 copy-done.1
  1.8 0.0 copy-done.3
  1.8 0.0 copy-start.2
  1.8 0.1 shard_map.60
  1.9 0.7 %collective-permute-start = (f32[128,128]{1,0:T(8,128)S(1)}, f32[128,128]{1,0:T(8,128)S(1)}, u32[]{:S(2)}, u32[]{:S(2)}) collective-permute-start(f32[128,128]{1,0:T(8,128)S(1)} %get-tuple-element.34), channel_id=1, source_target_pairs={{0,0},{1,2},{2,1},{3,4},{4,3},{5,6},{6,5},{7,8},{8,7},{9,10},{10,9... | collective-permute-start | bytes 196616 | tf_op jit(solution)/shard_map/ppermute | solution.py:469
  2.6 4.4 %collective-permute-start.1 = (f32[864,128]{1,0:T(8,128)S(1)}, f32[864,128]{1,0:T(8,128)S(1)}, u32[]{:S(2)}, u32[]{:S(2)}) collective-permute-start(f32[864,128]{1,0:T(8,128)S(1)} %get-tuple-element.35), channel_id=1, source_target_pairs={{0,1},{1,0},{2,3},{3,2},{4,5},{5,4},{6,7},{7,6},{8,9},{9,8},{10,11... | collective-permute-start | bytes 1327112 | tf_op jit(solution)/shard_map/ppermute | solution.py:469
  7.0 0.7 %collective-permute-start.3 = (f32[480,128]{1,0:T(8,128)S(1)}, f32[480,128]{1,0:T(8,128)S(1)}, u32[]{:S(2)}, u32[]{:S(2)}) collective-permute-start(f32[480,128]{1,0:T(8,128)S(1)} %get-tuple-element.37), channel_id=1, source_target_pairs={{16,16},{17,18},{18,17},{19,20},{20,19},{21,22},{22,21},{23,24},{2... | collective-permute-start | bytes 737288 | tf_op jit(solution)/shard_map/ppermute | solution.py:469
  7.7 0.0 copy-done.2
  7.7 0.5 %shard_map.62 = (bf16[512,256]{1,0:T(8,128)(2,1)S(1)}, bf16[512,256]{1,0:T(8,128)(2,1)S(1)}, bf16[512,256]{1,0:T(8,128)(2,1)S(1)}, bf16[512,256]{1,0:T(8,128)(2,1)S(1)}, f32[16,128]{1,0:T(8,128)S(1)}) custom-call(f32[2,3,256,128]{3,2,1,0:T(8,128)S(1)} %bitcast.9, s32[3,2,8]{2,1,0:T(2,128)S(1)} %bitcast.11, f32[2,4,8,8]{3,2,1,0:T(8,128)S(1)} %copy-done.2), custom_call_target="tpu_custom_call" | custom-call | flops 1000000 | bytes 100000 | tf_op jit(solution)/shard_map/pallas_call | solution.py:33
  8.2 0.0 collective-permute-done.edge
  8.2 0.2 collective-permute-done.1.near_a.far_a
  8.4 0.6 %shard_map.63 = (f32[32,512]{1,0:T(8,128)S(1)}, f32[32,256]{1,0:T(8,128)S(1)}, f32[32,384]{1,0:T(8,128)S(1)}) custom-call(f32[32,128]{1,0:T(8,128)S(1)} %slice.20.edge_b, f32[32,512]{1,0:T(8,128)S(1)} %copy-done.1, f32[32,128]{1,0:T(8,128)S(1)} %slice.21.edge_a, f32[128,128]{1,0:T(8,128)S(1)} %shard_map.61.near_b, ...), custom_call_target="tpu_custom_call" | custom-call | flops 3000000000 | bytes 100000 | tf_op jit(solution)/shard_map/pallas_call | solution.py:33
  9.0 0.1 collective-permute-start.2
  9.1 2.0 %collective-permute-start.4 = (f32[32,512]{1,0:T(8,128)S(1)}, f32[32,512]{1,0:T(8,128)S(1)}, u32[]{:S(2)}, u32[]{:S(2)}) collective-permute-start(f32[32,512]{1,0:T(8,128)S(1)} %get-tuple-element.47.u.refs_0_), channel_id=1, source_target_pairs={{0,16},{1,17},{2,18},{3,19},{4,20},{5,21},{6,22},{7,23},{8,24},{9,... | collective-permute-start | bytes 196616 | tf_op jit(solution)/shard_map/ppermute | solution.py:473
  11.1 1.3 %collective-permute-start.5 = (f32[32,384]{1,0:T(8,128)S(1)}, f32[32,384]{1,0:T(8,128)S(1)}, u32[]{:S(2)}, u32[]{:S(2)}) collective-permute-start(f32[32,384]{1,0:T(8,128)S(1)} %get-tuple-element.48), channel_id=1, source_target_pairs={{0,17},{1,16},{2,19},{3,18},{4,21},{5,20},{6,23},{7,22},{8,25},{9,... | collective-permute-start | bytes 147464 | tf_op jit(solution)/shard_map/ppermute | solution.py:473
  12.4 0.7 %collective-permute-start.8 = (f32[96,128]{1,0:T(8,128)S(1)}, f32[96,128]{1,0:T(8,128)S(1)}, u32[]{:S(2)}, u32[]{:S(2)}) collective-permute-start(f32[96,128]{1,0:T(8,128)S(1)} %get-tuple-element.55), channel_id=1, source_target_pairs={{0,0},{1,2},{2,1},{3,4},{4,3},{5,6},{6,5},{7,8},{8,7},{9,10},{10,9... | collective-permute-start | bytes 147464 | tf_op jit(solution)/shard_map/ppermute | solution.py:469
  13.1 0.3 shard_map.66.old
  13.4 0.0 collective-permute-done.3.far_b
  13.4 0.0 collective-permute-done.2.edge
  13.4 1.8 %collective-permute-done.5.edge_a = f32[32,384]{1,0:T(8,128)S(1)} collective-permute-done((f32[32,384]{1,0:T(8,128)S(1)}, f32[32,384]{1,0:T(8,128)S(1)}, u32[]{:S(2)}, u32[]{:S(2)}) %collective-permute-start.5) | collective-permute-done | bytes 49184 | tf_op jit(solution)/shard_map/ppermute | solution.py:473
  15.3 0.0 collective-permute-done.4.main
  15.3 3.6 %collective-permute-start.7 = (f32[176,128]{1,0:T(8,128)S(1)}, f32[176,128]{1,0:T(8,128)S(1)}, u32[]{:S(2)}, u32[]{:S(2)}) collective-permute-start(f32[176,128]{1,0:T(8,128)S(1)} %get-tuple-element.54.refs_2_), channel_id=1, source_target_pairs={{16,0},{17,1},{18,2},{19,3},{20,4},{21,5},{22,6},{23,7},{24,8},{25... | collective-permute-start | bytes 270344 | tf_op jit(solution)/shard_map/ppermute | solution.py:473
  18.9 0.1 collective-permute-start.6
  19.0 0.0 collective-permute-done.8.late_b
  19.0 0.2 shard_map.69
  19.2 3.5 %collective-permute-done.6.edge = f32[32,128]{1,0:T(8,128)S(1)} collective-permute-done((f32[32,128]{1,0:T(8,128)S(1)}, f32[32,128]{1,0:T(8,128)S(1)}, u32[]{:S(2)}, u32[]{:S(2)}) %collective-permute-start.6) | collective-permute-done | bytes 16416 | tf_op jit(solution)/shard_map/ppermute | solution.py:473
  22.6 0.0 collective-permute-done.7.main
  22.7 0.7 %shard_map.70 = (f32[32,512]{1,0:T(8,128)S(1)}, f32[16,128]{1,0:T(8,128)S(1)}, f32[16,8,128]{2,1,0:T(8,128)S(1)}) custom-call(f32[32,128]{1,0:T(8,128)S(1)} %shard_map.68.edge_b, f32[176,128]{1,0:T(8,128)S(1)} %collective-permute-done.7.main, f32[32,128]{1,0:T(8,128)S(1)} %slice.22.edge_a, bf16[512,256]{1,0:T(8,128)(2,1)S(1)} %get-tuple-element.41.a_hi, ...), custom_call_target="tpu_custom_call" | custom-call | flops 1000000 | bytes 100000 | tf_op jit(solution)/shard_map/pallas_call | solution.py:33
  23.4 12.7 %all_to_all.5.grams = f32[16,8,128]{2,1,0:T(8,128)S(1)} all-to-all(f32[16,8,128]{2,1,0:T(8,128)S(1)} %get-tuple-element.60), channel_id=1, replica_groups=mesh['tm'=2,'space'=16] {'space'}, dimensions={0} | all-to-all | bytes 131072 | tf_op jit(solution)/shard_map/all_to_all | solution.py:569
  36.1 1.6 %shard_map.71 = (f32[32,512]{1,0:T(8,128)}, f32[32,512]{1,0:T(8,128)}) custom-call(f32[16,8,128]{2,1,0:T(8,128)S(1)} %all_to_all.5.grams, f32[16,128]{1,0:T(8,128)S(1)} %get-tuple-element.61.meta, f32[32,512]{1,0:T(8,128)S(1)} %get-tuple-element.47.u.refs_0_, f32[32,512]{1,0:T(8,128)S(1)} %get-tuple-element.62.refs_1_, ...), custom_call_target="tpu_custom_call" | custom-call | flops 1000000 | bytes 100000 | tf_op jit(solution)/shard_map/pallas_call | solution.py:33
  (11 shorter events, 0.0 us)
Async XLA Ops:
  0.6 1.1 %copy-start = (f32[2,8,3,4096]{3,1,2,0:T(8,128)S(1)}, f32[2,8,3,4096]{3,1,2,0:T(8,128)}, u32[]{:S(2)}) copy-start(f32[2,8,3,4096]{3,1,2,0:T(8,128)} %param.5) | copy-start | bytes 2359300
  0.6 1.1 %copy-start.1 = (f32[32,512]{1,0:T(8,128)S(1)}, f32[32,512]{1,0:T(8,128)}, u32[]{:S(2)}) copy-start(f32[32,512]{1,0:T(8,128)} %main.1) | copy-start | bytes 196612
  0.7 1.1 %copy-start.3 = (s32[2,8,3]{1,0,2:T(2,128)S(1)}, s32[2,8,3]{1,0,2:T(2,128)}, u32[]{:S(2)}) copy-start(s32[2,8,3]{1,0,2:T(2,128)} %param.6) | copy-start | bytes 580
  1.8 5.9 %copy-start.2 = (f32[2,4,8,8]{3,2,1,0:T(8,128)S(1)}, f32[2,4,8,8]{3,2,1,0:T(8,128)}, u32[]{:S(2)}) copy-start(f32[2,4,8,8]{3,2,1,0:T(8,128)} %mixing) | copy-start | bytes 6148
  1.9 6.3 %collective-permute-start = (f32[128,128]{1,0:T(8,128)S(1)}, f32[128,128]{1,0:T(8,128)S(1)}, u32[]{:S(2)}, u32[]{:S(2)}) collective-permute-start(f32[128,128]{1,0:T(8,128)S(1)} %get-tuple-element.34), channel_id=1, source_target_pairs={{0,0},{1,2},{2,1},{3,4},{4,3},{5,6},{6,5},{7,8},{8,7},{9,10},{10,9... | collective-permute-start | bytes 196616 | tf_op jit(solution)/shard_map/ppermute | solution.py:469
  2.6 5.8 %collective-permute-start.1 = (f32[864,128]{1,0:T(8,128)S(1)}, f32[864,128]{1,0:T(8,128)S(1)}, u32[]{:S(2)}, u32[]{:S(2)}) collective-permute-start(f32[864,128]{1,0:T(8,128)S(1)} %get-tuple-element.35), channel_id=1, source_target_pairs={{0,1},{1,0},{2,3},{3,2},{4,5},{5,4},{6,7},{7,6},{8,9},{9,8},{10,11... | collective-permute-start | bytes 1327112 | tf_op jit(solution)/shard_map/ppermute | solution.py:469
  7.0 6.4 %collective-permute-start.3 = (f32[480,128]{1,0:T(8,128)S(1)}, f32[480,128]{1,0:T(8,128)S(1)}, u32[]{:S(2)}, u32[]{:S(2)}) collective-permute-start(f32[480,128]{1,0:T(8,128)S(1)} %get-tuple-element.37), channel_id=1, source_target_pairs={{16,16},{17,18},{18,17},{19,20},{20,19},{21,22},{22,21},{23,24},{2... | collective-permute-start | bytes 737288 | tf_op jit(solution)/shard_map/ppermute | solution.py:469
  9.0 4.4 %collective-permute-start.2 = (f32[32,256]{1,0:T(8,128)S(1)}, f32[32,256]{1,0:T(8,128)S(1)}, u32[]{:S(2)}, u32[]{:S(2)}) collective-permute-start(f32[32,256]{1,0:T(8,128)S(1)} %get-tuple-element.45), channel_id=1, source_target_pairs={{0,16},{1,18},{2,17},{3,20},{4,19},{5,22},{6,21},{7,24},{8,23},{9,... | collective-permute-start | bytes 98312 | tf_op jit(solution)/shard_map/ppermute | solution.py:473
  9.1 6.2 %collective-permute-start.4 = (f32[32,512]{1,0:T(8,128)S(1)}, f32[32,512]{1,0:T(8,128)S(1)}, u32[]{:S(2)}, u32[]{:S(2)}) collective-permute-start(f32[32,512]{1,0:T(8,128)S(1)} %get-tuple-element.47.u.refs_0_), channel_id=1, source_target_pairs={{0,16},{1,17},{2,18},{3,19},{4,20},{5,21},{6,22},{7,23},{8,24},{9,... | collective-permute-start | bytes 196616 | tf_op jit(solution)/shard_map/ppermute | solution.py:473
  11.1 4.2 %collective-permute-start.5 = (f32[32,384]{1,0:T(8,128)S(1)}, f32[32,384]{1,0:T(8,128)S(1)}, u32[]{:S(2)}, u32[]{:S(2)}) collective-permute-start(f32[32,384]{1,0:T(8,128)S(1)} %get-tuple-element.48), channel_id=1, source_target_pairs={{0,17},{1,16},{2,19},{3,18},{4,21},{5,20},{6,23},{7,22},{8,25},{9,... | collective-permute-start | bytes 147464 | tf_op jit(solution)/shard_map/ppermute | solution.py:473
  12.4 6.6 %collective-permute-start.8 = (f32[96,128]{1,0:T(8,128)S(1)}, f32[96,128]{1,0:T(8,128)S(1)}, u32[]{:S(2)}, u32[]{:S(2)}) collective-permute-start(f32[96,128]{1,0:T(8,128)S(1)} %get-tuple-element.55), channel_id=1, source_target_pairs={{0,0},{1,2},{2,1},{3,4},{4,3},{5,6},{6,5},{7,8},{8,7},{9,10},{10,9... | collective-permute-start | bytes 147464 | tf_op jit(solution)/shard_map/ppermute | solution.py:469
  15.3 7.4 %collective-permute-start.7 = (f32[176,128]{1,0:T(8,128)S(1)}, f32[176,128]{1,0:T(8,128)S(1)}, u32[]{:S(2)}, u32[]{:S(2)}) collective-permute-start(f32[176,128]{1,0:T(8,128)S(1)} %get-tuple-element.54.refs_2_), channel_id=1, source_target_pairs={{16,0},{17,1},{18,2},{19,3},{20,4},{21,5},{22,6},{23,7},{24,8},{25... | collective-permute-start | bytes 270344 | tf_op jit(solution)/shard_map/ppermute | solution.py:473
  18.9 3.7 %collective-permute-start.6 = (f32[32,128]{1,0:T(8,128)S(1)}, f32[32,128]{1,0:T(8,128)S(1)}, u32[]{:S(2)}, u32[]{:S(2)}) collective-permute-start(f32[32,128]{1,0:T(8,128)S(1)} %get-tuple-element.53), channel_id=1, source_target_pairs={{16,0},{17,2},{18,1},{19,4},{20,3},{21,6},{22,5},{23,8},{24,7},{25... | collective-permute-start | bytes 49160 | tf_op jit(solution)/shard_map/ppermute | solution.py:473

commit v8 on v7

--- a/solution.py
+++ b/solution.py
@@ -74,20 +74,44 @@
     return blocks[t, j, pl.ds(b, BLOCK // 2, stride=nb), :] * column[t][j][b : b + 1, :]
 
 
-def edge_kernel(nb, turning, _, blocks, mask, panels, near_b, late_b, to_a, *far_b):
+def edge_kernel(nb, turning, _, blocks, mask, panels, to_b, late_b, to_a, *refs):
     width = panels.shape[1]
+    far_b, tile = refs[:-1], refs[-1]
     turns = lax.axis_index("tm") == turning
     column = [[presence(mask, t, j, nb) for j in range(3)] for t in range(RUN)]
 
-    def near(dst, later, at, low_side, keep=1.0):
+    def near_a(dst, low_side):
+        edge = 0 if low_side else nb - 1
+        for j in range(3):
+            dst[j * 32 : (j + 1) * 32, :] = block_of(blocks, column, 0, j, edge, nb)
+        dst[96:128, :] = panels[:, :128] if low_side else panels[:, width - 128 :]
+        later(dst, 128, low_side, False, 1.0)
+
+    def near_b(dst, rest, low_side):
+        keep = inside()
+        edge = 0 if low_side else nb - 1
+        y = [block_of(blocks, column, 0, j, edge, nb) for j in range(3)]
+        dst[:32, :] = (y[0] if low_side else y[2]) * keep
+        for p in range(2):
+            first, second = banded(y, p)
+            tile[pl.ds(p, 32, stride=2), :] = second[1] if low_side else first[0]
+        group = panels[:, :128] if low_side else panels[:, width - 128 :]
+        x, w = jnp.concatenate(split3(group), axis=0), jnp.concatenate(split2(tile[...]), axis=0)
+        o = lax.dot_general(x, w, NT, preferred_element_type=F32)
+        o = (o[2 * ROWS :] + o[ROWS : 2 * ROWS]) + o[:ROWS]
+        share = (o + pltpu.roll(o, BLOCK, 1)) * keep
+        low = iota((ROWS, 128), 1) < BLOCK
+        dst[32:64, :] = jnp.where(low, group, share) if low_side else jnp.where(low, share, group)
+        later(rest, 0, low_side, rest.shape[0] > 96, keep)
+
+    def later(dst, at, low_side, more, keep):
         edge = 0 if low_side else nb - 1
         inner = 1 if low_side else nb - 2
-        for j in range(3):
-            dst[j * 32 : (j + 1) * 32, :] = block_of(blocks, column, 0, j, edge, nb) * keep
-        dst[96:128, :] = panels[:, :128] if low_side else panels[:, width - 128 :]
-        rest = [(edge, 0), (edge, 1), (inner, 0)] if low_side else [(inner, 2), (edge, 1), (edge, 2)]
-        for i, (b, j) in enumerate(rest):
-            later[at + i * 32 : at + (i + 1) * 32, :] = block_of(blocks, column, 1, j, b, nb) * keep
+        rest = [(1, edge, 0), (1, edge, 1), (1, inner, 0)] if low_side else [(1, inner, 2), (1, edge, 1), (1, edge, 2)]
+        if more:
+            rest += [(0, edge, 1), (0, edge, 2)] if low_side else [(0, edge, 0), (0, edge, 1)]
+        for i, (t, b, j) in enumerate(rest):
+            dst[at + i * 32 : at + (i + 1) * 32, :] = block_of(blocks, column, t, j, b, nb) * keep
 
     def far(dst, deep_a, deep_b, low_side, keep=1.0):
         at = 0
@@ -101,8 +125,8 @@
 
         @pl.when((parity() == side) & jnp.logical_not(turns))
         def _():
-            near(near_b, late_b, 0, side == 0, inside())
-            near(to_a, to_a, 128, side == 1)
+            near_b(to_b, late_b, side == 0)
+            near_a(to_a, side == 1)
 
         if far_b:
 
@@ -174,9 +198,14 @@
             dst[half, pl.ds(index * BLOCK + p, 32, stride=2), :] = tiles[half]
 
 
-def edge_rows(near_a, near_b, dst):
+def edge_rows(near_a, near_b, dst, rest=None):
+    even = parity() == 0
+    block, none = near_b[:32, :], jnp.zeros((32, 128), F32)
+    others = [none, none] if rest is None else [rest[96:128, :], rest[128:160, :]]
     for left in (True, False):
-        rim_row(dst, 1 - left, left, [taken(near_a, near_b, left, j * 32) for j in range(3)])
+        from_b = others + [block] if left else [block] + others
+        y = [jnp.where(even == left, from_b[j], near_a[j * 32 : (j + 1) * 32, :]) for j in range(3)]
+        rim_row(dst, 1 - left, left, y)
 
 
 def rim_kernel(turning, far_b, far_a, a_hi, a_lo, b_hi, b_lo, wide_a, wide_b):
@@ -302,16 +331,22 @@
     refs[-1][...] = edge[...]
 
 
-def push_kernel(nb, owner, edge_b, main, edge_a, near_b, near_a, a_hi, a_lo, b_hi, b_lo, out, out_b, out_a, wide):
+def push_kernel(nb, owner, edge_b, main, edge_a, near_b, near_a, a_hi, a_lo, b_hi, b_lo, *refs):
     own = nb * BLOCK
+    *late, out, out_b, out_a, wide = refs
 
     @pl.when(lax.axis_index("tm") == owner)
     def _():
-        edge_rows(near_a, near_b, wide)
+        edge_rows(near_a, near_b, wide, *late)
         rim_hi, rim_lo = split2(jnp.concatenate([wide[0], wide[1]], axis=1))
         left, right = by_side(edge_a[...], edge_b[...])
         v = jnp.concatenate([left, main[:, :own], right], axis=1)
         w = push(v, tiles_of((a_hi, a_lo, rim_hi, rim_lo), 1, nb, -1, nb))
+        if not late:
+            low, even = iota((ROWS, 128), 1) < BLOCK, parity() == 0
+            at_left = jnp.where(low & even, edge_b[...], 0.0)
+            at_right = jnp.where(low | even, 0.0, edge_b[...])
+            w = jnp.concatenate([w[:, :128] + at_left, w[:, 128:own], w[:, own:] + at_right], axis=1)
         u = push(w, tiles_of((b_hi, b_lo, None, None), 0, nb, 0, nb))
         out[...] = u
         wide_b, wide_a = out_b.shape[1], out_a.shape[1]
@@ -484,11 +519,12 @@
     turn = owners % GROUP != 0
     turning = owners - 1 if turn else owners
     begin = call(first_kernel, [f32(8, 128)], (), flops=10**9)
-    sizes = [128, 96] + ([96 * (RIM_A + RIM_B), 96 * (FAR_A + FAR_B)] if turn else [224])
+    sizes = [64, 96 if owners == 2 else 160] + ([96 * (RIM_A + RIM_B), 96 * (FAR_A + FAR_B)] if turn else [224])
     edges = call(
         functools.partial(edge_kernel, nb, turning),
         [f32(n, 128) for n in sizes],
         (*begin, rows, mask, panels_in),
+        [vm(BLOCK, 128)],
     )
     near_b, near_a = beside(edges[0], partner_b, range(turning)), beside(edges[2], partner_a)
     (near_b,) = call(aside_kernel, [f32(*near_b.shape)], (near_b,), flops=ASIDE_0)
@@ -509,15 +545,16 @@
 
     def late_rims(after):
         late, _ = lax.optimization_barrier((edges[1], after))
-        args = (near_a, near_b, beside(late, partner_b, range(turning)))
-        return rim_call(functools.partial(pull_rim_kernel, turning), 1, 2, args)
+        late = beside(late, partner_b, range(turning))
+        args = (near_a, near_b, late)
+        return late, rim_call(functools.partial(pull_rim_kernel, turning), 1, 2, args)
 
     pull_rims = None
     if turn:
         turn_rims = rim_call(functools.partial(rim_kernel, turning), RIM_A, RIM_B, (far_b, near_a))
 
     meta = jnp.zeros((2 * COLS, 128), F32)
-    main, edge_a, edge_b = panels_in, near_a[96:128], near_b[96:128]
+    main, edge_a, edge_b = panels_in, near_a[96:128], near_b[32:64]
     stages = 2 * owners
     owner_of = [k if k < owners else stages - 1 - k for k in range(stages)]
     kept, result, k = [], None, 0
@@ -540,12 +577,12 @@
                 main, send_b, send_a = call(
                     functools.partial(push_kernel, nb, owner),
                     [f32(ROWS, own)] + [f32(ROWS, w) for w in ((256, 384) if turns_next else (128, 128))],
-                    (edge_b, main, edge_a, near_b, near_a, *own_tiles),
+                    (edge_b, main, edge_a, near_b, near_a, *own_tiles, *([late_b] if k else [])),
                     [vm(2, 2 * BLOCK, 128)],
                     flops=PUSH,
                 )
                 if pull_rims is None:
-                    pull_rims = late_rims(send_b)
+                    late_b, pull_rims = late_rims(send_b)
                 (meta,) = call(
                     functools.partial(note_kernel, nb, owner, slot),
                     [f32(2 * COLS, 128)],

time: 38 us -> 37.9 us (level)
  starting transfers between devices: 13.5 us -> 12.7 us
  waiting for transfers between devices: 5.51 us -> 6.26 us
    ppermute x5, waiting for transfers between devices: 5.31 us -> 6.05 us  [hop(): lax.ppermute(x, ('tm', 'space'), [(i * count + s, k * count + to(s)) for...]
    ppermute x5, starting transfers between devices: 7.08 us -> 6.34 us  [hop(): lax.ppermute(x, ('tm', 'space'), [(i * count + s, k * count + to(s)) for...]
where the time goes in v8:
time: 37.9 us; the launch traced here: 37.6 us
  starting transfers between devices  12.7 us (34%)
  blocking collectives  12.4 us (33%)
  waiting for transfers between devices  6.26 us (17%)
  Pallas kernels  4.37 us (12%)
  local copies, waits for them, and re-layouts  1.12 us (3%)
  between operations  0.82 us (2%)
    all_to_all x1, blocking collectives, shards(): grams = lax.all_to_all(every, 'space', 0, 0)  12.4 us
    ppermute x4, starting transfers between devices, beside(): return lax.ppermute(x, ('tm', 'space'), route)  6.36 us
    ppermute x5, starting transfers between devices, hop(): lax.ppermute(x, ('tm', 'space'), [(i * count + s, k * count + to(s)) for...  6.34 us
    ppermute x5, waiting for transfers between devices, hop(): lax.ppermute(x, ('tm', 'space'), [(i * count + s, k * count + to(s)) for...  6.05 us
    pallas_call x13, Pallas kernels, call(): pl.pallas_call(kernel, out_shape=shapes, in_specs=[pl.BlockSpec(memory_sp...  4.37 us
    unnamed x8, local copies, waits for them, and re-layouts  1.11 us
  transfers between devices with their start and end apart: 9, of which 3 were waited for; matrix products, arithmetic and copies ran while one was open for 0% of the time, Pallas kernels for 4%

profile of v8, /device:TPU:0, one launch (start us, length us, event | category | flops | bytes accessed | tf_op | source)
XLA Modules:
  0.0 37.6 jit_solution(9934125655689073920)
XLA Ops:
  0.6 0.0 copy-start
  0.6 0.0 copy-start.1
  0.7 0.0 copy-start.3
  0.7 1.1 %copy-done = f32[2,8,3,4096]{3,1,2,0:T(8,128)S(1)} copy-done((f32[2,8,3,4096]{3,1,2,0:T(8,128)S(1)}, f32[2,8,3,4096]{3,1,2,0:T(8,128)}, u32[]{:S(2)}) %copy-start) | copy-done | bytes 786456
  1.8 0.0 copy-done.1
  1.8 0.0 copy-done.3
  1.8 0.0 copy-start.2
  1.8 0.4 %shard_map.60 = (f32[64,128]{1,0:T(8,128)S(1)}, f32[96,128]{1,0:T(8,128)S(1)}, f32[864,128]{1,0:T(8,128)S(1)}, f32[480,128]{1,0:T(8,128)S(1)}) custom-call(f32[8,128]{1,0:T(8,128)S(1)} %shard_map.59._, f32[2,3,256,128]{3,2,1,0:T(8,128)S(1)} %bitcast.8, s32[3,2,8]{2,1,0:T(2,128)S(1)} %bitcast.10, f32[32,512]{1,0:T(8,128)S(1)} %copy-done.1), custom_call_target="tpu_custom_call" | custom-call | flops 1000000 | bytes 100000 | tf_op jit(solution)/shard_map/pallas_call | solution.py:33
  2.2 0.7 %collective-permute-start = (f32[64,128]{1,0:T(8,128)S(1)}, f32[64,128]{1,0:T(8,128)S(1)}, u32[]{:S(2)}, u32[]{:S(2)}) collective-permute-start(f32[64,128]{1,0:T(8,128)S(1)} %get-tuple-element.34), channel_id=1, source_target_pairs={{0,0},{1,2},{2,1},{3,4},{4,3},{5,6},{6,5},{7,8},{8,7},{9,10},{10,9... | collective-permute-start | bytes 98312 | tf_op jit(solution)/shard_map/ppermute | solution.py:504
  2.8 4.4 %collective-permute-start.1 = (f32[864,128]{1,0:T(8,128)S(1)}, f32[864,128]{1,0:T(8,128)S(1)}, u32[]{:S(2)}, u32[]{:S(2)}) collective-permute-start(f32[864,128]{1,0:T(8,128)S(1)} %get-tuple-element.35), channel_id=1, source_target_pairs={{0,1},{1,0},{2,3},{3,2},{4,5},{5,4},{6,7},{7,6},{8,9},{9,8},{10,11... | collective-permute-start | bytes 1327112 | tf_op jit(solution)/shard_map/ppermute | solution.py:504
  7.2 0.7 %collective-permute-start.3 = (f32[480,128]{1,0:T(8,128)S(1)}, f32[480,128]{1,0:T(8,128)S(1)}, u32[]{:S(2)}, u32[]{:S(2)}) collective-permute-start(f32[480,128]{1,0:T(8,128)S(1)} %get-tuple-element.37), channel_id=1, source_target_pairs={{16,16},{17,18},{18,17},{19,20},{20,19},{21,22},{22,21},{23,24},{2... | collective-permute-start | bytes 737288 | tf_op jit(solution)/shard_map/ppermute | solution.py:504
  7.9 0.0 copy-done.2
  7.9 0.5 %shard_map.62 = (bf16[512,256]{1,0:T(8,128)(2,1)S(1)}, bf16[512,256]{1,0:T(8,128)(2,1)S(1)}, bf16[512,256]{1,0:T(8,128)(2,1)S(1)}, bf16[512,256]{1,0:T(8,128)(2,1)S(1)}, f32[16,128]{1,0:T(8,128)S(1)}) custom-call(f32[2,3,256,128]{3,2,1,0:T(8,128)S(1)} %bitcast.9, s32[3,2,8]{2,1,0:T(2,128)S(1)} %bitcast.11, f32[2,4,8,8]{3,2,1,0:T(8,128)S(1)} %copy-done.2), custom_call_target="tpu_custom_call" | custom-call | flops 1000000 | bytes 100000 | tf_op jit(solution)/shard_map/pallas_call | solution.py:33
  8.4 0.0 collective-permute-done.edge
  8.5 0.2 collective-permute-done.1.near_a.far_a
  8.6 0.6 %shard_map.63 = (f32[32,512]{1,0:T(8,128)S(1)}, f32[32,256]{1,0:T(8,128)S(1)}, f32[32,384]{1,0:T(8,128)S(1)}) custom-call(f32[32,128]{1,0:T(8,128)S(1)} %slice.20.edge_b, f32[32,512]{1,0:T(8,128)S(1)} %copy-done.1, f32[32,128]{1,0:T(8,128)S(1)} %slice.21.edge_a, f32[64,128]{1,0:T(8,128)S(1)} %shard_map.61.near_b, ...), custom_call_target="tpu_custom_call" | custom-call | flops 3000000000 | bytes 100000 | tf_op jit(solution)/shard_map/pallas_call | solution.py:33
  9.3 0.1 collective-permute-start.2
  9.3 2.0 %collective-permute-start.4 = (f32[32,512]{1,0:T(8,128)S(1)}, f32[32,512]{1,0:T(8,128)S(1)}, u32[]{:S(2)}, u32[]{:S(2)}) collective-permute-start(f32[32,512]{1,0:T(8,128)S(1)} %get-tuple-element.47.u.refs_0_), channel_id=1, source_target_pairs={{0,16},{1,17},{2,18},{3,19},{4,20},{5,21},{6,22},{7,23},{8,24},{9,... | collective-permute-start | bytes 196616 | tf_op jit(solution)/shard_map/ppermute | solution.py:508
  11.3 0.9 %collective-permute-start.5 = (f32[32,384]{1,0:T(8,128)S(1)}, f32[32,384]{1,0:T(8,128)S(1)}, u32[]{:S(2)}, u32[]{:S(2)}) collective-permute-start(f32[32,384]{1,0:T(8,128)S(1)} %get-tuple-element.48), channel_id=1, source_target_pairs={{0,17},{1,16},{2,19},{3,18},{4,21},{5,20},{6,23},{7,22},{8,25},{9,... | collective-permute-start | bytes 147464 | tf_op jit(solution)/shard_map/ppermute | solution.py:508
  12.3 0.7 %collective-permute-start.8 = (f32[96,128]{1,0:T(8,128)S(1)}, f32[96,128]{1,0:T(8,128)S(1)}, u32[]{:S(2)}, u32[]{:S(2)}) collective-permute-start(f32[96,128]{1,0:T(8,128)S(1)} %get-tuple-element.55), channel_id=1, source_target_pairs={{0,0},{1,2},{2,1},{3,4},{4,3},{5,6},{6,5},{7,8},{8,7},{9,10},{10,9... | collective-permute-start | bytes 147464 | tf_op jit(solution)/shard_map/ppermute | solution.py:504
  13.0 0.3 shard_map.66.old
  13.3 0.0 collective-permute-done.3.far_b
  13.3 0.0 collective-permute-done.2.edge
  13.3 2.6 %collective-permute-done.5.edge_a = f32[32,384]{1,0:T(8,128)S(1)} collective-permute-done((f32[32,384]{1,0:T(8,128)S(1)}, f32[32,384]{1,0:T(8,128)S(1)}, u32[]{:S(2)}, u32[]{:S(2)}) %collective-permute-start.5) | collective-permute-done | bytes 49184 | tf_op jit(solution)/shard_map/ppermute | solution.py:508
  15.9 0.0 collective-permute-done.4.main
  15.9 3.2 %collective-permute-start.7 = (f32[176,128]{1,0:T(8,128)S(1)}, f32[176,128]{1,0:T(8,128)S(1)}, u32[]{:S(2)}, u32[]{:S(2)}) collective-permute-start(f32[176,128]{1,0:T(8,128)S(1)} %get-tuple-element.54.refs_2_), channel_id=1, source_target_pairs={{16,0},{17,1},{18,2},{19,3},{20,4},{21,5},{22,6},{23,7},{24,8},{25... | collective-permute-start | bytes 270344 | tf_op jit(solution)/shard_map/ppermute | solution.py:508
  19.1 0.1 collective-permute-start.6
  19.2 0.0 collective-permute-done.8.late_b
  19.2 0.2 shard_map.69
  19.4 3.5 %collective-permute-done.6.edge = f32[32,128]{1,0:T(8,128)S(1)} collective-permute-done((f32[32,128]{1,0:T(8,128)S(1)}, f32[32,128]{1,0:T(8,128)S(1)}, u32[]{:S(2)}, u32[]{:S(2)}) %collective-permute-start.6) | collective-permute-done | bytes 16416 | tf_op jit(solution)/shard_map/ppermute | solution.py:508
  22.9 0.0 collective-permute-done.7.main
  22.9 0.7 %shard_map.70 = (f32[32,512]{1,0:T(8,128)S(1)}, f32[16,128]{1,0:T(8,128)S(1)}, f32[16,8,128]{2,1,0:T(8,128)S(1)}) custom-call(f32[32,128]{1,0:T(8,128)S(1)} %shard_map.68.edge_b, f32[176,128]{1,0:T(8,128)S(1)} %collective-permute-done.7.main, f32[32,128]{1,0:T(8,128)S(1)} %slice.22.edge_a, bf16[512,256]{1,0:T(8,128)(2,1)S(1)} %get-tuple-element.41.a_hi, ...), custom_call_target="tpu_custom_call" | custom-call | flops 1000000 | bytes 100000 | tf_op jit(solution)/shard_map/pallas_call | solution.py:33
  23.6 12.4 %all_to_all.5.grams = f32[16,8,128]{2,1,0:T(8,128)S(1)} all-to-all(f32[16,8,128]{2,1,0:T(8,128)S(1)} %get-tuple-element.60), channel_id=1, replica_groups=mesh['tm'=2,'space'=16] {'space'}, dimensions={0} | all-to-all | bytes 131072 | tf_op jit(solution)/shard_map/all_to_all | solution.py:606
  36.0 1.6 %shard_map.71 = (f32[32,512]{1,0:T(8,128)}, f32[32,512]{1,0:T(8,128)}) custom-call(f32[16,8,128]{2,1,0:T(8,128)S(1)} %all_to_all.5.grams, f32[16,128]{1,0:T(8,128)S(1)} %get-tuple-element.61.meta, f32[32,512]{1,0:T(8,128)S(1)} %get-tuple-element.47.u.refs_0_, f32[32,512]{1,0:T(8,128)S(1)} %get-tuple-element.62.refs_1_, ...), custom_call_target="tpu_custom_call" | custom-call | flops 1000000 | bytes 100000 | tf_op jit(solution)/shard_map/pallas_call | solution.py:33
  (11 shorter events, 0.0 us)
Async XLA Ops:
  0.6 1.1 %copy-start = (f32[2,8,3,4096]{3,1,2,0:T(8,128)S(1)}, f32[2,8,3,4096]{3,1,2,0:T(8,128)}, u32[]{:S(2)}) copy-start(f32[2,8,3,4096]{3,1,2,0:T(8,128)} %param.5) | copy-start | bytes 2359300
  0.6 1.1 %copy-start.1 = (f32[32,512]{1,0:T(8,128)S(1)}, f32[32,512]{1,0:T(8,128)}, u32[]{:S(2)}) copy-start(f32[32,512]{1,0:T(8,128)} %main.1) | copy-start | bytes 196612
  0.7 1.1 %copy-start.3 = (s32[2,8,3]{1,0,2:T(2,128)S(1)}, s32[2,8,3]{1,0,2:T(2,128)}, u32[]{:S(2)}) copy-start(s32[2,8,3]{1,0,2:T(2,128)} %param.6) | copy-start | bytes 580
  1.8 6.1 %copy-start.2 = (f32[2,4,8,8]{3,2,1,0:T(8,128)S(1)}, f32[2,4,8,8]{3,2,1,0:T(8,128)}, u32[]{:S(2)}) copy-start(f32[2,4,8,8]{3,2,1,0:T(8,128)} %mixing) | copy-start | bytes 6148
  2.2 6.2 %collective-permute-start = (f32[64,128]{1,0:T(8,128)S(1)}, f32[64,128]{1,0:T(8,128)S(1)}, u32[]{:S(2)}, u32[]{:S(2)}) collective-permute-start(f32[64,128]{1,0:T(8,128)S(1)} %get-tuple-element.34), channel_id=1, source_target_pairs={{0,0},{1,2},{2,1},{3,4},{4,3},{5,6},{6,5},{7,8},{8,7},{9,10},{10,9... | collective-permute-start | bytes 98312 | tf_op jit(solution)/shard_map/ppermute | solution.py:504
  2.8 5.8 %collective-permute-start.1 = (f32[864,128]{1,0:T(8,128)S(1)}, f32[864,128]{1,0:T(8,128)S(1)}, u32[]{:S(2)}, u32[]{:S(2)}) collective-permute-start(f32[864,128]{1,0:T(8,128)S(1)} %get-tuple-element.35), channel_id=1, source_target_pairs={{0,1},{1,0},{2,3},{3,2},{4,5},{5,4},{6,7},{7,6},{8,9},{9,8},{10,11... | collective-permute-start | bytes 1327112 | tf_op jit(solution)/shard_map/ppermute | solution.py:504
  7.2 6.1 %collective-permute-start.3 = (f32[480,128]{1,0:T(8,128)S(1)}, f32[480,128]{1,0:T(8,128)S(1)}, u32[]{:S(2)}, u32[]{:S(2)}) collective-permute-start(f32[480,128]{1,0:T(8,128)S(1)} %get-tuple-element.37), channel_id=1, source_target_pairs={{16,16},{17,18},{18,17},{19,20},{20,19},{21,22},{22,21},{23,24},{2... | collective-permute-start | bytes 737288 | tf_op jit(solution)/shard_map/ppermute | solution.py:504
  9.3 4.1 %collective-permute-start.2 = (f32[32,256]{1,0:T(8,128)S(1)}, f32[32,256]{1,0:T(8,128)S(1)}, u32[]{:S(2)}, u32[]{:S(2)}) collective-permute-start(f32[32,256]{1,0:T(8,128)S(1)} %get-tuple-element.45), channel_id=1, source_target_pairs={{0,16},{1,18},{2,17},{3,20},{4,19},{5,22},{6,21},{7,24},{8,23},{9,... | collective-permute-start | bytes 98312 | tf_op jit(solution)/shard_map/ppermute | solution.py:508
  9.3 6.6 %collective-permute-start.4 = (f32[32,512]{1,0:T(8,128)S(1)}, f32[32,512]{1,0:T(8,128)S(1)}, u32[]{:S(2)}, u32[]{:S(2)}) collective-permute-start(f32[32,512]{1,0:T(8,128)S(1)} %get-tuple-element.47.u.refs_0_), channel_id=1, source_target_pairs={{0,16},{1,17},{2,18},{3,19},{4,20},{5,21},{6,22},{7,23},{8,24},{9,... | collective-permute-start | bytes 196616 | tf_op jit(solution)/shard_map/ppermute | solution.py:508
  11.3 4.6 %collective-permute-start.5 = (f32[32,384]{1,0:T(8,128)S(1)}, f32[32,384]{1,0:T(8,128)S(1)}, u32[]{:S(2)}, u32[]{:S(2)}) collective-permute-start(f32[32,384]{1,0:T(8,128)S(1)} %get-tuple-element.48), channel_id=1, source_target_pairs={{0,17},{1,16},{2,19},{3,18},{4,21},{5,20},{6,23},{7,22},{8,25},{9,... | collective-permute-start | bytes 147464 | tf_op jit(solution)/shard_map/ppermute | solution.py:508
  12.3 6.9 %collective-permute-start.8 = (f32[96,128]{1,0:T(8,128)S(1)}, f32[96,128]{1,0:T(8,128)S(1)}, u32[]{:S(2)}, u32[]{:S(2)}) collective-permute-start(f32[96,128]{1,0:T(8,128)S(1)} %get-tuple-element.55), channel_id=1, source_target_pairs={{0,0},{1,2},{2,1},{3,4},{4,3},{5,6},{6,5},{7,8},{8,7},{9,10},{10,9... | collective-permute-start | bytes 147464 | tf_op jit(solution)/shard_map/ppermute | solution.py:504
  15.9 7.0 %collective-permute-start.7 = (f32[176,128]{1,0:T(8,128)S(1)}, f32[176,128]{1,0:T(8,128)S(1)}, u32[]{:S(2)}, u32[]{:S(2)}) collective-permute-start(f32[176,128]{1,0:T(8,128)S(1)} %get-tuple-element.54.refs_2_), channel_id=1, source_target_pairs={{16,0},{17,1},{18,2},{19,3},{20,4},{21,5},{22,6},{23,7},{24,8},{25... | collective-permute-start | bytes 270344 | tf_op jit(solution)/shard_map/ppermute | solution.py:508
  19.1 3.7 %collective-permute-start.6 = (f32[32,128]{1,0:T(8,128)S(1)}, f32[32,128]{1,0:T(8,128)S(1)}, u32[]{:S(2)}, u32[]{:S(2)}) collective-permute-start(f32[32,128]{1,0:T(8,128)S(1)} %get-tuple-element.53), channel_id=1, source_target_pairs={{16,0},{17,2},{18,1},{19,4},{20,3},{21,6},{22,5},{23,8},{24,7},{25... | collective-permute-start | bytes 49160 | tf_op jit(solution)/shard_map/ppermute | solution.py:508

commit v9 on v8

--- a/solution.py
+++ b/solution.py
@@ -74,9 +74,10 @@
     return blocks[t, j, pl.ds(b, BLOCK // 2, stride=nb), :] * column[t][j][b : b + 1, :]
 
 
-def edge_kernel(nb, turning, _, blocks, mask, panels, to_b, late_b, to_a, *refs):
+def edge_kernel(nb, turning, parts, _, blocks, mask, panels, *refs):
     width = panels.shape[1]
-    far_b, tile = refs[:-1], refs[-1]
+    to_b, tile = refs if parts == "first" else (None, None)
+    late_b, to_a, *far_b = (None, None) if parts == "first" else refs
     turns = lax.axis_index("tm") == turning
     column = [[presence(mask, t, j, nb) for j in range(3)] for t in range(RUN)]
 
@@ -87,7 +88,7 @@
         dst[96:128, :] = panels[:, :128] if low_side else panels[:, width - 128 :]
         later(dst, 128, low_side, False, 1.0)
 
-    def near_b(dst, rest, low_side):
+    def near_b(dst, low_side):
         keep = inside()
         edge = 0 if low_side else nb - 1
         y = [block_of(blocks, column, 0, j, edge, nb) for j in range(3)]
@@ -102,7 +103,6 @@
         share = (o + pltpu.roll(o, BLOCK, 1)) * keep
         low = iota((ROWS, 128), 1) < BLOCK
         dst[32:64, :] = jnp.where(low, group, share) if low_side else jnp.where(low, share, group)
-        later(rest, 0, low_side, rest.shape[0] > 96, keep)
 
     def later(dst, at, low_side, more, keep):
         edge = 0 if low_side else nb - 1
@@ -125,8 +125,11 @@
 
         @pl.when((parity() == side) & jnp.logical_not(turns))
         def _():
-            near_b(to_b, late_b, side == 0)
-            near_a(to_a, side == 1)
+            if parts == "first":
+                near_b(to_b, side == 0)
+            else:
+                later(late_b, 0, side == 0, late_b.shape[0] > 96, inside())
+                near_a(to_a, side == 1)
 
         if far_b:
 
@@ -519,18 +522,25 @@
     turn = owners % GROUP != 0
     turning = owners - 1 if turn else owners
     begin = call(first_kernel, [f32(8, 128)], (), flops=10**9)
-    sizes = [64, 96 if owners == 2 else 160] + ([96 * (RIM_A + RIM_B), 96 * (FAR_A + FAR_B)] if turn else [224])
-    edges = call(
-        functools.partial(edge_kernel, nb, turning),
-        [f32(n, 128) for n in sizes],
+    (near,) = call(
+        functools.partial(edge_kernel, nb, turning, "first"),
+        [f32(64, 128)],
         (*begin, rows, mask, panels_in),
         [vm(BLOCK, 128)],
     )
-    near_b, near_a = beside(edges[0], partner_b, range(turning)), beside(edges[2], partner_a)
+    near_b = beside(near, partner_b, range(turning))
+    begin, rows, mask, mixing, _ = lax.optimization_barrier((begin, rows, mask, mixing, near))
+    sizes = [96 if owners == 2 else 160]
+    sizes += [96 * (RIM_A + RIM_B), 96 * (FAR_A + FAR_B)] if turn else [224]
+    edges = call(
+        functools.partial(edge_kernel, nb, turning, "rest"),
+        [f32(n, 128) for n in sizes],
+        (*begin, rows, mask, panels_in),
+    )
+    near_a = beside(edges[1], partner_a)
     (near_b,) = call(aside_kernel, [f32(*near_b.shape)], (near_b,), flops=ASIDE_0)
     if turn:
-        far_b = beside(edges[3], partner_b, [turning])
-    rows, mask, mixing, _ = lax.optimization_barrier((rows, mask, mixing, edges))
+        far_b = beside(edges[2], partner_b, [turning])
     *own_tiles, expand = call(
         functools.partial(own_kernel, nb),
         [bf(own, 256)] * 4 + [f32(2 * COLS, 128)],
@@ -544,7 +554,7 @@
         return call(kernel, outs, args, scratch)
 
     def late_rims(after):
-        late, _ = lax.optimization_barrier((edges[1], after))
+        late, _ = lax.optimization_barrier((edges[0], after))
         late = beside(late, partner_b, range(turning))
         args = (near_a, near_b, late)
         return late, rim_call(functools.partial(pull_rim_kernel, turning), 1, 2, args)

time: 37.9 us -> 38 us (level)
    pallas_call x13 -> x14, Pallas kernels: 4.37 us -> 4.47 us  [call(): pl.pallas_call(kernel, out_shape=shapes, in_specs=[pl.BlockSpec(memory_sp...]
  transfers between devices with their start and end apart: 9 -> 9, of which waited for: 3 -> 4; matrix products, arithmetic and copies ran while one was open for 0% -> 0% of each run, Pallas kernels for 4% -> 5%
where the time goes in v9:
time: 38 us; the launch traced here: 37.8 us
  starting transfers between devices  12.6 us (33%)
  blocking collectives  12.2 us (32%)
  waiting for transfers between devices  6.55 us (17%)
  Pallas kernels  4.47 us (12%)
  local copies, waits for them, and re-layouts  1.12 us (3%)
  between operations  0.82 us (2%)
    all_to_all x1, blocking collectives, shards(): grams = lax.all_to_all(every, 'space', 0, 0)  12.2 us
    ppermute x4, starting transfers between devices, beside(): return lax.ppermute(x, ('tm', 'space'), route)  6.52 us
    ppermute x5, waiting for transfers between devices, hop(): lax.ppermute(x, ('tm', 'space'), [(i * count + s, k * count + to(s)) for...  6.35 us
    ppermute x5, starting transfers between devices, hop(): lax.ppermute(x, ('tm', 'space'), [(i * count + s, k * count + to(s)) for...  6.04 us
    pallas_call x14, Pallas kernels, call(): pl.pallas_call(kernel, out_shape=shapes, in_specs=[pl.BlockSpec(memory_sp...  4.47 us
    unnamed x8, local copies, waits for them, and re-layouts  1.11 us
  transfers between devices with their start and end apart: 9, of which 4 were waited for; matrix products, arithmetic and copies ran while one was open for 0% of the time, Pallas kernels for 5%

profile of v9, /device:TPU:0, one launch (start us, length us, event | category | flops | bytes accessed | tf_op | source)
XLA Modules:
  0.0 37.8 jit_solution(1739037576280349061)
XLA Ops:
  0.6 0.0 copy-start
  0.6 0.0 copy-start.1
  0.7 0.0 copy-start.3
  0.7 1.1 %copy-done = f32[2,8,3,4096]{3,1,2,0:T(8,128)S(1)} copy-done((f32[2,8,3,4096]{3,1,2,0:T(8,128)S(1)}, f32[2,8,3,4096]{3,1,2,0:T(8,128)}, u32[]{:S(2)}) %copy-start) | copy-done | bytes 786456
  1.8 0.0 copy-done.1
  1.8 0.0 copy-done.3
  1.8 0.4 shard_map.60
  2.1 0.0 copy-start.2
  2.1 0.8 %collective-permute-start = (f32[64,128]{1,0:T(8,128)S(1)}, f32[64,128]{1,0:T(8,128)S(1)}, u32[]{:S(2)}, u32[]{:S(2)}) collective-permute-start(f32[64,128]{1,0:T(8,128)S(1)} %shard_map.60), channel_id=1, source_target_pairs={{0,0},{1,2},{2,1},{3,4},{4,3},{5,6},{6,5},{7,8},{8,7},{9,10},{10,9... | collective-permute-start | bytes 98312 | tf_op jit(solution)/shard_map/ppermute | solution.py:507
  3.0 0.1 shard_map.62
  3.1 4.4 %collective-permute-start.1 = (f32[864,128]{1,0:T(8,128)S(1)}, f32[864,128]{1,0:T(8,128)S(1)}, u32[]{:S(2)}, u32[]{:S(2)}) collective-permute-start(f32[864,128]{1,0:T(8,128)S(1)} %get-tuple-element.37), channel_id=1, source_target_pairs={{0,1},{1,0},{2,3},{3,2},{4,5},{5,4},{6,7},{7,6},{8,9},{9,8},{10,11... | collective-permute-start | bytes 1327112 | tf_op jit(solution)/shard_map/ppermute | solution.py:507
  7.5 0.7 %collective-permute-start.3 = (f32[480,128]{1,0:T(8,128)S(1)}, f32[480,128]{1,0:T(8,128)S(1)}, u32[]{:S(2)}, u32[]{:S(2)}) collective-permute-start(f32[480,128]{1,0:T(8,128)S(1)} %get-tuple-element.44), channel_id=1, source_target_pairs={{16,16},{17,18},{18,17},{19,20},{20,19},{21,22},{22,21},{23,24},{2... | collective-permute-start | bytes 737288 | tf_op jit(solution)/shard_map/ppermute | solution.py:507
  8.2 0.0 copy-done.2
  8.2 0.5 %shard_map.63 = (bf16[512,256]{1,0:T(8,128)(2,1)S(1)}, bf16[512,256]{1,0:T(8,128)(2,1)S(1)}, bf16[512,256]{1,0:T(8,128)(2,1)S(1)}, bf16[512,256]{1,0:T(8,128)(2,1)S(1)}, f32[16,128]{1,0:T(8,128)S(1)}) custom-call(f32[2,3,256,128]{3,2,1,0:T(8,128)S(1)} %bitcast.10, s32[3,2,8]{2,1,0:T(2,128)S(1)} %bitcast.13, f32[2,4,8,8]{3,2,1,0:T(8,128)S(1)} %copy-done.2), custom_call_target="tpu_custom_call" | custom-call | flops 1000000 | bytes 100000 | tf_op jit(solution)/shard_map/pallas_call | solution.py:33
  8.7 0.0 collective-permute-done.edge
  8.7 0.2 collective-permute-done.1.near_a.far_a
  8.9 0.6 %shard_map.64 = (f32[32,512]{1,0:T(8,128)S(1)}, f32[32,256]{1,0:T(8,128)S(1)}, f32[32,384]{1,0:T(8,128)S(1)}) custom-call(f32[32,128]{1,0:T(8,128)S(1)} %slice.20.edge_b, f32[32,512]{1,0:T(8,128)S(1)} %copy-done.1, f32[32,128]{1,0:T(8,128)S(1)} %slice.21.edge_a, f32[64,128]{1,0:T(8,128)S(1)} %shard_map.61.near_b, ...), custom_call_target="tpu_custom_call" | custom-call | flops 3000000000 | bytes 100000 | tf_op jit(solution)/shard_map/pallas_call | solution.py:33
  9.5 0.1 collective-permute-start.2
  9.6 2.0 %collective-permute-start.4 = (f32[32,512]{1,0:T(8,128)S(1)}, f32[32,512]{1,0:T(8,128)S(1)}, u32[]{:S(2)}, u32[]{:S(2)}) collective-permute-start(f32[32,512]{1,0:T(8,128)S(1)} %get-tuple-element.46.u.refs_0_), channel_id=1, source_target_pairs={{0,16},{1,17},{2,18},{3,19},{4,20},{5,21},{6,22},{7,23},{8,24},{9,... | collective-permute-start | bytes 196616 | tf_op jit(solution)/shard_map/ppermute | solution.py:511
  11.6 0.8 %collective-permute-start.5 = (f32[32,384]{1,0:T(8,128)S(1)}, f32[32,384]{1,0:T(8,128)S(1)}, u32[]{:S(2)}, u32[]{:S(2)}) collective-permute-start(f32[32,384]{1,0:T(8,128)S(1)} %get-tuple-element.47), channel_id=1, source_target_pairs={{0,17},{1,16},{2,19},{3,18},{4,21},{5,20},{6,23},{7,22},{8,25},{9,... | collective-permute-start | bytes 147464 | tf_op jit(solution)/shard_map/ppermute | solution.py:511
  12.4 0.7 %collective-permute-start.8 = (f32[96,128]{1,0:T(8,128)S(1)}, f32[96,128]{1,0:T(8,128)S(1)}, u32[]{:S(2)}, u32[]{:S(2)}) collective-permute-start(f32[96,128]{1,0:T(8,128)S(1)} %get-tuple-element.55), channel_id=1, source_target_pairs={{0,0},{1,2},{2,1},{3,4},{4,3},{5,6},{6,5},{7,8},{8,7},{9,10},{10,9... | collective-permute-start | bytes 147464 | tf_op jit(solution)/shard_map/ppermute | solution.py:507
  13.1 0.3 shard_map.67.old
  13.4 0.0 collective-permute-done.3.far_b
  13.4 0.1 collective-permute-done.2.edge
  13.5 2.8 %collective-permute-done.5.edge_a = f32[32,384]{1,0:T(8,128)S(1)} collective-permute-done((f32[32,384]{1,0:T(8,128)S(1)}, f32[32,384]{1,0:T(8,128)S(1)}, u32[]{:S(2)}, u32[]{:S(2)}) %collective-permute-start.5) | collective-permute-done | bytes 49184 | tf_op jit(solution)/shard_map/ppermute | solution.py:511
  16.3 0.0 collective-permute-done.4.main
  16.3 3.1 %collective-permute-start.7 = (f32[176,128]{1,0:T(8,128)S(1)}, f32[176,128]{1,0:T(8,128)S(1)}, u32[]{:S(2)}, u32[]{:S(2)}) collective-permute-start(f32[176,128]{1,0:T(8,128)S(1)} %get-tuple-element.53.refs_2_), channel_id=1, source_target_pairs={{16,0},{17,1},{18,2},{19,3},{20,4},{21,5},{22,6},{23,7},{24,8},{25... | collective-permute-start | bytes 270344 | tf_op jit(solution)/shard_map/ppermute | solution.py:511
  19.4 0.1 collective-permute-start.6
  19.5 0.0 collective-permute-done.8.late_b
  19.5 0.2 shard_map.70
  19.7 3.5 %collective-permute-done.6.edge = f32[32,128]{1,0:T(8,128)S(1)} collective-permute-done((f32[32,128]{1,0:T(8,128)S(1)}, f32[32,128]{1,0:T(8,128)S(1)}, u32[]{:S(2)}, u32[]{:S(2)}) %collective-permute-start.6) | collective-permute-done | bytes 16416 | tf_op jit(solution)/shard_map/ppermute | solution.py:511
  23.1 0.0 collective-permute-done.7.main
  23.2 0.7 %shard_map.71 = (f32[32,512]{1,0:T(8,128)S(1)}, f32[16,128]{1,0:T(8,128)S(1)}, f32[16,8,128]{2,1,0:T(8,128)S(1)}) custom-call(f32[32,128]{1,0:T(8,128)S(1)} %shard_map.69.edge_b, f32[176,128]{1,0:T(8,128)S(1)} %collective-permute-done.7.main, f32[32,128]{1,0:T(8,128)S(1)} %slice.22.edge_a, bf16[512,256]{1,0:T(8,128)(2,1)S(1)} %get-tuple-element.39.a_hi, ...), custom_call_target="tpu_custom_call" | custom-call | flops 1000000 | bytes 100000 | tf_op jit(solution)/shard_map/pallas_call | solution.py:33
  23.9 12.2 %all_to_all.5.grams = f32[16,8,128]{2,1,0:T(8,128)S(1)} all-to-all(f32[16,8,128]{2,1,0:T(8,128)S(1)} %get-tuple-element.60), channel_id=1, replica_groups=mesh['tm'=2,'space'=16] {'space'}, dimensions={0} | all-to-all | bytes 131072 | tf_op jit(solution)/shard_map/all_to_all | solution.py:616
  36.1 1.6 %shard_map.72 = (f32[32,512]{1,0:T(8,128)}, f32[32,512]{1,0:T(8,128)}) custom-call(f32[16,8,128]{2,1,0:T(8,128)S(1)} %all_to_all.5.grams, f32[16,128]{1,0:T(8,128)S(1)} %get-tuple-element.61.meta, f32[32,512]{1,0:T(8,128)S(1)} %get-tuple-element.46.u.refs_0_, f32[32,512]{1,0:T(8,128)S(1)} %get-tuple-element.62.refs_1_, ...), custom_call_target="tpu_custom_call" | custom-call | flops 1000000 | bytes 100000 | tf_op jit(solution)/shard_map/pallas_call | solution.py:33
  (11 shorter events, 0.0 us)
Async XLA Ops:
  0.6 1.1 %copy-start = (f32[2,8,3,4096]{3,1,2,0:T(8,128)S(1)}, f32[2,8,3,4096]{3,1,2,0:T(8,128)}, u32[]{:S(2)}) copy-start(f32[2,8,3,4096]{3,1,2,0:T(8,128)} %param.5) | copy-start | bytes 2359300
  0.6 1.1 %copy-start.1 = (f32[32,512]{1,0:T(8,128)S(1)}, f32[32,512]{1,0:T(8,128)}, u32[]{:S(2)}) copy-start(f32[32,512]{1,0:T(8,128)} %main.1) | copy-start | bytes 196612
  0.7 1.1 %copy-start.3 = (s32[2,8,3]{1,0,2:T(2,128)S(1)}, s32[2,8,3]{1,0,2:T(2,128)}, u32[]{:S(2)}) copy-start(s32[2,8,3]{1,0,2:T(2,128)} %param.6) | copy-start | bytes 580
  2.1 6.0 %copy-start.2 = (f32[2,4,8,8]{3,2,1,0:T(8,128)S(1)}, f32[2,4,8,8]{3,2,1,0:T(8,128)}, u32[]{:S(2)}) copy-start(f32[2,4,8,8]{3,2,1,0:T(8,128)} %mixing) | copy-start | bytes 6148
  2.1 6.5 %collective-permute-start = (f32[64,128]{1,0:T(8,128)S(1)}, f32[64,128]{1,0:T(8,128)S(1)}, u32[]{:S(2)}, u32[]{:S(2)}) collective-permute-start(f32[64,128]{1,0:T(8,128)S(1)} %shard_map.60), channel_id=1, source_target_pairs={{0,0},{1,2},{2,1},{3,4},{4,3},{5,6},{6,5},{7,8},{8,7},{9,10},{10,9... | collective-permute-start | bytes 98312 | tf_op jit(solution)/shard_map/ppermute | solution.py:507
  3.1 5.8 %collective-permute-start.1 = (f32[864,128]{1,0:T(8,128)S(1)}, f32[864,128]{1,0:T(8,128)S(1)}, u32[]{:S(2)}, u32[]{:S(2)}) collective-permute-start(f32[864,128]{1,0:T(8,128)S(1)} %get-tuple-element.37), channel_id=1, source_target_pairs={{0,1},{1,0},{2,3},{3,2},{4,5},{5,4},{6,7},{7,6},{8,9},{9,8},{10,11... | collective-permute-start | bytes 1327112 | tf_op jit(solution)/shard_map/ppermute | solution.py:507
  7.5 5.9 %collective-permute-start.3 = (f32[480,128]{1,0:T(8,128)S(1)}, f32[480,128]{1,0:T(8,128)S(1)}, u32[]{:S(2)}, u32[]{:S(2)}) collective-permute-start(f32[480,128]{1,0:T(8,128)S(1)} %get-tuple-element.44), channel_id=1, source_target_pairs={{16,16},{17,18},{18,17},{19,20},{20,19},{21,22},{22,21},{23,24},{2... | collective-permute-start | bytes 737288 | tf_op jit(solution)/shard_map/ppermute | solution.py:507
  9.5 4.0 %collective-permute-start.2 = (f32[32,256]{1,0:T(8,128)S(1)}, f32[32,256]{1,0:T(8,128)S(1)}, u32[]{:S(2)}, u32[]{:S(2)}) collective-permute-start(f32[32,256]{1,0:T(8,128)S(1)} %get-tuple-element.43), channel_id=1, source_target_pairs={{0,16},{1,18},{2,17},{3,20},{4,19},{5,22},{6,21},{7,24},{8,23},{9,... | collective-permute-start | bytes 98312 | tf_op jit(solution)/shard_map/ppermute | solution.py:511
  9.6 6.7 %collective-permute-start.4 = (f32[32,512]{1,0:T(8,128)S(1)}, f32[32,512]{1,0:T(8,128)S(1)}, u32[]{:S(2)}, u32[]{:S(2)}) collective-permute-start(f32[32,512]{1,0:T(8,128)S(1)} %get-tuple-element.46.u.refs_0_), channel_id=1, source_target_pairs={{0,16},{1,17},{2,18},{3,19},{4,20},{5,21},{6,22},{7,23},{8,24},{9,... | collective-permute-start | bytes 196616 | tf_op jit(solution)/shard_map/ppermute | solution.py:511
  11.6 4.7 %collective-permute-start.5 = (f32[32,384]{1,0:T(8,128)S(1)}, f32[32,384]{1,0:T(8,128)S(1)}, u32[]{:S(2)}, u32[]{:S(2)}) collective-permute-start(f32[32,384]{1,0:T(8,128)S(1)} %get-tuple-element.47), channel_id=1, source_target_pairs={{0,17},{1,16},{2,19},{3,18},{4,21},{5,20},{6,23},{7,22},{8,25},{9,... | collective-permute-start | bytes 147464 | tf_op jit(solution)/shard_map/ppermute | solution.py:511
  12.4 7.1 %collective-permute-start.8 = (f32[96,128]{1,0:T(8,128)S(1)}, f32[96,128]{1,0:T(8,128)S(1)}, u32[]{:S(2)}, u32[]{:S(2)}) collective-permute-start(f32[96,128]{1,0:T(8,128)S(1)} %get-tuple-element.55), channel_id=1, source_target_pairs={{0,0},{1,2},{2,1},{3,4},{4,3},{5,6},{6,5},{7,8},{8,7},{9,10},{10,9... | collective-permute-start | bytes 147464 | tf_op jit(solution)/shard_map/ppermute | solution.py:507
  16.3 6.8 %collective-permute-start.7 = (f32[176,128]{1,0:T(8,128)S(1)}, f32[176,128]{1,0:T(8,128)S(1)}, u32[]{:S(2)}, u32[]{:S(2)}) collective-permute-start(f32[176,128]{1,0:T(8,128)S(1)} %get-tuple-element.53.refs_2_), channel_id=1, source_target_pairs={{16,0},{17,1},{18,2},{19,3},{20,4},{21,5},{22,6},{23,7},{24,8},{25... | collective-permute-start | bytes 270344 | tf_op jit(solution)/shard_map/ppermute | solution.py:511
  19.4 3.7 %collective-permute-start.6 = (f32[32,128]{1,0:T(8,128)S(1)}, f32[32,128]{1,0:T(8,128)S(1)}, u32[]{:S(2)}, u32[]{:S(2)}) collective-permute-start(f32[32,128]{1,0:T(8,128)S(1)} %get-tuple-element.52), channel_id=1, source_target_pairs={{16,0},{17,2},{18,1},{19,4},{20,3},{21,6},{22,5},{23,8},{24,7},{25... | collective-permute-start | bytes 49160 | tf_op jit(solution)/shard_map/ppermute | solution.py:511

commit v10 on v7

--- a/solution.py
+++ b/solution.py
@@ -446,8 +446,12 @@
         else:
             back, u = select[forward]
             left = jnp.concatenate(split3(full(back)[:, :ROWS].T), axis=0)
-            o = lax.dot_general(left, jnp.concatenate(split3(u), axis=1), NN, preferred_element_type=F32)
-            out[...] = pieces_sum(o, ROWS, own, 3)
+            total = None
+            for i, part in reversed(list(enumerate(split3(u)))):
+                o = lax.dot_general(left[: (3 - i) * ROWS], part, NN, preferred_element_type=F32)
+                piece = pieces_sum(o, ROWS, own)
+                total = piece if total is None else total + piece
+            out[...] = total
 
 
 def shards(panels_in, blocks, block_mask, mixing):

time: 38 us -> 38 us (level)
  no operation moved by 1% of the time
where the time goes in v10:
time: 38 us; the launch traced here: 37.7 us
  starting transfers between devices  13.5 us (36%)
  blocking collectives  12.7 us (33%)
  waiting for transfers between devices  5.51 us (14%)
  Pallas kernels  4.1 us (11%)
  local copies, waits for them, and re-layouts  1.12 us (3%)
  between operations  0.83 us (2%)
    all_to_all x1, blocking collectives, shards(): grams = lax.all_to_all(every, 'space', 0, 0)  12.7 us
    ppermute x5, starting transfers between devices, hop(): lax.ppermute(x, ('tm', 'space'), [(i * count + s, k * count + to(s)) for...  7.08 us
    ppermute x4, starting transfers between devices, beside(): return lax.ppermute(x, ('tm', 'space'), route)  6.37 us
    ppermute x5, waiting for transfers between devices, hop(): lax.ppermute(x, ('tm', 'space'), [(i * count + s, k * count + to(s)) for...  5.31 us
    pallas_call x13, Pallas kernels, call(): pl.pallas_call(kernel, out_shape=shapes, in_specs=[pl.BlockSpec(memory_sp...  4.1 us
    unnamed x8, local copies, waits for them, and re-layouts  1.11 us
  transfers between devices with their start and end apart: 9, of which 3 were waited for; matrix products, arithmetic and copies ran while one was open for 0% of the time, Pallas kernels for 4%

profile of v10, /device:TPU:0, one launch (start us, length us, event | category | flops | bytes accessed | tf_op | source)
XLA Modules:
  0.0 37.7 jit_solution(10361337117163525289)
XLA Ops:
  0.6 0.0 copy-start
  0.6 0.0 copy-start.1
  0.7 0.0 copy-start.3
  0.7 1.1 %copy-done = f32[2,8,3,4096]{3,1,2,0:T(8,128)S(1)} copy-done((f32[2,8,3,4096]{3,1,2,0:T(8,128)S(1)}, f32[2,8,3,4096]{3,1,2,0:T(8,128)}, u32[]{:S(2)}) %copy-start) | copy-done | bytes 786456
  1.8 0.0 copy-done.1
  1.8 0.0 copy-done.3
  1.8 0.0 copy-start.2
  1.8 0.1 shard_map.60
  1.9 0.7 %collective-permute-start = (f32[128,128]{1,0:T(8,128)S(1)}, f32[128,128]{1,0:T(8,128)S(1)}, u32[]{:S(2)}, u32[]{:S(2)}) collective-permute-start(f32[128,128]{1,0:T(8,128)S(1)} %get-tuple-element.34), channel_id=1, source_target_pairs={{0,0},{1,2},{2,1},{3,4},{4,3},{5,6},{6,5},{7,8},{8,7},{9,10},{10,9... | collective-permute-start | bytes 196616 | tf_op jit(solution)/shard_map/ppermute | solution.py:473
  2.6 4.4 %collective-permute-start.1 = (f32[864,128]{1,0:T(8,128)S(1)}, f32[864,128]{1,0:T(8,128)S(1)}, u32[]{:S(2)}, u32[]{:S(2)}) collective-permute-start(f32[864,128]{1,0:T(8,128)S(1)} %get-tuple-element.35), channel_id=1, source_target_pairs={{0,1},{1,0},{2,3},{3,2},{4,5},{5,4},{6,7},{7,6},{8,9},{9,8},{10,11... | collective-permute-start | bytes 1327112 | tf_op jit(solution)/shard_map/ppermute | solution.py:473
  7.0 0.7 %collective-permute-start.3 = (f32[480,128]{1,0:T(8,128)S(1)}, f32[480,128]{1,0:T(8,128)S(1)}, u32[]{:S(2)}, u32[]{:S(2)}) collective-permute-start(f32[480,128]{1,0:T(8,128)S(1)} %get-tuple-element.37), channel_id=1, source_target_pairs={{16,16},{17,18},{18,17},{19,20},{20,19},{21,22},{22,21},{23,24},{2... | collective-permute-start | bytes 737288 | tf_op jit(solution)/shard_map/ppermute | solution.py:473
  7.7 0.0 copy-done.2
  7.7 0.5 %shard_map.62 = (bf16[512,256]{1,0:T(8,128)(2,1)S(1)}, bf16[512,256]{1,0:T(8,128)(2,1)S(1)}, bf16[512,256]{1,0:T(8,128)(2,1)S(1)}, bf16[512,256]{1,0:T(8,128)(2,1)S(1)}, f32[16,128]{1,0:T(8,128)S(1)}) custom-call(f32[2,3,256,128]{3,2,1,0:T(8,128)S(1)} %bitcast.9, s32[3,2,8]{2,1,0:T(2,128)S(1)} %bitcast.11, f32[2,4,8,8]{3,2,1,0:T(8,128)S(1)} %copy-done.2), custom_call_target="tpu_custom_call" | custom-call | flops 1000000 | bytes 100000 | tf_op jit(solution)/shard_map/pallas_call | solution.py:33
  8.2 0.0 collective-permute-done.edge
  8.2 0.2 collective-permute-done.1.near_a.far_a
  8.4 0.6 %shard_map.63 = (f32[32,512]{1,0:T(8,128)S(1)}, f32[32,256]{1,0:T(8,128)S(1)}, f32[32,384]{1,0:T(8,128)S(1)}) custom-call(f32[32,128]{1,0:T(8,128)S(1)} %slice.20.edge_b, f32[32,512]{1,0:T(8,128)S(1)} %copy-done.1, f32[32,128]{1,0:T(8,128)S(1)} %slice.21.edge_a, f32[128,128]{1,0:T(8,128)S(1)} %shard_map.61.near_b, ...), custom_call_target="tpu_custom_call" | custom-call | flops 3000000000 | bytes 100000 | tf_op jit(solution)/shard_map/pallas_call | solution.py:33
  9.0 0.1 collective-permute-start.2
  9.1 2.0 %collective-permute-start.4 = (f32[32,512]{1,0:T(8,128)S(1)}, f32[32,512]{1,0:T(8,128)S(1)}, u32[]{:S(2)}, u32[]{:S(2)}) collective-permute-start(f32[32,512]{1,0:T(8,128)S(1)} %get-tuple-element.47.u.refs_0_), channel_id=1, source_target_pairs={{0,16},{1,17},{2,18},{3,19},{4,20},{5,21},{6,22},{7,23},{8,24},{9,... | collective-permute-start | bytes 196616 | tf_op jit(solution)/shard_map/ppermute | solution.py:477
  11.1 1.3 %collective-permute-start.5 = (f32[32,384]{1,0:T(8,128)S(1)}, f32[32,384]{1,0:T(8,128)S(1)}, u32[]{:S(2)}, u32[]{:S(2)}) collective-permute-start(f32[32,384]{1,0:T(8,128)S(1)} %get-tuple-element.48), channel_id=1, source_target_pairs={{0,17},{1,16},{2,19},{3,18},{4,21},{5,20},{6,23},{7,22},{8,25},{9,... | collective-permute-start | bytes 147464 | tf_op jit(solution)/shard_map/ppermute | solution.py:477
  12.4 0.7 %collective-permute-start.8 = (f32[96,128]{1,0:T(8,128)S(1)}, f32[96,128]{1,0:T(8,128)S(1)}, u32[]{:S(2)}, u32[]{:S(2)}) collective-permute-start(f32[96,128]{1,0:T(8,128)S(1)} %get-tuple-element.55), channel_id=1, source_target_pairs={{0,0},{1,2},{2,1},{3,4},{4,3},{5,6},{6,5},{7,8},{8,7},{9,10},{10,9... | collective-permute-start | bytes 147464 | tf_op jit(solution)/shard_map/ppermute | solution.py:473
  13.1 0.3 shard_map.66.old
  13.4 0.0 collective-permute-done.3.far_b
  13.4 0.0 collective-permute-done.2.edge
  13.4 1.8 %collective-permute-done.5.edge_a = f32[32,384]{1,0:T(8,128)S(1)} collective-permute-done((f32[32,384]{1,0:T(8,128)S(1)}, f32[32,384]{1,0:T(8,128)S(1)}, u32[]{:S(2)}, u32[]{:S(2)}) %collective-permute-start.5) | collective-permute-done | bytes 49184 | tf_op jit(solution)/shard_map/ppermute | solution.py:477
  15.3 0.0 collective-permute-done.4.main
  15.3 3.6 %collective-permute-start.7 = (f32[176,128]{1,0:T(8,128)S(1)}, f32[176,128]{1,0:T(8,128)S(1)}, u32[]{:S(2)}, u32[]{:S(2)}) collective-permute-start(f32[176,128]{1,0:T(8,128)S(1)} %get-tuple-element.54.refs_2_), channel_id=1, source_target_pairs={{16,0},{17,1},{18,2},{19,3},{20,4},{21,5},{22,6},{23,7},{24,8},{25... | collective-permute-start | bytes 270344 | tf_op jit(solution)/shard_map/ppermute | solution.py:477
  18.9 0.1 collective-permute-start.6
  19.0 0.0 collective-permute-done.8.late_b
  19.0 0.2 shard_map.69
  19.2 3.5 %collective-permute-done.6.edge = f32[32,128]{1,0:T(8,128)S(1)} collective-permute-done((f32[32,128]{1,0:T(8,128)S(1)}, f32[32,128]{1,0:T(8,128)S(1)}, u32[]{:S(2)}, u32[]{:S(2)}) %collective-permute-start.6) | collective-permute-done | bytes 16416 | tf_op jit(solution)/shard_map/ppermute | solution.py:477
  22.6 0.0 collective-permute-done.7.main
  22.7 0.7 %shard_map.70 = (f32[32,512]{1,0:T(8,128)S(1)}, f32[16,128]{1,0:T(8,128)S(1)}, f32[16,8,128]{2,1,0:T(8,128)S(1)}) custom-call(f32[32,128]{1,0:T(8,128)S(1)} %shard_map.68.edge_b, f32[176,128]{1,0:T(8,128)S(1)} %collective-permute-done.7.main, f32[32,128]{1,0:T(8,128)S(1)} %slice.22.edge_a, bf16[512,256]{1,0:T(8,128)(2,1)S(1)} %get-tuple-element.41.a_hi, ...), custom_call_target="tpu_custom_call" | custom-call | flops 1000000 | bytes 100000 | tf_op jit(solution)/shard_map/pallas_call | solution.py:33
  23.4 12.7 %all_to_all.5.grams = f32[16,8,128]{2,1,0:T(8,128)S(1)} all-to-all(f32[16,8,128]{2,1,0:T(8,128)S(1)} %get-tuple-element.60), channel_id=1, replica_groups=mesh['tm'=2,'space'=16] {'space'}, dimensions={0} | all-to-all | bytes 131072 | tf_op jit(solution)/shard_map/all_to_all | solution.py:573
  36.1 1.6 %shard_map.71 = (f32[32,512]{1,0:T(8,128)}, f32[32,512]{1,0:T(8,128)}) custom-call(f32[16,8,128]{2,1,0:T(8,128)S(1)} %all_to_all.5.grams, f32[16,128]{1,0:T(8,128)S(1)} %get-tuple-element.61.meta, f32[32,512]{1,0:T(8,128)S(1)} %get-tuple-element.47.u.refs_0_, f32[32,512]{1,0:T(8,128)S(1)} %get-tuple-element.62.refs_1_, ...), custom_call_target="tpu_custom_call" | custom-call | flops 1000000 | bytes 100000 | tf_op jit(solution)/shard_map/pallas_call | solution.py:33
  (11 shorter events, 0.0 us)
Async XLA Ops:
  0.6 1.1 %copy-start = (f32[2,8,3,4096]{3,1,2,0:T(8,128)S(1)}, f32[2,8,3,4096]{3,1,2,0:T(8,128)}, u32[]{:S(2)}) copy-start(f32[2,8,3,4096]{3,1,2,0:T(8,128)} %param.5) | copy-start | bytes 2359300
  0.6 1.1 %copy-start.1 = (f32[32,512]{1,0:T(8,128)S(1)}, f32[32,512]{1,0:T(8,128)}, u32[]{:S(2)}) copy-start(f32[32,512]{1,0:T(8,128)} %main.1) | copy-start | bytes 196612
  0.7 1.1 %copy-start.3 = (s32[2,8,3]{1,0,2:T(2,128)S(1)}, s32[2,8,3]{1,0,2:T(2,128)}, u32[]{:S(2)}) copy-start(s32[2,8,3]{1,0,2:T(2,128)} %param.6) | copy-start | bytes 580
  1.8 5.9 %copy-start.2 = (f32[2,4,8,8]{3,2,1,0:T(8,128)S(1)}, f32[2,4,8,8]{3,2,1,0:T(8,128)}, u32[]{:S(2)}) copy-start(f32[2,4,8,8]{3,2,1,0:T(8,128)} %mixing) | copy-start | bytes 6148
  1.9 6.3 %collective-permute-start = (f32[128,128]{1,0:T(8,128)S(1)}, f32[128,128]{1,0:T(8,128)S(1)}, u32[]{:S(2)}, u32[]{:S(2)}) collective-permute-start(f32[128,128]{1,0:T(8,128)S(1)} %get-tuple-element.34), channel_id=1, source_target_pairs={{0,0},{1,2},{2,1},{3,4},{4,3},{5,6},{6,5},{7,8},{8,7},{9,10},{10,9... | collective-permute-start | bytes 196616 | tf_op jit(solution)/shard_map/ppermute | solution.py:473
  2.6 5.8 %collective-permute-start.1 = (f32[864,128]{1,0:T(8,128)S(1)}, f32[864,128]{1,0:T(8,128)S(1)}, u32[]{:S(2)}, u32[]{:S(2)}) collective-permute-start(f32[864,128]{1,0:T(8,128)S(1)} %get-tuple-element.35), channel_id=1, source_target_pairs={{0,1},{1,0},{2,3},{3,2},{4,5},{5,4},{6,7},{7,6},{8,9},{9,8},{10,11... | collective-permute-start | bytes 1327112 | tf_op jit(solution)/shard_map/ppermute | solution.py:473
  7.0 6.4 %collective-permute-start.3 = (f32[480,128]{1,0:T(8,128)S(1)}, f32[480,128]{1,0:T(8,128)S(1)}, u32[]{:S(2)}, u32[]{:S(2)}) collective-permute-start(f32[480,128]{1,0:T(8,128)S(1)} %get-tuple-element.37), channel_id=1, source_target_pairs={{16,16},{17,18},{18,17},{19,20},{20,19},{21,22},{22,21},{23,24},{2... | collective-permute-start | bytes 737288 | tf_op jit(solution)/shard_map/ppermute | solution.py:473
  9.0 4.4 %collective-permute-start.2 = (f32[32,256]{1,0:T(8,128)S(1)}, f32[32,256]{1,0:T(8,128)S(1)}, u32[]{:S(2)}, u32[]{:S(2)}) collective-permute-start(f32[32,256]{1,0:T(8,128)S(1)} %get-tuple-element.45), channel_id=1, source_target_pairs={{0,16},{1,18},{2,17},{3,20},{4,19},{5,22},{6,21},{7,24},{8,23},{9,... | collective-permute-start | bytes 98312 | tf_op jit(solution)/shard_map/ppermute | solution.py:477
  9.1 6.2 %collective-permute-start.4 = (f32[32,512]{1,0:T(8,128)S(1)}, f32[32,512]{1,0:T(8,128)S(1)}, u32[]{:S(2)}, u32[]{:S(2)}) collective-permute-start(f32[32,512]{1,0:T(8,128)S(1)} %get-tuple-element.47.u.refs_0_), channel_id=1, source_target_pairs={{0,16},{1,17},{2,18},{3,19},{4,20},{5,21},{6,22},{7,23},{8,24},{9,... | collective-permute-start | bytes 196616 | tf_op jit(solution)/shard_map/ppermute | solution.py:477
  11.1 4.2 %collective-permute-start.5 = (f32[32,384]{1,0:T(8,128)S(1)}, f32[32,384]{1,0:T(8,128)S(1)}, u32[]{:S(2)}, u32[]{:S(2)}) collective-permute-start(f32[32,384]{1,0:T(8,128)S(1)} %get-tuple-element.48), channel_id=1, source_target_pairs={{0,17},{1,16},{2,19},{3,18},{4,21},{5,20},{6,23},{7,22},{8,25},{9,... | collective-permute-start | bytes 147464 | tf_op jit(solution)/shard_map/ppermute | solution.py:477
  12.4 6.6 %collective-permute-start.8 = (f32[96,128]{1,0:T(8,128)S(1)}, f32[96,128]{1,0:T(8,128)S(1)}, u32[]{:S(2)}, u32[]{:S(2)}) collective-permute-start(f32[96,128]{1,0:T(8,128)S(1)} %get-tuple-element.55), channel_id=1, source_target_pairs={{0,0},{1,2},{2,1},{3,4},{4,3},{5,6},{6,5},{7,8},{8,7},{9,10},{10,9... | collective-permute-start | bytes 147464 | tf_op jit(solution)/shard_map/ppermute | solution.py:473
  15.3 7.4 %collective-permute-start.7 = (f32[176,128]{1,0:T(8,128)S(1)}, f32[176,128]{1,0:T(8,128)S(1)}, u32[]{:S(2)}, u32[]{:S(2)}) collective-permute-start(f32[176,128]{1,0:T(8,128)S(1)} %get-tuple-element.54.refs_2_), channel_id=1, source_target_pairs={{16,0},{17,1},{18,2},{19,3},{20,4},{21,5},{22,6},{23,7},{24,8},{25... | collective-permute-start | bytes 270344 | tf_op jit(solution)/shard_map/ppermute | solution.py:477
  18.9 3.7 %collective-permute-start.6 = (f32[32,128]{1,0:T(8,128)S(1)}, f32[32,128]{1,0:T(8,128)S(1)}, u32[]{:S(2)}, u32[]{:S(2)}) collective-permute-start(f32[32,128]{1,0:T(8,128)S(1)} %get-tuple-element.53), channel_id=1, source_target_pairs={{16,0},{17,2},{18,1},{19,4},{20,3},{21,6},{22,5},{23,8},{24,7},{25... | collective-permute-start | bytes 49160 | tf_op jit(solution)/shard_map/ppermute | solution.py:477
